TPU v7x, 32 devices: a whole 2x2x4 slice. The times are simulated.
32 devices in a mesh: tm: 16 (over z, y, x), rows: 2 (over core).
Axes of the slice: x: 2, y: 2, z: 4, core: 2. Of those that a mesh axis runs over, the one named last changes fastest.
Arguments:
- site_rates: float32 [256], replicated, may hold values from 0.0005 to 0.2
- prior_mean: float32 [512, 384], replicated, may hold values from -6 to 6
- observed: float32 [16, 256, 384], P('tm'), may hold values from -6 to 6
- obs_mask: int32 [16, 256], P('tm'), may hold values 0 or 1
- filter_gains: float32 [16, 512, 256], P('tm', 'rows'), may hold values from -0.05 to 0.8, as said below
- smooth_gains: float32 [16, 512, 512], P('tm', 'rows'), may hold values from -0.02 to 1, as said below
Outputs:
- filtered: float32 [16, 512, 384], P('tm', 'rows')
- smoothed: float32 [16, 512, 384], P('tm', 'rows')
Inputs may be any that keep to these rules, and one draw needn't show every extreme that they name: `filter_gains`: gain of each step; row 2i + c is component c of site i, column j a site. `smooth_gains`: smoother gain of each step; rows and columns are state entries.
All inputs are finite; a program needn't handle non-finite values. No bound on the sum of `obs_mask` on one device may be relied on, other than what follows from the above.
Results may differ from a plain program's by a relative error of at most 0.0003.
Values sent between devices are 32-bit elements; how exact they have to be, the bound alone decides.
No kernel may reach another device: no remote copies, remote signals or barrier semaphores. Data moves between devices by JAX's collectives and lax.ppermute only.
A program may use at most 128 MiB of HBM per device.

v0:
```python
import jax
import jax.numpy as jnp
from jax import lax
from jax.sharding import PartitionSpec as P


def shifted(value, axis, steps):
    count = lax.axis_size(axis)
    first, last = (max(0, -steps), min(count, count - steps))
    return lax.ppermute(value, axis, [(source, source + steps) for source in range(first, last)])


def product(left, right):
    return jnp.dot(left, right, precision=lax.Precision.HIGHEST, preferred_element_type=jnp.float32)


def transition_blocks(site_rates):
    decay = jnp.exp(-site_rates)
    top = jnp.stack([decay * (1.0 + site_rates), decay], -1)
    bottom = jnp.stack([-decay * site_rates * site_rates, decay * (1.0 - site_rates)], -1)
    return jnp.stack([top, bottom], 1)


def apply_transition(values, site_rates):
    blocks = transition_blocks(site_rates)
    paired = values.reshape(site_rates.shape[0], 2, values.shape[-1])
    moved = jnp.einsum("scd,sdb->scb", blocks, paired, precision=lax.Precision.HIGHEST)
    return moved.reshape(values.shape)


def combine_levels(mapping, offset, toward):
    time_count = lax.axis_size("tm")
    time_index = lax.axis_index("tm")
    for level in range(time_count.bit_length() - 1):
        stride = 1 << level
        if toward > 0:
            active = time_index >= stride
        else:
            active = time_index + stride < time_count
        far_map, far_offset = shifted((mapping, offset), "tm", stride * toward)
        current = mapping
        joined_map = product(current, lax.all_gather(far_map, "rows", axis=0, tiled=True))
        joined_offset = (jnp.zeros_like(mapping), offset)[1] + product(
            current, lax.all_gather(far_offset, "rows", axis=0, tiled=True)
        )
        mapping = jnp.where(active, joined_map, mapping)
        offset = jnp.where(active, joined_offset, offset)
    return offset


def body(site_rates, prior_mean, observed, obs_mask, filter_gains, smooth_gains):
    time_count = lax.axis_size("tm")
    time_index = lax.axis_index("tm")
    row_index = lax.axis_index("rows")
    panel_rows = filter_gains.shape[1]
    site_count = site_rates.shape[0]
    state_dim = 2 * site_count
    panel_sites = panel_rows // 2
    start_site = row_index * panel_sites
    blocks = transition_blocks(site_rates)
    panel_blocks = lax.dynamic_slice_in_dim(blocks, start_site, panel_sites, 0)
    own_site = (
        jnp.arange(site_count)[None, :] == (start_site + jnp.arange(panel_sites))[:, None]
    ).astype(jnp.float32)
    trans_rows = (panel_blocks[:, :, None, :] * own_site[:, None, :, None]).reshape(
        panel_rows, state_dim
    )
    kept_gain = filter_gains[0] * obs_mask[0].astype(jnp.float32)[None, :]
    correction = jnp.stack(
        [kept_gain * blocks[:, 0, 0][None, :], kept_gain * blocks[:, 0, 1][None, :]], -1
    ).reshape(panel_rows, state_dim)
    step_map = trans_rows - correction
    drive = product(kept_gain, observed[0])
    at_start = time_index == 0
    mapping = jnp.where(at_start, jnp.zeros_like(step_map), step_map)
    offset = drive + jnp.where(at_start, product(step_map, prior_mean), jnp.zeros_like(drive))
    filtered = combine_levels(mapping, offset, 1)
    filt_full = lax.all_gather(filtered, "rows", axis=0, tiled=True)
    at_end = time_index == time_count - 1
    backward = jnp.where(at_end, jnp.zeros_like(smooth_gains[0]), smooth_gains[0])
    residual_term = filtered - product(backward, apply_transition(filt_full, site_rates))
    smoothed = combine_levels(backward, residual_term, -1)
    return (filtered[None], smoothed[None])


def solution(mesh):
    placed = (
        P(),
        P(),
        P("tm", None, None),
        P("tm", None),
        P("tm", "rows", None),
        P("tm", "rows", None),
    )
    return jax.shard_map(
        body,
        mesh=mesh,
        in_specs=placed,
        out_specs=(P("tm", "rows", None), P("tm", "rows", None)),
        check_vma=False,
    )
```

profile of v0, /device:TPU:0, one launch (start us, length us, event | category | flops | bytes accessed | tf_op | source)
XLA Modules:
  0.0 282.4 jit_solution(3277240408825140147)
XLA Ops:
  8.3 11.5 %broadcast_multiply_fusion = f32[128,2,256,2]{3,2,1,0:T(8,128)} fusion(f32[128,256]{1,0:T(8,128)S(1)} %fusion.16, f32[128,2,2]{2,1,0:T(2,128)S(1)} %copy.15), kind=kLoop, calls=%fused_computation | loop fusion | flops 131072 | bytes 657408 | tf_op jit(solution)/shard_map/mul | solution.py:65
  19.8 24.2 %mul.110 = f32[256,512]{1,0:T(8,128)S(1)} reshape(f32[128,2,256,2]{3,2,1,0:T(8,128)} %broadcast_multiply_fusion) | data formatting | bytes 1048576 | tf_op jit(solution)/shard_map/mul | solution.py:65
  45.0 4.9 %collective-permute-start.1 = (f32[256,512]{1,0:T(8,128)S(1)}, f32[256,512]{1,0:T(8,128)S(1)}, u32[]{:S(2)}, u32[]{:S(2)}) collective-permute-start(f32[256,512]{1,0:T(8,128)S(1)} %broadcast_select_fusion), channel_id=1, source_target_pairs={{0,2},{2,4},{4,6},{6,8},{8,10},{10,12},{12,14},{14,16},{16,18},{18... | collective-permute-start | bytes 1572872 | tf_op jit(solution)/shard_map/ppermute | solution.py:10
  49.9 11.1 %collective-permute-done.1 = f32[256,512]{1,0:T(8,128)S(1)} collective-permute-done((f32[256,512]{1,0:T(8,128)S(1)}, f32[256,512]{1,0:T(8,128)S(1)}, u32[]{:S(2)}, u32[]{:S(2)}) %collective-permute-start.1) | collective-permute-done | bytes 524320 | tf_op jit(solution)/shard_map/ppermute | solution.py:10
  61.9 11.4 %all-gather.7.cloned.1.call-done = f32[512,512]{1,0:T(8,128)} async-done(((f32[256,512]{1,0:T(8,128)}), f32[512,512]{1,0:T(8,128)}) %all-gather.7.cloned.1.call-update) | async-done | bytes 1048592 | tf_op jit(solution)/shard_map/all_gather | solution.py:42
  75.6 4.4 %collective-permute-start.3 = (f32[256,512]{1,0:T(8,128)S(1)}, f32[256,512]{1,0:T(8,128)}, u32[]{:S(2)}, u32[]{:S(2)}) collective-permute-start(f32[256,512]{1,0:T(8,128)S(1)} %convolution_select_fusion.5), channel_id=1, source_target_pairs={{0,4},{2,6},{4,8},{6,10},{8,12},{10,14},{12,16},{14,18},{16,20},{1... | collective-permute-start | bytes 1572872 | tf_op jit(solution)/shard_map/ppermute | solution.py:10
  80.0 10.8 %collective-permute-done.3 = f32[256,512]{1,0:T(8,128)} collective-permute-done((f32[256,512]{1,0:T(8,128)S(1)}, f32[256,512]{1,0:T(8,128)}, u32[]{:S(2)}, u32[]{:S(2)}) %collective-permute-start.3) | collective-permute-done | bytes 524320 | tf_op jit(solution)/shard_map/ppermute | solution.py:10
  92.6 3.4 %collective-permute-start = (f32[256,384]{1,0:T(8,128)S(1)}, f32[256,384]{1,0:T(8,128)S(1)}, u32[]{:S(2)}, u32[]{:S(2)}) collective-permute-start(f32[256,384]{1,0:T(8,128)S(1)} %convolution_add_fusion.8), channel_id=1, source_target_pairs={{0,2},{2,4},{4,6},{6,8},{8,10},{10,12},{12,14},{14,16},{16,18},{18... | collective-permute-start | bytes 1179656 | tf_op jit(solution)/shard_map/ppermute | solution.py:10
  98.4 16.9 %collective-permute-done = f32[256,384]{1,0:T(8,128)S(1)} collective-permute-done((f32[256,384]{1,0:T(8,128)S(1)}, f32[256,384]{1,0:T(8,128)S(1)}, u32[]{:S(2)}, u32[]{:S(2)}) %collective-permute-start) | collective-permute-done | bytes 393248 | tf_op jit(solution)/shard_map/ppermute | solution.py:10
  115.3 2.4 all_gather.45
  121.9 2.3 convolution_select_fusion.4
  124.2 7.1 %collective-permute-start.5 = (f32[256,512]{1,0:T(8,128)S(1)}, f32[256,512]{1,0:T(8,128)}, u32[]{:S(2)}, u32[]{:S(2)}) collective-permute-start(f32[256,512]{1,0:T(8,128)S(1)} %convolution_select_fusion.4), channel_id=1, source_target_pairs={{0,8},{2,10},{4,12},{6,14},{8,16},{10,18},{12,20},{14,22},{16,24},... | collective-permute-start | bytes 1572872 | tf_op jit(solution)/shard_map/ppermute | solution.py:10
  131.3 2.4 all_gather.47
  134.6 8.6 %collective-permute-start.4 = (f32[256,384]{1,0:T(8,128)S(1)}, f32[256,384]{1,0:T(8,128)S(1)}, u32[]{:S(2)}, u32[]{:S(2)}) collective-permute-start(f32[256,384]{1,0:T(8,128)S(1)} %fusion.7), channel_id=1, source_target_pairs={{0,8},{2,10},{4,12},{6,14},{8,16},{10,18},{12,20},{14,22},{16,24},... | collective-permute-start | bytes 1179656 | tf_op jit(solution)/shard_map/ppermute | solution.py:10
  143.4 2.3 convolution_select_fusion.2
  147.0 4.9 %collective-permute-done.4 = f32[256,384]{1,0:T(8,128)S(1)} collective-permute-done((f32[256,384]{1,0:T(8,128)S(1)}, f32[256,384]{1,0:T(8,128)S(1)}, u32[]{:S(2)}, u32[]{:S(2)}) %collective-permute-start.4) | collective-permute-done | bytes 393248 | tf_op jit(solution)/shard_map/ppermute | solution.py:10
  151.9 2.5 all_gather.49
  155.5 5.3 %collective-permute-start.6 = (f32[256,384]{1,0:T(8,128)S(1)}, f32[256,384]{1,0:T(8,128)S(1)}, u32[]{:S(2)}, u32[]{:S(2)}) collective-permute-start(f32[256,384]{1,0:T(8,128)S(1)} %fusion.6), channel_id=1, source_target_pairs={{0,16},{2,18},{4,20},{6,22},{8,24},{10,26},{12,28},{14,30},{1,17},... | collective-permute-start | bytes 1179656 | tf_op jit(solution)/shard_map/ppermute | solution.py:10
  162.3 7.2 %collective-permute-done.6 = f32[256,384]{1,0:T(8,128)S(1)} collective-permute-done((f32[256,384]{1,0:T(8,128)S(1)}, f32[256,384]{1,0:T(8,128)S(1)}, u32[]{:S(2)}, u32[]{:S(2)}) %collective-permute-start.6) | collective-permute-done | bytes 393248 | tf_op jit(solution)/shard_map/ppermute | solution.py:10
  169.5 2.4 all_gather.51
  171.8 2.4 convolution_select_fusion.3
  176.2 2.4 all_gather.52
  179.9 5.6 %fusion.19 = f32[256,2,384]{2,1,0:T(2,128)} fusion(f32[256,2,2]{2,1,0:T(2,128)} %copy.18, f32[256,2,384]{2,1,0:T(2,128)} %reshape.189), kind=kOutput, calls=%fused_computation.52 | convolution fusion | flops 4718592 | bytes 1576960 | tf_op jit(solution)/shard_map/scd,sdb->scb/dot_general | solution.py:27
  193.9 9.0 %collective-permute-done.7 = f32[256,384]{1,0:T(8,128)S(1)} collective-permute-done((f32[256,384]{1,0:T(8,128)}, f32[256,384]{1,0:T(8,128)S(1)}, u32[]{:S(2)}, u32[]{:S(2)}) %collective-permute-start.7) | collective-permute-done | bytes 393248 | tf_op jit(solution)/shard_map/ppermute | solution.py:10
  202.9 2.4 all_gather.53
  208.6 13.3 %collective-permute-done.12 = f32[256,512]{1,0:T(8,128)} collective-permute-done((f32[256,512]{1,0:T(8,128)S(1)}, f32[256,512]{1,0:T(8,128)}, u32[]{:S(2)}, u32[]{:S(2)}) %collective-permute-start.12) | collective-permute-done | bytes 524320 | tf_op jit(solution)/shard_map/ppermute | solution.py:10
  221.9 2.6 all_gather.55
  226.8 18.5 %collective-permute-done.11 = f32[256,384]{1,0:T(8,128)S(1)} collective-permute-done((f32[256,384]{1,0:T(8,128)S(1)}, f32[256,384]{1,0:T(8,128)S(1)}, u32[]{:S(2)}, u32[]{:S(2)}) %collective-permute-start.11) | collective-permute-done | bytes 393248 | tf_op jit(solution)/shard_map/ppermute | solution.py:10
  245.3 2.4 all_gather.57
  250.0 2.3 convolution_select_fusion
  252.3 19.1 %collective-permute-done.13 = f32[256,384]{1,0:T(8,128)S(1)} collective-permute-done((f32[256,384]{1,0:T(8,128)S(1)}, f32[256,384]{1,0:T(8,128)S(1)}, u32[]{:S(2)}, u32[]{:S(2)}) %collective-permute-start.13) | collective-permute-done | bytes 393248 | tf_op jit(solution)/shard_map/ppermute | solution.py:10
  271.4 2.4 all_gather.59
  (78 shorter events, 39.8 us)
Async XLA Ops:
  7.2 83.7 %copy-start = (f32[512,384]{1,0:T(8,128)S(1)}, f32[512,384]{1,0:T(8,128)}, u32[]{:S(2)}) copy-start(f32[512,384]{1,0:T(8,128)} %param.7) | copy-start | bytes 2359300
  7.2 66.1 %all-gather.7.cloned.1.call-start = ((), (), s32[]{:S(2)}) async-start(), calls=%async_computation | async-start | bytes 1572864 | tf_op jit(solution)/shard_map/all_gather | solution.py:42
  8.3 35.7 %copy-start.7 = (s32[1,256]{1,0:T(1,128)S(1)}, s32[1,256]{1,0:T(1,128)}, u32[]{:S(2)}) copy-start(s32[1,256]{1,0:T(1,128)} %param.9) | copy-start | bytes 3076
  8.3 35.7 %copy-start.4 = (f32[1,256,256]{2,1,0:T(8,128)S(1)}, f32[1,256,256]{2,1,0:T(8,128)}, u32[]{:S(2)}) copy-start(f32[1,256,256]{2,1,0:T(8,128)} %param.10) | copy-start | bytes 786436
  8.3 83.6 %copy-start.6 = (f32[1,256,384]{2,1,0:T(8,128)S(1)}, f32[1,256,384]{2,1,0:T(8,128)}, u32[]{:S(2)}) copy-start(f32[1,256,384]{2,1,0:T(8,128)} %param.8) | copy-start | bytes 1179652
  45.0 16.0 %collective-permute-start.1 = (f32[256,512]{1,0:T(8,128)S(1)}, f32[256,512]{1,0:T(8,128)S(1)}, u32[]{:S(2)}, u32[]{:S(2)}) collective-permute-start(f32[256,512]{1,0:T(8,128)S(1)} %broadcast_select_fusion), channel_id=1, source_target_pairs={{0,2},{2,4},{4,6},{6,8},{8,10},{10,12},{12,14},{14,16},{16,18},{18... | collective-permute-start | bytes 1572872 | tf_op jit(solution)/shard_map/ppermute | solution.py:10
  61.0 0.8 copy-start.5
  61.8 60.0 %all-gather.9.cloned.1.call-start = ((), (), s32[]{:S(2)}) async-start(), calls=%async_computation.1 | async-start | bytes 1572864 | tf_op jit(solution)/shard_map/all_gather | solution.py:42
  75.6 15.3 %collective-permute-start.3 = (f32[256,512]{1,0:T(8,128)S(1)}, f32[256,512]{1,0:T(8,128)}, u32[]{:S(2)}, u32[]{:S(2)}) collective-permute-start(f32[256,512]{1,0:T(8,128)S(1)} %convolution_select_fusion.5), channel_id=1, source_target_pairs={{0,4},{2,6},{4,8},{6,10},{8,12},{10,14},{12,16},{14,18},{16,20},{1... | collective-permute-start | bytes 1572872 | tf_op jit(solution)/shard_map/ppermute | solution.py:10
  90.9 52.5 %all-gather.13.cloned.1.call-start = ((), (), s32[]{:S(2)}) async-start(), calls=%async_computation.3 | async-start | bytes 1572864 | tf_op jit(solution)/shard_map/all_gather | solution.py:42
  92.6 5.8 %copy-start.3 = (f32[256,384]{1,0:T(8,128)}, f32[256,384]{1,0:T(8,128)S(1)}, u32[]{:S(2)}) copy-start(f32[256,384]{1,0:T(8,128)S(1)} %convolution_add_fusion.8) | copy-start | bytes 1179652
  92.6 22.7 %collective-permute-start = (f32[256,384]{1,0:T(8,128)S(1)}, f32[256,384]{1,0:T(8,128)S(1)}, u32[]{:S(2)}, u32[]{:S(2)}) collective-permute-start(f32[256,384]{1,0:T(8,128)S(1)} %convolution_add_fusion.8), channel_id=1, source_target_pairs={{0,2},{2,4},{4,6},{6,8},{8,10},{10,12},{12,14},{14,16},{16,18},{18... | collective-permute-start | bytes 1179656 | tf_op jit(solution)/shard_map/ppermute | solution.py:10
  97.1 21.3 %collective-permute-start.8 = (f32[256,512]{1,0:T(8,128)S(1)}, f32[256,512]{1,0:T(8,128)}, u32[]{:S(2)}, u32[]{:S(2)}) collective-permute-start(f32[256,512]{1,0:T(8,128)S(1)} %select_bitcast_fusion), channel_id=1, source_target_pairs={{2,0},{4,2},{6,4},{8,6},{10,8},{12,10},{14,12},{16,14},{18,16},{20... | collective-permute-start | bytes 1572872 | tf_op jit(solution)/shard_map/ppermute | solution.py:10
  118.4 53.5 %all-gather.11.cloned.1.call-start = ((), (), s32[]{:S(2)}) async-start(), calls=%async_computation.2 | async-start | bytes 1572864 | tf_op jit(solution)/shard_map/all_gather | solution.py:42
  120.5 10.8 %collective-permute-start.2 = (f32[256,384]{1,0:T(8,128)S(1)}, f32[256,384]{1,0:T(8,128)S(1)}, u32[]{:S(2)}, u32[]{:S(2)}) collective-permute-start(f32[256,384]{1,0:T(8,128)S(1)} %fusion.8), channel_id=1, source_target_pairs={{0,4},{2,6},{4,8},{6,10},{8,12},{10,14},{12,16},{14,18},{16,20},{1... | collective-permute-start | bytes 1179656 | tf_op jit(solution)/shard_map/ppermute | solution.py:10
  124.2 19.1 %collective-permute-start.5 = (f32[256,512]{1,0:T(8,128)S(1)}, f32[256,512]{1,0:T(8,128)}, u32[]{:S(2)}, u32[]{:S(2)}) collective-permute-start(f32[256,512]{1,0:T(8,128)S(1)} %convolution_select_fusion.4), channel_id=1, source_target_pairs={{0,8},{2,10},{4,12},{6,14},{8,16},{10,18},{12,20},{14,22},{16,24},... | collective-permute-start | bytes 1572872 | tf_op jit(solution)/shard_map/ppermute | solution.py:10
  134.6 17.2 %collective-permute-start.4 = (f32[256,384]{1,0:T(8,128)S(1)}, f32[256,384]{1,0:T(8,128)S(1)}, u32[]{:S(2)}, u32[]{:S(2)}) collective-permute-start(f32[256,384]{1,0:T(8,128)S(1)} %fusion.7), channel_id=1, source_target_pairs={{0,8},{2,10},{4,12},{6,14},{8,16},{10,18},{12,20},{14,22},{16,24},... | collective-permute-start | bytes 1179656 | tf_op jit(solution)/shard_map/ppermute | solution.py:10
  143.3 47.0 %all-gather.15.cloned.1.call-start = ((), (), s32[]{:S(2)}) async-start(), calls=%async_computation.4 | async-start | bytes 1572864 | tf_op jit(solution)/shard_map/all_gather | solution.py:42
  145.7 16.6 %collective-permute-start.10 = (f32[256,512]{1,0:T(8,128)S(1)}, f32[256,512]{1,0:T(8,128)}, u32[]{:S(2)}, u32[]{:S(2)}) collective-permute-start(f32[256,512]{1,0:T(8,128)S(1)} %convolution_select_fusion.2), channel_id=1, source_target_pairs={{4,0},{6,2},{8,4},{10,6},{12,8},{14,10},{16,12},{18,14},{20,16},{2... | collective-permute-start | bytes 1572872 | tf_op jit(solution)/shard_map/ppermute | solution.py:10
  155.5 6.9 %copy-start.2 = (f32[256,384]{1,0:T(8,128)}, f32[256,384]{1,0:T(8,128)S(1)}, u32[]{:S(2)}) copy-start(f32[256,384]{1,0:T(8,128)S(1)} %fusion.6) | copy-start | bytes 1179652
  155.5 14.0 %collective-permute-start.6 = (f32[256,384]{1,0:T(8,128)S(1)}, f32[256,384]{1,0:T(8,128)S(1)}, u32[]{:S(2)}, u32[]{:S(2)}) collective-permute-start(f32[256,384]{1,0:T(8,128)S(1)} %fusion.6), channel_id=1, source_target_pairs={{0,16},{2,18},{4,20},{6,22},{8,24},{10,26},{12,28},{14,30},{1,17},... | collective-permute-start | bytes 1179656 | tf_op jit(solution)/shard_map/ppermute | solution.py:10
  162.3 87.8 %all-gather.17.cloned.1.call-start = ((), (), s32[]{:S(2)}) async-start(), calls=%async_computation.5 | async-start | bytes 1572864 | tf_op jit(solution)/shard_map/all_gather | solution.py:42
  176.2 99.3 %copy-start.1 = (f32[256,384]{1,0:T(8,128)}, f32[256,384]{1,0:T(8,128)S(1)}, u32[]{:S(2)}) copy-start(f32[256,384]{1,0:T(8,128)S(1)} %fusion.5) | copy-start | bytes 1179652
  189.0 13.9 %collective-permute-start.7 = (f32[256,384]{1,0:T(8,128)}, f32[256,384]{1,0:T(8,128)S(1)}, u32[]{:S(2)}, u32[]{:S(2)}) collective-permute-start(f32[256,384]{1,0:T(8,128)} %convolution_subtract_fusion), channel_id=1, source_target_pairs={{2,0},{4,2},{6,4},{8,6},{10,8},{12,10},{14,12},{16,14},{18,16},{20... | collective-permute-start | bytes 1179656 | tf_op jit(solution)/shard_map/ppermute | solution.py:10
  192.6 29.3 %collective-permute-start.12 = (f32[256,512]{1,0:T(8,128)S(1)}, f32[256,512]{1,0:T(8,128)}, u32[]{:S(2)}, u32[]{:S(2)}) collective-permute-start(f32[256,512]{1,0:T(8,128)S(1)} %convolution_select_fusion.1), channel_id=1, source_target_pairs={{8,0},{10,2},{12,4},{14,6},{16,8},{18,10},{20,12},{22,14},{24,16},... | collective-permute-start | bytes 1572872 | tf_op jit(solution)/shard_map/ppermute | solution.py:10
  207.3 14.6 %collective-permute-start.9 = (f32[256,384]{1,0:T(8,128)S(1)}, f32[256,384]{1,0:T(8,128)S(1)}, u32[]{:S(2)}, u32[]{:S(2)}) collective-permute-start(f32[256,384]{1,0:T(8,128)S(1)} %fusion.4), channel_id=1, source_target_pairs={{4,0},{6,2},{8,4},{10,6},{12,8},{14,10},{16,12},{18,14},{20,16},{2... | collective-permute-start | bytes 1179656 | tf_op jit(solution)/shard_map/ppermute | solution.py:10
  225.5 19.8 %collective-permute-start.11 = (f32[256,384]{1,0:T(8,128)S(1)}, f32[256,384]{1,0:T(8,128)S(1)}, u32[]{:S(2)}, u32[]{:S(2)}) collective-permute-start(f32[256,384]{1,0:T(8,128)S(1)} %fusion.3), channel_id=1, source_target_pairs={{8,0},{10,2},{12,4},{14,6},{16,8},{18,10},{20,12},{22,14},{24,16},... | collective-permute-start | bytes 1179656 | tf_op jit(solution)/shard_map/ppermute | solution.py:10
  248.7 22.7 %collective-permute-start.13 = (f32[256,384]{1,0:T(8,128)S(1)}, f32[256,384]{1,0:T(8,128)S(1)}, u32[]{:S(2)}, u32[]{:S(2)}) collective-permute-start(f32[256,384]{1,0:T(8,128)S(1)} %fusion.2), channel_id=1, source_target_pairs={{16,0},{18,2},{20,4},{22,6},{24,8},{26,10},{28,12},{30,14},{17,1},... | collective-permute-start | bytes 1179656 | tf_op jit(solution)/shard_map/ppermute | solution.py:10
Sparse Core Ops, SparseCore 0:
  62.0 11.2 all-gather.6
  91.0 11.0 all-gather.8
  118.5 10.3 all-gather.12
  143.4 13.6 all-gather.10
  162.4 12.2 all-gather.14
  222.0 8.6 all-gather.16
where the time goes:
time: 285 us; the launch traced here: 282 us
  waiting for transfers between devices  124 us (44%)
  starting transfers between devices  44.4 us (16%)
  matrix products  34.6 us (12%)
  local copies, waits for them, and re-layouts  29.8 us (10%)
  blocking collectives  21.6 us (8%)
  between operations  14.7 us (5%)
  other arithmetic  13.6 us (5%)
    ppermute x14, waiting for transfers between devices, shifted(): lax.ppermute(value, axis, [(source, source + steps) for source in range(f...  112 us
    ppermute x14, starting transfers between devices, shifted(): lax.ppermute(value, axis, [(source, source + steps) for source in range(f...  44.1 us
    dot_general x17, matrix products, product(): jnp.dot(left, right, precision=lax.Precision.HIGHEST, preferred_element_t...  29 us
    mul x1, local copies, waits for them, and re-layouts, body(): panel_blocks[:, :, None, :] * own_site[:, None, :, None]  24.2 us
    all_gather x8, blocking collectives, combine_levels(): lax.all_gather(far_offset, 'rows', axis=0, tiled=True)  19.3 us
    mul x1, other arithmetic, body(): panel_blocks[:, :, None, :] * own_site[:, None, :, None]  11.5 us
    all_gather x6, waiting for transfers between devices, combine_levels(): lax.all_gather(far_map, 'rows', axis=0, tiled=True)  11.5 us
  transfers between devices with their start and end apart: 20, of which 12 were waited for; matrix products, arithmetic and copies ran while one was open for 13% of the time, Pallas kernels for 0%

commit v1 on v0

v1 whole, which is shorter than its diff:
```python
import functools

import jax
import jax.numpy as jnp
from jax import lax
from jax.experimental import pallas as pl
from jax.experimental.pallas import tpu as pltpu
from jax.sharding import PartitionSpec as P

GROUP = 4
LANES = 128
BF16 = jnp.bfloat16
F32 = jnp.float32


def whole(count):
    return [pl.BlockSpec(memory_space=pltpu.VMEM)] * count


def call(kernel, operands, shapes, scratch=(), aliases=None, flops=0, bytes_accessed=0):
    return pl.pallas_call(
        kernel,
        out_shape=[jax.ShapeDtypeStruct(shape, dtype) for shape, dtype in shapes],
        in_specs=whole(len(operands)),
        out_specs=whole(len(shapes)),
        scratch_shapes=list(scratch),
        input_output_aliases=aliases or {},
        compiler_params=pltpu.CompilerParams(vmem_limit_bytes=24 << 20),
        cost_estimate=pl.CostEstimate(flops=flops, bytes_accessed=bytes_accessed, transcendentals=0),
    )(*operands)


def place():
    step = lax.axis_index("tm")
    return lax.div(step, GROUP), lax.rem(step, GROUP), lax.axis_index("rows")


def split(value):
    high = value.astype(BF16)
    return high, (value - high.astype(F32)).astype(BF16)


def multiply(value, high_ref, low_ref):
    high, low = split(value)
    count = value.shape[0]
    both = jnp.dot(jnp.concatenate([high, low], 0), high_ref, preferred_element_type=F32)
    return both[:count] + both[count:] + jnp.dot(high, low_ref, preferred_element_type=F32)


def transition(state, coef_ref, half):
    values, slopes = [], []
    for block in range(state.shape[1] // (2 * half)):
        at = 2 * half * block
        value, slope = state[:, at : at + half], state[:, at + half : at + 2 * half]
        lanes = slice(block * half, (block + 1) * half)
        values.append(coef_ref[0:1, lanes] * value + coef_ref[1:2, lanes] * slope)
        slopes.append(coef_ref[2:3, lanes] * value + coef_ref[3:4, lanes] * slope)
    moved = jnp.concatenate([part for pair in zip(values, slopes) for part in pair], 1)
    return moved, jnp.concatenate(values, 1)


def lane_tiles(value):
    return [value[:, at : at + LANES] for at in range(0, value.shape[1], LANES)]


def gain_kernel(
    share, rates_ref, mask_ref, gain_ref, obs_ref, first_ref, second_ref, own_ref, coef_ref, turned, tiles
):
    _, spot, row = place()
    panel, sites = gain_ref.shape
    half = panel // 2
    mask = mask_ref[...].astype(F32)
    for at, tile in enumerate(lane_tiles(gain_ref[...] * mask)):
        tiles[at] = tile
        lines = slice(at * LANES, (at + 1) * LANES)
        for part in range(2):
            piece = tiles[at, pl.ds(part, half, stride=2), :].T
            lanes = slice(part * half, (part + 1) * half)
            first_ref[lines, lanes] = piece
            second_ref[lines, lanes] = piece
    turned[...] = obs_ref[...].T
    rows = lax.axis_size("rows")

    def slice_for(flip):
        start = (jnp.bitwise_xor(spot, flip) * rows + row) * share
        return turned[pl.ds(pl.multiple_of(start, 8), share), :]

    first_ref[sites : sites + share, :] = slice_for(1 + row)
    first_ref[sites + share : sites + 2 * share, :] = slice_for(3)
    second_ref[sites : sites + share, :] = slice_for(2 - row)
    own_ref[...] = slice_for(0)
    rate = rates_ref[...]
    decay = jnp.exp(-rate)
    coef_ref[0:1, :] = decay * (1.0 + rate)
    coef_ref[1:2, :] = decay
    coef_ref[2:3, :] = -decay * rate * rate
    coef_ref[3:4, :] = decay * (1.0 - rate)
    coef_ref[4:8, :] = jnp.zeros((4, sites), F32)


def prior_kernel(share, half, prior_ref, out_ref, turned, tiles):
    _, spot, row = place()
    rows = lax.axis_size("rows")
    for at, tile in enumerate(lane_tiles(prior_ref[...])):
        tiles[at] = tile
        for block in range(prior_ref.shape[0] // half):
            start = (block // 2) * 2 * half + block % 2
            piece = tiles[at, pl.ds(start, half, stride=2), :].T
            turned[at * LANES : (at + 1) * LANES, block * half : (block + 1) * half] = piece
    start = (spot * rows + row) * share
    out_ref[...] = turned[pl.ds(pl.multiple_of(start, 8), share), :]


def smoother_gain_kernel(gain_ref, out_ref, turned, tiles):
    panel, states = gain_ref.shape
    half = panel // 2
    for at, tile in enumerate(lane_tiles(gain_ref[...])):
        tiles[at] = tile
        for part in range(2):
            turned[part, at * LANES : (at + 1) * LANES, :] = tiles[at, pl.ds(part, half, stride=2), :].T
    for block in range(states // half):
        start = (block // 2) * 2 * half + block % 2
        for part in range(2):
            piece = turned[part, pl.ds(start, half, stride=2), :]
            out_ref[block * half : (block + 1) * half, part * half : (part + 1) * half] = piece


def gather_kernel(share, depth, own, a, b, d, other, other_a, other_b, other_d, *rest):
    _, spot, row = place()
    high_ref, low_ref = rest[-2 - (share > 0)], rest[-1 - (share > 0)]
    for ref, flip, block in (
        (own, 0, row),
        (a, 1 + row, row),
        (b, 2 - row, row),
        (d, 3, row),
        (other, 0, 1 - row),
        (other_a, 2 - row, 1 - row),
        (other_b, 1 + row, 1 - row),
        (other_d, 3, 1 - row),
    ):
        at = jnp.bitwise_xor(spot, flip)
        high, low = split(ref[0:depth, :])
        high_ref[at, block] = high
        low_ref[at, block] = low
    if share:
        own_obs, obs_ref = rest[0], rest[-1]
        obs_ref[spot] = own_obs[...]
        obs_ref[jnp.bitwise_xor(spot, 1 + row)] = a[depth : depth + share, :]
        obs_ref[jnp.bitwise_xor(spot, 2 - row)] = b[depth : depth + share, :]
        obs_ref[jnp.bitwise_xor(spot, 3)] = d[depth + share : depth + 2 * share, :]


def filter_kernel(turn, start_ref, coef_ref, high_ref, low_ref, obs_ref, *rest):
    out_ref, last_ref = rest[-2:]
    group, _, _ = place()
    half = high_ref.shape[3] // 2

    @pl.when(group == turn)
    def _():
        state = start_ref[...]
        for step in range(GROUP):
            moved, values = transition(state, coef_ref, half)
            innovation = obs_ref[step] - values
            update = [
                multiply(innovation, high_ref[step, block], low_ref[step, block])
                for block in range(high_ref.shape[1])
            ]
            state = moved + jnp.concatenate(update, 1)
            out_ref[step] = state
        last_ref[...] = state


def smooth_kernel(turn, groups, start_ref, coef_ref, high_ref, low_ref, filt_ref, *rest):
    mine, other, first_ref = rest[-9:-5], rest[-5:-1], rest[-1]
    group, spot, row = place()
    blocks, lanes = high_ref.shape[1], high_ref.shape[3]
    half = lanes // 2

    def pack(step, kind, state):
        near = jnp.where(row == 0, state[:, :lanes], state[:, lanes:])
        far = jnp.where(row == 0, state[:, lanes:], state[:, :lanes])
        for flip in range(GROUP):

            @pl.when(spot == (step ^ flip))
            def _():
                mine[flip][kind] = near
                other[flip][kind] = far

    @pl.when(group == groups - 1 - turn)
    def _():
        state = start_ref[...]
        for step in range(GROUP - 1, -1, -1):
            filt = filt_ref[step]
            if turn == 0 and step == GROUP - 1:
                state = filt
            else:
                change = state - transition(filt, coef_ref, half)[0]
                update = [multiply(change, high_ref[step, block], low_ref[step, block]) for block in range(blocks)]
                state = filt + jnp.concatenate(update, 1)
            pack(step, 0, filt)
            pack(step, 1, state)
        first_ref[...] = state


def home_kernel(share, m0, m1, m2, m3, o0, o1, o2, o3, filt_ref, smooth_ref, turned, tiles):
    _, spot, row = place()
    rows = lax.axis_size("rows")
    half = filt_ref.shape[0] // 2
    for flip, (near, far) in enumerate(((m0, o0), (m1, o1), (m2, o2), (m3, o3))):
        start = jnp.bitwise_xor(spot, flip) * rows
        for kind in range(2):
            turned[kind, pl.ds(pl.multiple_of((start + row) * share, 8), share), :] = near[kind]
            turned[kind, pl.ds(pl.multiple_of((start + 1 - row) * share, 8), share), :] = far[kind]
    for kind, ref in enumerate((filt_ref, smooth_ref)):
        for at in range(ref.shape[1] // LANES):
            lines = slice(at * LANES, (at + 1) * LANES)
            for part in range(2):
                piece = turned[kind, lines, part * half : (part + 1) * half].T
                tiles[kind, at, pl.ds(part, half, stride=2), :] = piece
            ref[:, lines] = tiles[kind, at]


def after(value, other):
    return lax.optimization_barrier((value, other))[0]


def body(site_rates, prior_mean, observed, obs_mask, filter_gains, smooth_gains):
    count, rows = lax.axis_size("tm"), lax.axis_size("rows")
    groups = count // GROUP
    panel, sites = filter_gains.shape[1:]
    states, paths = prior_mean.shape
    half = panel // 2
    share = paths // (GROUP * rows)
    both = ("tm", "rows")

    def swap(value, target):
        pairs = [(t * rows + r, target(t, r)) for t in range(count) for r in range(rows)]
        return lax.ppermute(value, both, pairs)

    def across(value, flip, core=0):
        return swap(value, lambda t, r: (t ^ flip) * rows + (r ^ core))

    def first_way(value):
        return swap(value, lambda t, r: (t ^ (1 + r)) * rows + r)

    def second_way(value):
        return swap(value, lambda t, r: (t ^ (2 - r)) * rows + r)

    def hop(value, source, target):
        pairs = [
            ((source * GROUP + m) * rows + r, (target * GROUP + m) * rows + r) for m in range(GROUP) for r in range(rows)
        ]
        return lax.ppermute(value, both, pairs)

    def exchange(first, second):
        own_x = across(first, 0, 1)
        a, b = first_way(first), second_way(second)
        d = second_way(a)
        return (first, a, b, d, own_x, across(a, 0, 1), across(b, 0, 1), across(d, 0, 1))

    message, second, own_obs, coef = call(
        functools.partial(gain_kernel, share),
        (site_rates.reshape(1, sites), obs_mask, filter_gains[0], observed[0]),
        [((sites + 2 * share, panel), F32), ((sites + share, panel), F32), ((share, sites), F32), ((8, sites), F32)],
        [pltpu.VMEM((paths, sites), F32), pltpu.VMEM((sites // LANES, panel, LANES), F32)],
    )
    gains = exchange(message, second)
    (prior,) = call(
        functools.partial(prior_kernel, share, half),
        (prior_mean,),
        [((share, states), F32)],
        [pltpu.VMEM((paths, states), F32), pltpu.VMEM((paths // LANES, states, LANES), F32)],
    )
    (turned_gain,) = call(
        smoother_gain_kernel,
        (smooth_gains[0],),
        [((states, panel), F32)],
        [pltpu.VMEM((2, states, half), F32), pltpu.VMEM((states // LANES, panel, LANES), F32)],
    )
    turned_gain = after(turned_gain, gains[3])
    smooth_parts = exchange(turned_gain, turned_gain)

    high, low, obs = call(
        functools.partial(gather_kernel, share, sites),
        (*gains, own_obs),
        [((GROUP, rows, sites, panel), BF16)] * 2 + [((GROUP, share, sites), F32)],
    )
    start, filtered = prior, None
    for turn in range(groups):
        operands = (start, coef, high, low, obs) + (() if filtered is None else (filtered,))
        filtered, last = call(
            functools.partial(filter_kernel, turn),
            operands,
            [((GROUP, share, states), F32), ((share, states), F32)],
            aliases=None if filtered is None else {5: 0},
        )
        if turn < groups - 1:
            start = hop(last, turn, turn + 1)

    high, low = call(
        functools.partial(gather_kernel, 0, states),
        smooth_parts,
        [((GROUP, rows, states, panel), BF16)] * 2,
    )
    start, packed = last, ()
    for turn in range(groups):
        *packed, first = call(
            functools.partial(smooth_kernel, turn, groups),
            (start, coef, high, low, filtered, *packed),
            [((2, share, panel), F32)] * (2 * GROUP) + [((share, states), F32)],
            aliases={5 + i: i for i in range(len(packed))},
        )
        if turn < groups - 1:
            start = hop(first, groups - 1 - turn, groups - 2 - turn)
    mine = [packed[0]] + [across(packed[flip], flip) for flip in range(1, GROUP)]
    other = [across(packed[GROUP + flip], flip, 1) for flip in range(GROUP)]
    filt, smooth = call(
        functools.partial(home_kernel, share),
        (*mine, *other),
        [((panel, paths), F32)] * 2,
        [pltpu.VMEM((2, paths, panel), F32), pltpu.VMEM((2, paths // LANES, panel, LANES), F32)],
    )
    return filt[None], smooth[None]


def solution(mesh):
    placed = (
        P(),
        P(),
        P("tm", None, None),
        P("tm", None),
        P("tm", "rows", None),
        P("tm", "rows", None),
    )
    return jax.shard_map(
        body,
        mesh=mesh,
        in_specs=placed,
        out_specs=(P("tm", "rows", None), P("tm", "rows", None)),
        check_vma=False,
    )
```

time: 285 us -> 100 us (0.35)
  waiting for transfers between devices: 124 us -> 62 us
  matrix products: 34.6 us -> 0 us
  local copies, waits for them, and re-layouts: 29.8 us -> 4.41 us
  blocking collectives: 21.6 us -> 0 us
  starting transfers between devices: 44.4 us -> 27 us
  between operations: 14.7 us -> 0.87 us
  other arithmetic: 13.6 us -> 0 us
  Pallas kernels: 0 us -> 5.81 us
    ppermute x14 -> x27, waiting for transfers between devices: 112 us -> 62 us  [the longest x21 31.8 us: swap(): return lax.ppermute(value, both, pairs)]
    dot_general x18 -> x0, matrix products: 34.6 us -> none  [the longest x17 29 us: product(): jnp.dot(left, right, precision=lax.Precision.HIGHEST, preferred_element_t...]
    mul x1 -> x0, local copies, waits for them, and re-layouts: 24.2 us -> none  [body(): panel_blocks[:, :, None, :] * own_site[:, None, :, None]]
    all_gather x9 -> x0, blocking collectives: 21.6 us -> none  [the longest x8 19.3 us: combine_levels(): lax.all_gather(far_offset, 'rows', axis=0, tiled=True)]
    ppermute x14 -> x27, starting transfers between devices: 44.1 us -> 27 us  [the longest x21 19.7 us: swap(): return lax.ppermute(value, both, pairs)]
    mul x3 -> x0, other arithmetic: 12.3 us -> none  [the longest x1 11.5 us: body(): panel_blocks[:, :, None, :] * own_site[:, None, :, None]]
    all_gather x6 -> x0, waiting for transfers between devices: 11.5 us -> none  [combine_levels(): lax.all_gather(far_map, 'rows', axis=0, tiled=True)]
    pallas_call x0 -> x14, Pallas kernels: none -> 5.81 us  [call(): pl.pallas_call(kernel, out_shape=[jax.ShapeDtypeStruct(shape, dtype) for...]
  transfers between devices with their start and end apart: 20 -> 27, of which waited for: 12 -> 10; matrix products, arithmetic and copies ran while one was open for 13% -> 0% of each run, Pallas kernels for 0% -> 2%
where the time goes in v1:
time: 100 us
  waiting for transfers between devices  62 us (62%)
  starting transfers between devices  27 us (27%)
  Pallas kernels  5.81 us (6%)
  local copies, waits for them, and re-layouts  4.41 us (4%)
    ppermute x21, waiting for transfers between devices, swap(): return lax.ppermute(value, both, pairs)  31.8 us
    ppermute x6, waiting for transfers between devices, hop(): return lax.ppermute(value, both, pairs)  30.2 us
    ppermute x21, starting transfers between devices, swap(): return lax.ppermute(value, both, pairs)  19.7 us
    ppermute x6, starting transfers between devices, hop(): return lax.ppermute(value, both, pairs)  7.22 us
    pallas_call x14, Pallas kernels, call(): pl.pallas_call(kernel, out_shape=[jax.ShapeDtypeStruct(shape, dtype) for...  5.81 us
    unnamed x12, local copies, waits for them, and re-layouts  4.41 us
  transfers between devices with their start and end apart: 27, of which 10 were waited for; matrix products, arithmetic and copies ran while one was open for 0% of the time, Pallas kernels for 2%

profile of v1, /device:TPU:0, one launch (start us, length us, event | category | flops | bytes accessed | tf_op | source)
XLA Modules:
  0.0 100.1 jit_solution(4788726330311825830)
XLA Ops:
  0.7 1.1 %copy-done.2 = f32[1,256,384]{2,1,0:T(8,128)S(1)} copy-done((f32[1,256,384]{2,1,0:T(8,128)S(1)}, f32[1,256,384]{2,1,0:T(8,128)}, u32[]{:S(2)}) %copy-start.2) | copy-done | bytes 393240
  1.7 0.9 copy-done.3
  2.7 0.7 copy-done.4
  3.3 0.7 copy-done.5
  4.3 3.0 %collective-permute-start = (f32[352,256]{1,0:T(8,128)S(1)}, f32[352,256]{1,0:T(8,128)S(1)}, u32[]{:S(2)}, u32[]{:S(2)}) collective-permute-start(f32[352,256]{1,0:T(8,128)S(1)} %get-tuple-element.58.own), channel_id=1, source_target_pairs={{0,2},{1,5},{2,0},{3,7},{4,6},{5,1},{6,4},{7,3},{8,10},{9,13},{10,... | collective-permute-start | bytes 1081352 | tf_op jit(solution)/shard_map/ppermute | solution.py:238
  7.3 5.4 %collective-permute-done.a = f32[352,256]{1,0:T(8,128)S(1)} collective-permute-done((f32[352,256]{1,0:T(8,128)S(1)}, f32[352,256]{1,0:T(8,128)S(1)}, u32[]{:S(2)}, u32[]{:S(2)}) %collective-permute-start) | collective-permute-done | bytes 360480 | tf_op jit(solution)/shard_map/ppermute | solution.py:238
  12.7 2.0 %collective-permute-start.2 = (f32[352,256]{1,0:T(8,128)S(1)}, f32[352,256]{1,0:T(8,128)S(1)}, u32[]{:S(2)}, u32[]{:S(2)}) collective-permute-start(f32[352,256]{1,0:T(8,128)S(1)} %collective-permute-done.a), channel_id=1, source_target_pairs={{0,4},{1,3},{2,6},{3,1},{4,0},{5,7},{6,2},{7,5},{8,12},{9,11},{10,... | collective-permute-start | bytes 1081352 | tf_op jit(solution)/shard_map/ppermute | solution.py:238
  14.7 1.0 %copy-done.1 = f32[1,256,512]{2,1,0:T(8,128)S(1)} copy-done((f32[1,256,512]{2,1,0:T(8,128)S(1)}, f32[1,256,512]{2,1,0:T(8,128)}, u32[]{:S(2)}) %copy-start.1) | copy-done | bytes 524312
  16.1 4.1 %collective-permute-done.2.d = f32[352,256]{1,0:T(8,128)S(1)} collective-permute-done((f32[352,256]{1,0:T(8,128)S(1)}, f32[352,256]{1,0:T(8,128)S(1)}, u32[]{:S(2)}, u32[]{:S(2)}) %collective-permute-start.2) | collective-permute-done | bytes 360480 | tf_op jit(solution)/shard_map/ppermute | solution.py:238
  20.1 2.0 %collective-permute-start.10 = (f32[512,256]{1,0:T(8,128)S(1)}, f32[512,256]{1,0:T(8,128)S(1)}, u32[]{:S(2)}, u32[]{:S(2)}) collective-permute-start(f32[512,256]{1,0:T(8,128)S(1)} %shard_map.84.own), channel_id=1, source_target_pairs={{0,2},{1,5},{2,0},{3,7},{4,6},{5,1},{6,4},{7,3},{8,10},{9,13},{10,... | collective-permute-start | bytes 1572872 | tf_op jit(solution)/shard_map/ppermute | solution.py:238
  22.1 1.5 %collective-permute-start.1 = (f32[304,256]{1,0:T(8,128)S(1)}, f32[304,256]{1,0:T(8,128)S(1)}, u32[]{:S(2)}, u32[]{:S(2)}) collective-permute-start(f32[304,256]{1,0:T(8,128)S(1)} %get-tuple-element.59), channel_id=1, source_target_pairs={{0,4},{1,3},{2,6},{3,1},{4,0},{5,7},{6,2},{7,5},{8,12},{9,11},{10,... | collective-permute-start | bytes 933896 | tf_op jit(solution)/shard_map/ppermute | solution.py:238
  24.2 10.8 %collective-permute-done.10.a = f32[512,256]{1,0:T(8,128)S(1)} collective-permute-done((f32[512,256]{1,0:T(8,128)S(1)}, f32[512,256]{1,0:T(8,128)S(1)}, u32[]{:S(2)}, u32[]{:S(2)}) %collective-permute-start.10) | collective-permute-done | bytes 524320 | tf_op jit(solution)/shard_map/ppermute | solution.py:238
  35.0 2.1 %collective-permute-start.12 = (f32[512,256]{1,0:T(8,128)S(1)}, f32[512,256]{1,0:T(8,128)S(1)}, u32[]{:S(2)}, u32[]{:S(2)}) collective-permute-start(f32[512,256]{1,0:T(8,128)S(1)} %collective-permute-done.10.a), channel_id=1, source_target_pairs={{0,4},{1,3},{2,6},{3,1},{4,0},{5,7},{6,2},{7,5},{8,12},{9,11},{10,... | collective-permute-start | bytes 1572872 | tf_op jit(solution)/shard_map/ppermute | solution.py:238
  37.6 1.2 %collective-permute-done.3.other = f32[352,256]{1,0:T(8,128)S(1)} collective-permute-done((f32[352,256]{1,0:T(8,128)S(1)}, f32[352,256]{1,0:T(8,128)S(1)}, u32[]{:S(2)}, u32[]{:S(2)}) %collective-permute-start.3) | collective-permute-done | bytes 360480 | tf_op jit(solution)/shard_map/ppermute | solution.py:238
  38.8 0.8 collective-permute-done.5.other_b
  40.3 3.9 %collective-permute-done.12.d = f32[512,256]{1,0:T(8,128)S(1)} collective-permute-done((f32[512,256]{1,0:T(8,128)S(1)}, f32[512,256]{1,0:T(8,128)S(1)}, u32[]{:S(2)}, u32[]{:S(2)}) %collective-permute-start.12) | collective-permute-done | bytes 524320 | tf_op jit(solution)/shard_map/ppermute | solution.py:238
  44.8 0.7 shard_map.80
  45.6 3.3 %collective-permute-start.7 = (f32[48,512]{1,0:T(8,128)S(1)}, f32[48,512]{1,0:T(8,128)S(1)}, u32[]{:S(2)}, u32[]{:S(2)}) collective-permute-start(f32[48,512]{1,0:T(8,128)S(1)} %get-tuple-element.64), channel_id=1, source_target_pairs={{0,8},{1,9},{2,10},{3,11},{4,12},{5,13},{6,14},{7,15}} | collective-permute-start | bytes 294920 | tf_op jit(solution)/shard_map/ppermute | solution.py:253
  48.9 2.7 %collective-permute-done.7.start_ref = f32[48,512]{1,0:T(8,128)S(1)} collective-permute-done((f32[48,512]{1,0:T(8,128)S(1)}, f32[48,512]{1,0:T(8,128)S(1)}, u32[]{:S(2)}, u32[]{:S(2)}) %collective-permute-start.7) | collective-permute-done | bytes 98336 | tf_op jit(solution)/shard_map/ppermute | solution.py:253
  53.0 0.8 shard_map.85
  53.8 0.7 collective-permute-start.17
  55.3 1.3 %collective-permute-start.19 = (f32[48,512]{1,0:T(8,128)S(1)}, f32[48,512]{1,0:T(8,128)S(1)}, u32[]{:S(2)}, u32[]{:S(2)}) collective-permute-start(f32[48,512]{1,0:T(8,128)S(1)} %get-tuple-element.93), channel_id=1, source_target_pairs={{8,0},{9,1},{10,2},{11,3},{12,4},{13,5},{14,6},{15,7}} | collective-permute-start | bytes 294920 | tf_op jit(solution)/shard_map/ppermute | solution.py:253
  56.6 27.5 %collective-permute-done.19.start_ref = f32[48,512]{1,0:T(8,128)S(1)} collective-permute-done((f32[48,512]{1,0:T(8,128)S(1)}, f32[48,512]{1,0:T(8,128)S(1)}, u32[]{:S(2)}, u32[]{:S(2)}) %collective-permute-start.19) | collective-permute-done | bytes 98336 | tf_op jit(solution)/shard_map/ppermute | solution.py:253
  84.1 1.9 %shard_map.89 = (f32[2,48,256]{2,1,0:T(8,128)S(1)}, f32[2,48,256]{2,1,0:T(8,128)S(1)}, f32[2,48,256]{2,1,0:T(8,128)S(1)}, f32[2,48,256]{2,1,0:T(8,128)S(1)}, f32...) custom-call(f32[48,512]{1,0:T(8,128)S(1)} %collective-permute-done.1, ...), custom_call_target="tpu_custom_call", output_to_operand_aliasing={{0}: (5, {}), {1}: (6, {}), {2}: (7, {}), {3}: (8, {}), {4}... | custom-call | tf_op jit(solution)/shard_map/pallas_call | solution.py:21
  86.0 1.5 %collective-permute-start.20 = (f32[2,48,256]{2,1,0:T(8,128)S(1)}, f32[2,48,256]{2,1,0:T(8,128)S(1)}, u32[]{:S(2)}, u32[]{:S(2)}) collective-permute-start(f32[2,48,256]{2,1,0:T(8,128)S(1)} %get-tuple-element.103), channel_id=1, source_target_pairs={{0,2},{1,3},{2,0},{3,1},{4,6},{5,7},{6,4},{7,5},{8,10},{9,11},{10,... | collective-permute-start | bytes 294920 | tf_op jit(solution)/shard_map/ppermute | solution.py:238
  87.5 1.5 %collective-permute-start.21 = (f32[2,48,256]{2,1,0:T(8,128)S(1)}, f32[2,48,256]{2,1,0:T(8,128)S(1)}, u32[]{:S(2)}, u32[]{:S(2)}) collective-permute-start(f32[2,48,256]{2,1,0:T(8,128)S(1)} %get-tuple-element.104), channel_id=1, source_target_pairs={{0,4},{1,5},{2,6},{3,7},{4,0},{5,1},{6,2},{7,3},{8,12},{9,13},{10,... | collective-permute-start | bytes 294920 | tf_op jit(solution)/shard_map/ppermute | solution.py:238
  89.5 1.6 %collective-permute-start.24 = (f32[2,48,256]{2,1,0:T(8,128)S(1)}, f32[2,48,256]{2,1,0:T(8,128)S(1)}, u32[]{:S(2)}, u32[]{:S(2)}) collective-permute-start(f32[2,48,256]{2,1,0:T(8,128)S(1)} %get-tuple-element.107), channel_id=1, source_target_pairs={{0,3},{1,2},{2,1},{3,0},{4,7},{5,6},{6,5},{7,4},{8,11},{9,10},{10,... | collective-permute-start | bytes 294920 | tf_op jit(solution)/shard_map/ppermute | solution.py:238
  91.1 1.1 %collective-permute-start.25 = (f32[2,48,256]{2,1,0:T(8,128)S(1)}, f32[2,48,256]{2,1,0:T(8,128)S(1)}, u32[]{:S(2)}, u32[]{:S(2)}) collective-permute-start(f32[2,48,256]{2,1,0:T(8,128)S(1)} %get-tuple-element.108), channel_id=1, source_target_pairs={{0,5},{1,4},{2,7},{3,6},{4,1},{5,0},{6,3},{7,2},{8,13},{9,12},{10,... | collective-permute-start | bytes 294920 | tf_op jit(solution)/shard_map/ppermute | solution.py:238
  92.2 1.1 %collective-permute-start.26 = (f32[2,48,256]{2,1,0:T(8,128)S(1)}, f32[2,48,256]{2,1,0:T(8,128)S(1)}, u32[]{:S(2)}, u32[]{:S(2)}) collective-permute-start(f32[2,48,256]{2,1,0:T(8,128)S(1)} %get-tuple-element.109), channel_id=1, source_target_pairs={{0,7},{1,6},{2,5},{3,4},{4,3},{5,2},{6,1},{7,0},{8,15},{9,14},{10,... | collective-permute-start | bytes 294920 | tf_op jit(solution)/shard_map/ppermute | solution.py:238
  93.3 2.3 %collective-permute-done.22.m3 = f32[2,48,256]{2,1,0:T(8,128)S(1)} collective-permute-done((f32[2,48,256]{2,1,0:T(8,128)S(1)}, f32[2,48,256]{2,1,0:T(8,128)S(1)}, u32[]{:S(2)}, u32[]{:S(2)}) %collective-permute-start.22) | collective-permute-done | bytes 98336 | tf_op jit(solution)/shard_map/ppermute | solution.py:238
  95.6 3.3 %collective-permute-done.25.o2 = f32[2,48,256]{2,1,0:T(8,128)S(1)} collective-permute-done((f32[2,48,256]{2,1,0:T(8,128)S(1)}, f32[2,48,256]{2,1,0:T(8,128)S(1)}, u32[]{:S(2)}, u32[]{:S(2)}) %collective-permute-start.25) | collective-permute-done | bytes 98336 | tf_op jit(solution)/shard_map/ppermute | solution.py:238
  98.9 1.2 %shard_map.90 = (f32[256,384]{1,0:T(8,128)}, f32[256,384]{1,0:T(8,128)}) custom-call(f32[2,48,256]{2,1,0:T(8,128)S(1)} %get-tuple-element.102.m0, f32[2,48,256]{2,1,0:T(8,128)S(1)} %collective-permute-done.20.m1, f32[2,48,256]{2,1,0:T(8,128)S(1)} %collective-permute-done.21.m2, f32[2,48,256]{2,1,0:T(8,128)S(1)} %collective-permute-done.22.m3, ...), custom_call_target="tpu_custom_call" | custom-call | tf_op jit(solution)/shard_map/pallas_call | solution.py:21
  (48 shorter events, 5.6 us)
Async XLA Ops:
  0.6 43.6 %copy-start = (f32[512,384]{1,0:T(8,128)S(1)}, f32[512,384]{1,0:T(8,128)}, u32[]{:S(2)}) copy-start(f32[512,384]{1,0:T(8,128)} %prior_ref.1) | copy-start | bytes 2359300
  0.6 1.1 %copy-start.2 = (f32[1,256,384]{2,1,0:T(8,128)S(1)}, f32[1,256,384]{2,1,0:T(8,128)}, u32[]{:S(2)}) copy-start(f32[1,256,384]{2,1,0:T(8,128)} %param.8) | copy-start | bytes 1179652
  1.7 0.9 copy-start.3
  3.3 0.7 copy-start.5
  4.3 8.4 %collective-permute-start = (f32[352,256]{1,0:T(8,128)S(1)}, f32[352,256]{1,0:T(8,128)S(1)}, u32[]{:S(2)}, u32[]{:S(2)}) collective-permute-start(f32[352,256]{1,0:T(8,128)S(1)} %get-tuple-element.58.own), channel_id=1, source_target_pairs={{0,2},{1,5},{2,0},{3,7},{4,6},{5,1},{6,4},{7,3},{8,10},{9,13},{10,... | collective-permute-start | bytes 1081352 | tf_op jit(solution)/shard_map/ppermute | solution.py:238
  12.7 7.5 %collective-permute-start.2 = (f32[352,256]{1,0:T(8,128)S(1)}, f32[352,256]{1,0:T(8,128)S(1)}, u32[]{:S(2)}, u32[]{:S(2)}) collective-permute-start(f32[352,256]{1,0:T(8,128)S(1)} %collective-permute-done.a), channel_id=1, source_target_pairs={{0,4},{1,3},{2,6},{3,1},{4,0},{5,7},{6,2},{7,5},{8,12},{9,11},{10,... | collective-permute-start | bytes 1081352 | tf_op jit(solution)/shard_map/ppermute | solution.py:238
  14.7 1.0 %copy-start.1 = (f32[1,256,512]{2,1,0:T(8,128)S(1)}, f32[1,256,512]{2,1,0:T(8,128)}, u32[]{:S(2)}) copy-start(f32[1,256,512]{2,1,0:T(8,128)} %param.11) | copy-start | bytes 1572868
  20.1 14.8 %collective-permute-start.10 = (f32[512,256]{1,0:T(8,128)S(1)}, f32[512,256]{1,0:T(8,128)S(1)}, u32[]{:S(2)}, u32[]{:S(2)}) collective-permute-start(f32[512,256]{1,0:T(8,128)S(1)} %shard_map.84.own), channel_id=1, source_target_pairs={{0,2},{1,5},{2,0},{3,7},{4,6},{5,1},{6,4},{7,3},{8,10},{9,13},{10,... | collective-permute-start | bytes 1572872 | tf_op jit(solution)/shard_map/ppermute | solution.py:238
  22.1 15.4 %collective-permute-start.1 = (f32[304,256]{1,0:T(8,128)S(1)}, f32[304,256]{1,0:T(8,128)S(1)}, u32[]{:S(2)}, u32[]{:S(2)}) collective-permute-start(f32[304,256]{1,0:T(8,128)S(1)} %get-tuple-element.59), channel_id=1, source_target_pairs={{0,4},{1,3},{2,6},{3,1},{4,0},{5,7},{6,2},{7,5},{8,12},{9,11},{10,... | collective-permute-start | bytes 933896 | tf_op jit(solution)/shard_map/ppermute | solution.py:238
  23.7 16.5 %collective-permute-start.11 = (f32[512,256]{1,0:T(8,128)S(1)}, f32[512,256]{1,0:T(8,128)S(1)}, u32[]{:S(2)}, u32[]{:S(2)}) collective-permute-start(f32[512,256]{1,0:T(8,128)S(1)} %shard_map.84.own), channel_id=1, source_target_pairs={{0,4},{1,3},{2,6},{3,1},{4,0},{5,7},{6,2},{7,5},{8,12},{9,11},{10,... | collective-permute-start | bytes 1572872 | tf_op jit(solution)/shard_map/ppermute | solution.py:238
  35.0 9.2 %collective-permute-start.12 = (f32[512,256]{1,0:T(8,128)S(1)}, f32[512,256]{1,0:T(8,128)S(1)}, u32[]{:S(2)}, u32[]{:S(2)}) collective-permute-start(f32[512,256]{1,0:T(8,128)S(1)} %collective-permute-done.10.a), channel_id=1, source_target_pairs={{0,4},{1,3},{2,6},{3,1},{4,0},{5,7},{6,2},{7,5},{8,12},{9,11},{10,... | collective-permute-start | bytes 1572872 | tf_op jit(solution)/shard_map/ppermute | solution.py:238
  37.0 1.7 %collective-permute-start.3 = (f32[352,256]{1,0:T(8,128)S(1)}, f32[352,256]{1,0:T(8,128)S(1)}, u32[]{:S(2)}, u32[]{:S(2)}) collective-permute-start(f32[352,256]{1,0:T(8,128)S(1)} %get-tuple-element.58.own), channel_id=1, source_target_pairs={{0,1},{1,0},{2,3},{3,2},{4,5},{5,4},{6,7},{7,6},{8,9},{9,8},{10,11... | collective-permute-start | bytes 1081352 | tf_op jit(solution)/shard_map/ppermute | solution.py:238
  37.0 2.8 %collective-permute-start.4 = (f32[352,256]{1,0:T(8,128)S(1)}, f32[352,256]{1,0:T(8,128)S(1)}, u32[]{:S(2)}, u32[]{:S(2)}) collective-permute-start(f32[352,256]{1,0:T(8,128)S(1)} %collective-permute-done.a), channel_id=1, source_target_pairs={{0,1},{1,0},{2,3},{3,2},{4,5},{5,4},{6,7},{7,6},{8,9},{9,8},{10,11... | collective-permute-start | bytes 1081352 | tf_op jit(solution)/shard_map/ppermute | solution.py:238
  37.5 2.1 %collective-permute-start.5 = (f32[304,256]{1,0:T(8,128)S(1)}, f32[304,256]{1,0:T(8,128)S(1)}, u32[]{:S(2)}, u32[]{:S(2)}) collective-permute-start(f32[304,256]{1,0:T(8,128)S(1)} %collective-permute-done.1.b), channel_id=1, source_target_pairs={{0,1},{1,0},{2,3},{3,2},{4,5},{5,4},{6,7},{7,6},{8,9},{9,8},{10,11... | collective-permute-start | bytes 933896 | tf_op jit(solution)/shard_map/ppermute | solution.py:238
  38.7 5.8 %collective-permute-start.6 = (f32[352,256]{1,0:T(8,128)S(1)}, f32[352,256]{1,0:T(8,128)S(1)}, u32[]{:S(2)}, u32[]{:S(2)}) collective-permute-start(f32[352,256]{1,0:T(8,128)S(1)} %collective-permute-done.2.d), channel_id=1, source_target_pairs={{0,1},{1,0},{2,3},{3,2},{4,5},{5,4},{6,7},{7,6},{8,9},{9,8},{10,11... | collective-permute-start | bytes 1081352 | tf_op jit(solution)/shard_map/ppermute | solution.py:238
  39.7 13.3 %collective-permute-start.13 = (f32[512,256]{1,0:T(8,128)S(1)}, f32[512,256]{1,0:T(8,128)S(1)}, u32[]{:S(2)}, u32[]{:S(2)}) collective-permute-start(f32[512,256]{1,0:T(8,128)S(1)} %shard_map.84.own), channel_id=1, source_target_pairs={{0,1},{1,0},{2,3},{3,2},{4,5},{5,4},{6,7},{7,6},{8,9},{9,8},{10,11... | collective-permute-start | bytes 1572872 | tf_op jit(solution)/shard_map/ppermute | solution.py:238
  39.8 13.2 %collective-permute-start.14 = (f32[512,256]{1,0:T(8,128)S(1)}, f32[512,256]{1,0:T(8,128)S(1)}, u32[]{:S(2)}, u32[]{:S(2)}) collective-permute-start(f32[512,256]{1,0:T(8,128)S(1)} %collective-permute-done.10.a), channel_id=1, source_target_pairs={{0,1},{1,0},{2,3},{3,2},{4,5},{5,4},{6,7},{7,6},{8,9},{9,8},{10,11... | collective-permute-start | bytes 1572872 | tf_op jit(solution)/shard_map/ppermute | solution.py:238
  40.2 12.8 %collective-permute-start.15 = (f32[512,256]{1,0:T(8,128)S(1)}, f32[512,256]{1,0:T(8,128)S(1)}, u32[]{:S(2)}, u32[]{:S(2)}) collective-permute-start(f32[512,256]{1,0:T(8,128)S(1)} %collective-permute-done.11.b), channel_id=1, source_target_pairs={{0,1},{1,0},{2,3},{3,2},{4,5},{5,4},{6,7},{7,6},{8,9},{9,8},{10,11... | collective-permute-start | bytes 1572872 | tf_op jit(solution)/shard_map/ppermute | solution.py:238
  44.2 8.8 %collective-permute-start.16 = (f32[512,256]{1,0:T(8,128)S(1)}, f32[512,256]{1,0:T(8,128)S(1)}, u32[]{:S(2)}, u32[]{:S(2)}) collective-permute-start(f32[512,256]{1,0:T(8,128)S(1)} %collective-permute-done.12.d), channel_id=1, source_target_pairs={{0,1},{1,0},{2,3},{3,2},{4,5},{5,4},{6,7},{7,6},{8,9},{9,8},{10,11... | collective-permute-start | bytes 1572872 | tf_op jit(solution)/shard_map/ppermute | solution.py:238
  45.6 6.0 %collective-permute-start.7 = (f32[48,512]{1,0:T(8,128)S(1)}, f32[48,512]{1,0:T(8,128)S(1)}, u32[]{:S(2)}, u32[]{:S(2)}) collective-permute-start(f32[48,512]{1,0:T(8,128)S(1)} %get-tuple-element.64), channel_id=1, source_target_pairs={{0,8},{1,9},{2,10},{3,11},{4,12},{5,13},{6,14},{7,15}} | collective-permute-start | bytes 294920 | tf_op jit(solution)/shard_map/ppermute | solution.py:253
  51.6 0.7 collective-permute-start.8
  52.3 0.7 collective-permute-start.9
  53.8 0.7 collective-permute-start.17
  54.5 0.7 collective-permute-start.18
  55.3 28.8 %collective-permute-start.19 = (f32[48,512]{1,0:T(8,128)S(1)}, f32[48,512]{1,0:T(8,128)S(1)}, u32[]{:S(2)}, u32[]{:S(2)}) collective-permute-start(f32[48,512]{1,0:T(8,128)S(1)} %get-tuple-element.93), channel_id=1, source_target_pairs={{8,0},{9,1},{10,2},{11,3},{12,4},{13,5},{14,6},{15,7}} | collective-permute-start | bytes 294920 | tf_op jit(solution)/shard_map/ppermute | solution.py:253
  86.0 5.1 %collective-permute-start.20 = (f32[2,48,256]{2,1,0:T(8,128)S(1)}, f32[2,48,256]{2,1,0:T(8,128)S(1)}, u32[]{:S(2)}, u32[]{:S(2)}) collective-permute-start(f32[2,48,256]{2,1,0:T(8,128)S(1)} %get-tuple-element.103), channel_id=1, source_target_pairs={{0,2},{1,3},{2,0},{3,1},{4,6},{5,7},{6,4},{7,5},{8,10},{9,11},{10,... | collective-permute-start | bytes 294920 | tf_op jit(solution)/shard_map/ppermute | solution.py:238
  87.5 4.7 %collective-permute-start.21 = (f32[2,48,256]{2,1,0:T(8,128)S(1)}, f32[2,48,256]{2,1,0:T(8,128)S(1)}, u32[]{:S(2)}, u32[]{:S(2)}) collective-permute-start(f32[2,48,256]{2,1,0:T(8,128)S(1)} %get-tuple-element.104), channel_id=1, source_target_pairs={{0,4},{1,5},{2,6},{3,7},{4,0},{5,1},{6,2},{7,3},{8,12},{9,13},{10,... | collective-permute-start | bytes 294920 | tf_op jit(solution)/shard_map/ppermute | solution.py:238
  89.0 6.6 %collective-permute-start.22 = (f32[2,48,256]{2,1,0:T(8,128)S(1)}, f32[2,48,256]{2,1,0:T(8,128)S(1)}, u32[]{:S(2)}, u32[]{:S(2)}) collective-permute-start(f32[2,48,256]{2,1,0:T(8,128)S(1)} %get-tuple-element.105), channel_id=1, source_target_pairs={{0,6},{1,7},{2,4},{3,5},{4,2},{5,3},{6,0},{7,1},{8,14},{9,15},{10,... | collective-permute-start | bytes 294920 | tf_op jit(solution)/shard_map/ppermute | solution.py:238
  89.4 6.2 %collective-permute-start.23 = (f32[2,48,256]{2,1,0:T(8,128)S(1)}, f32[2,48,256]{2,1,0:T(8,128)S(1)}, u32[]{:S(2)}, u32[]{:S(2)}) collective-permute-start(f32[2,48,256]{2,1,0:T(8,128)S(1)} %get-tuple-element.106), channel_id=1, source_target_pairs={{0,1},{1,0},{2,3},{3,2},{4,5},{5,4},{6,7},{7,6},{8,9},{9,8},{10,11... | collective-permute-start | bytes 294920 | tf_op jit(solution)/shard_map/ppermute | solution.py:238
  89.5 6.2 %collective-permute-start.24 = (f32[2,48,256]{2,1,0:T(8,128)S(1)}, f32[2,48,256]{2,1,0:T(8,128)S(1)}, u32[]{:S(2)}, u32[]{:S(2)}) collective-permute-start(f32[2,48,256]{2,1,0:T(8,128)S(1)} %get-tuple-element.107), channel_id=1, source_target_pairs={{0,3},{1,2},{2,1},{3,0},{4,7},{5,6},{6,5},{7,4},{8,11},{9,10},{10,... | collective-permute-start | bytes 294920 | tf_op jit(solution)/shard_map/ppermute | solution.py:238
  91.1 7.9 %collective-permute-start.25 = (f32[2,48,256]{2,1,0:T(8,128)S(1)}, f32[2,48,256]{2,1,0:T(8,128)S(1)}, u32[]{:S(2)}, u32[]{:S(2)}) collective-permute-start(f32[2,48,256]{2,1,0:T(8,128)S(1)} %get-tuple-element.108), channel_id=1, source_target_pairs={{0,5},{1,4},{2,7},{3,6},{4,1},{5,0},{6,3},{7,2},{8,13},{9,12},{10,... | collective-permute-start | bytes 294920 | tf_op jit(solution)/shard_map/ppermute | solution.py:238
  92.2 6.7 %collective-permute-start.26 = (f32[2,48,256]{2,1,0:T(8,128)S(1)}, f32[2,48,256]{2,1,0:T(8,128)S(1)}, u32[]{:S(2)}, u32[]{:S(2)}) collective-permute-start(f32[2,48,256]{2,1,0:T(8,128)S(1)} %get-tuple-element.109), channel_id=1, source_target_pairs={{0,7},{1,6},{2,5},{3,4},{4,3},{5,2},{6,1},{7,0},{8,15},{9,14},{10,... | collective-permute-start | bytes 294920 | tf_op jit(solution)/shard_map/ppermute | solution.py:238
  (1 other events, 0.7 us)

commit v2 on v1

v2 whole, which is shorter than its diff:
```python
import functools

import jax
import jax.numpy as jnp
from jax import lax
from jax.experimental import pallas as pl
from jax.experimental.pallas import tpu as pltpu
from jax.sharding import PartitionSpec as P

GROUP = 4
LANES = 128
PIECES = 1
FW = (0, 0, 10**11, 10**11)
BW = (0, 0, 10**10, 10**10)
G1 = G2 = G3 = 10**9
G4 = 10**9
G5 = 10**10
BF16 = jnp.bfloat16
F32 = jnp.float32


def call(kernel, operands, shapes, scratch=(), aliases=None, source=pltpu.VMEM, bytes_accessed=2 << 20, flops=0, grant=24 << 20):
    return pl.pallas_call(
        kernel,
        out_shape=[jax.ShapeDtypeStruct(shape, dtype) for shape, dtype in shapes],
        in_specs=[pl.BlockSpec(memory_space=source)] * len(operands),
        out_specs=[pl.BlockSpec(memory_space=pltpu.VMEM)] * len(shapes),
        scratch_shapes=list(scratch),
        input_output_aliases=aliases or {},
        compiler_params=pltpu.CompilerParams(vmem_limit_bytes=grant),
        cost_estimate=pl.CostEstimate(flops=flops, bytes_accessed=bytes_accessed, transcendentals=0),
    )(*operands)


def place():
    step = lax.axis_index("tm")
    return lax.div(step, GROUP), lax.rem(step, GROUP), lax.axis_index("rows")


def split(value):
    high = value.astype(BF16)
    return high, (value - high.astype(F32)).astype(BF16)


def multiply(value, high_ref, low_ref):
    high, low = split(value)
    count = value.shape[0]
    both = jnp.dot(jnp.concatenate([high, low], 0), high_ref, preferred_element_type=F32)
    return both[:count] + both[count:] + jnp.dot(high, low_ref, preferred_element_type=F32)


def transition(state, coef_ref, half):
    values, slopes = [], []
    for block in range(state.shape[1] // (2 * half)):
        at = 2 * half * block
        value, slope = state[:, at : at + half], state[:, at + half : at + 2 * half]
        lanes = slice(block * half, (block + 1) * half)
        values.append(coef_ref[0:1, lanes] * value + coef_ref[1:2, lanes] * slope)
        slopes.append(coef_ref[2:3, lanes] * value + coef_ref[3:4, lanes] * slope)
    moved = jnp.concatenate([part for pair in zip(values, slopes) for part in pair], 1)
    return moved, jnp.concatenate(values, 1)


def lane_tiles(value):
    return [value[:, at : at + LANES] for at in range(0, value.shape[1], LANES)]


def fetch(source, target, sem):
    copy = pltpu.make_async_copy(source, target, sem)
    copy.start()
    return copy


def gain_kernel(
    share,
    rates_hbm,
    mask_hbm,
    gain_hbm,
    obs_hbm,
    first_ref,
    second_ref,
    third_ref,
    own_ref,
    coef_ref,
    rates_ref,
    mask_ref,
    gain_ref,
    obs_ref,
    turned,
    tiles,
    sems,
):
    sent = (first_ref, second_ref, third_ref)
    copies = [
        fetch(source, target, sems.at[at])
        for at, (source, target) in enumerate(
            ((mask_hbm, mask_ref), (gain_hbm, gain_ref), (obs_hbm, obs_ref), (rates_hbm, rates_ref))
        )
    ]
    _, spot, row = place()
    panel, sites = gain_ref.shape
    half = panel // 2
    copies[0].wait()
    copies[1].wait()
    mask = mask_ref[...].astype(F32)
    for at, tile in enumerate(lane_tiles(gain_ref[...] * mask)):
        tiles[at] = tile
        lines = slice(at * LANES, (at + 1) * LANES)
        for part in range(2):
            piece = tiles[at, pl.ds(part, half, stride=2), :].T
            lanes = slice(part * half, (part + 1) * half)
            for ref in sent:
                ref[lines, lanes] = piece
    copies[2].wait()
    turned[...] = obs_ref[...].T
    rows = lax.axis_size("rows")

    def slice_for(flip):
        start = (jnp.bitwise_xor(spot, flip) * rows + row) * share
        return turned[pl.ds(pl.multiple_of(start, 8), share), :]

    for flip, ref in enumerate(sent, 1):
        ref[sites : sites + share, :] = slice_for(flip)
    own_ref[...] = slice_for(0)
    copies[3].wait()
    rate = rates_ref[...]
    decay = jnp.exp(-rate)
    coef_ref[0:1, :] = decay * (1.0 + rate)
    coef_ref[1:2, :] = decay
    coef_ref[2:3, :] = -decay * rate * rate
    coef_ref[3:4, :] = decay * (1.0 - rate)
    coef_ref[4:8, :] = jnp.zeros((4, sites), F32)


def prior_kernel(share, half, prior_ref, out_ref, turned, tiles):
    _, spot, row = place()
    rows = lax.axis_size("rows")
    for at, tile in enumerate(lane_tiles(prior_ref[...])):
        tiles[at] = tile
        for block in range(prior_ref.shape[0] // half):
            start = (block // 2) * 2 * half + block % 2
            piece = tiles[at, pl.ds(start, half, stride=2), :].T
            turned[at * LANES : (at + 1) * LANES, block * half : (block + 1) * half] = piece
    start = (spot * rows + row) * share
    out_ref[...] = turned[pl.ds(pl.multiple_of(start, 8), share), :]


def smoother_gain_kernel(gain_ref, *refs):
    parts, (turned, tiles) = refs[:-2], refs[-2:]
    depth = parts[0].shape[0]
    panel, states = gain_ref.shape
    half = panel // 2
    for at, tile in enumerate(lane_tiles(gain_ref[...])):
        tiles[at] = tile
        for part in range(2):
            turned[part, at * LANES : (at + 1) * LANES, :] = tiles[at, pl.ds(part, half, stride=2), :].T
    for block in range(states // half):
        start = (block // 2) * 2 * half + block % 2
        for part in range(2):
            piece = turned[part, pl.ds(start, half, stride=2), :]
            at = block * half % depth
            parts[block * half // depth][at : at + half, part * half : (part + 1) * half] = piece


def gather_kernel(share, depth, *refs):
    _, spot, row = place()
    near, far, rest = refs[:GROUP], refs[GROUP : 2 * GROUP], refs[2 * GROUP :]
    high_ref, low_ref = rest[-2 - (share > 0)], rest[-1 - (share > 0)]
    for flip in range(GROUP):
        at = jnp.bitwise_xor(spot, flip)
        for ref, block in ((near[flip], row), (far[flip], 1 - row)):
            high, low = split(ref[0:depth, :])
            high_ref[at, block] = high
            low_ref[at, block] = low
    if share:
        rest[-1][spot] = rest[0][...]
        for flip in range(1, GROUP):
            rest[-1][jnp.bitwise_xor(spot, flip)] = near[flip][depth : depth + share, :]


def choose_kernel(first_ref, second_ref, out_ref):
    _, _, row = place()

    @pl.when(row == 0)
    def _():
        out_ref[...] = first_ref[...]

    @pl.when(row != 0)
    def _():
        out_ref[...] = second_ref[...]


def pack(spot, step, refs, state):
    for flip, ref in enumerate(refs):

        @pl.when(spot == (step ^ flip))
        def _():
            ref[...] = state


def filter_kernel(turn, start_ref, coef_ref, high_ref, low_ref, obs_ref, *rest):
    out_ref, sent, last_ref = rest[-GROUP - 2], rest[-GROUP - 1 : -1], rest[-1]
    group, spot, _ = place()
    half = high_ref.shape[3] // 2

    @pl.when(group == turn)
    def _():
        state = start_ref[...]
        for step in range(GROUP):
            moved, values = transition(state, coef_ref, half)
            innovation = obs_ref[step] - values
            update = [
                multiply(innovation, high_ref[step, block], low_ref[step, block])
                for block in range(high_ref.shape[1])
            ]
            state = moved + jnp.concatenate(update, 1)
            out_ref[step] = state
            pack(spot, step, sent, state)
        last_ref[...] = state


def smooth_kernel(turn, groups, start_ref, coef_ref, high_ref, low_ref, filt_ref, *rest):
    sent, first_ref = rest[-GROUP - 1 : -1], rest[-1]
    group, spot, _ = place()
    half = high_ref.shape[3] // 2

    @pl.when(group == groups - 1 - turn)
    def _():
        state = start_ref[...]
        for step in range(GROUP - 1, -1, -1):
            filt = filt_ref[step]
            if turn == 0 and step == GROUP - 1:
                state = filt
            else:
                change = state - transition(filt, coef_ref, half)[0]
                update = [
                    multiply(change, high_ref[step, block], low_ref[step, block])
                    for block in range(high_ref.shape[1])
                ]
                state = filt + jnp.concatenate(update, 1)
            pack(spot, step, sent, state)
        first_ref[...] = state


def home_kernel(share, *refs):
    near, far, (out_ref, turned, tiles) = refs[:GROUP], refs[GROUP : 2 * GROUP], refs[2 * GROUP :]
    _, spot, row = place()
    rows = lax.axis_size("rows")
    half = out_ref.shape[0] // 2
    lanes = pl.ds(pl.multiple_of(row * 2 * half, LANES), 2 * half)
    for flip in range(GROUP):
        start = jnp.bitwise_xor(spot, flip) * rows
        turned[pl.ds(pl.multiple_of((start + row) * share, 8), share), :] = near[flip][:, lanes]
        turned[pl.ds(pl.multiple_of((start + 1 - row) * share, 8), share), :] = far[flip][:, lanes]
    for at in range(out_ref.shape[1] // LANES):
        lines = slice(at * LANES, (at + 1) * LANES)
        for part in range(2):
            tiles[at, pl.ds(part, half, stride=2), :] = turned[lines, part * half : (part + 1) * half].T
        out_ref[:, lines] = tiles[at]


def gate(values, token, flops):
    return call(
        lambda *refs: None,
        (*values, token),
        [(value.shape, value.dtype) for value in values],
        aliases={at: at for at in range(len(values))},
        flops=flops,
    )


def body(site_rates, prior_mean, observed, obs_mask, filter_gains, smooth_gains):
    count, rows = lax.axis_size("tm"), lax.axis_size("rows")
    groups = count // GROUP
    panel, sites = filter_gains.shape[1:]
    states, paths = prior_mean.shape
    half = panel // 2
    share = paths // (GROUP * rows)
    both = ("tm", "rows")

    def swap(value, target):
        pairs = [(t * rows + r, target(t, r)) for t in range(count) for r in range(rows)]
        return lax.ppermute(value, both, pairs)

    def across(value, flip, core=0):
        return swap(value, lambda t, r: (t ^ flip) * rows + (r ^ core))

    def forward(value):
        return swap(value, lambda t, r: (t ^ (2 - r)) * rows + r)

    def neighbour(value):
        return across(value, 0, 1)

    def hop(value, source, target):
        pairs = [
            ((source * GROUP + m) * rows + r, (target * GROUP + m) * rows + r)
            for m in range(GROUP)
            for r in range(rows)
        ]
        return lax.ppermute(value, both, pairs)

    def send_home(sent):
        return [sent[0]] + [across(sent[flip], flip) for flip in range(1, GROUP)]

    def settle(near):
        (out,) = call(
            functools.partial(home_kernel, share),
            (*near, *[neighbour(value) for value in near]),
            [((panel, paths), F32)],
            [pltpu.VMEM((paths, panel), F32), pltpu.VMEM((paths // LANES, panel, LANES), F32)],
        )
        return out[None]

    *messages, own_obs, coef = call(
        functools.partial(gain_kernel, share),
        tuple(pltpu.with_memory_space_constraint(x, pltpu.HBM) for x in (site_rates.reshape(1, sites), obs_mask, filter_gains[0], observed[0])),
        [((sites + share, panel), F32)] * (GROUP - 1) + [((share, sites), F32), ((8, sites), F32)],
        [
            pltpu.VMEM((1, sites), F32),
            pltpu.VMEM((1, sites), jnp.int32),
            pltpu.VMEM((panel, sites), F32),
            pltpu.VMEM((sites, paths), F32),
            pltpu.VMEM((paths, sites), F32),
            pltpu.VMEM((sites // LANES, panel, LANES), F32),
            pltpu.SemaphoreType.DMA((4,)),
        ],
        source=pltpu.HBM,
    )
    near = [across(value, flip) for flip, value in enumerate(messages, 1)]
    (prior,) = call(
        functools.partial(prior_kernel, share, half),
        (prior_mean,),
        [((share, states), F32)],
        [pltpu.VMEM((paths, states), F32), pltpu.VMEM((paths // LANES, states, LANES), F32)],
    )
    pieces = call(
        smoother_gain_kernel,
        (smooth_gains[0],),
        [((states // PIECES, panel), F32)] * PIECES,
        [pltpu.VMEM((2, states, half), F32), pltpu.VMEM((states // LANES, panel, LANES), F32)],
    )
    (turned_gain,) = pieces
    gain_x, gain_y = across(turned_gain, 1), across(turned_gain, 2)
    own_far, prior = lax.optimization_barrier((neighbour(messages[0]), prior))
    *near, own_far, prior, turned_gain = lax.optimization_barrier((*near, own_far, prior, turned_gain))
    far = [own_far] + [neighbour(value) for value in near]
    near = [messages[0], *near]
    high, low, obs = call(
        functools.partial(gather_kernel, share, sites),
        (*near, *far, own_obs),
        [((GROUP, rows, sites, panel), BF16)] * 2 + [((GROUP, share, sites), F32)],
    )
    start, filtered = prior, ()
    for turn in range(groups):
        *filtered, last = call(
            functools.partial(filter_kernel, turn),
            (start, coef, high, low, obs, *filtered),
            [((GROUP, share, states), F32)] + [((share, states), F32)] * (GROUP + 1),
            aliases={5 + i: i for i in range(len(filtered))},
            flops=FW[min(turn,3)],
        )
        if turn < groups - 1:
            start = hop(last, turn, turn + 1)
        if turn == groups - 3:
            turned_gain, gain_x, gain_y = gate((turned_gain, gain_x, gain_y), last, G1)
            (gain_d,) = call(choose_kernel, (gain_x, gain_y), [((states, panel), F32)], flops=G1)
            gain_d = forward(gain_d)
            gain_near = list(gate((turned_gain, gain_x, gain_y), start, G2))
            gain_far = [neighbour(value) for value in gain_near]
        if turn == groups - 2:
            (gain_d,) = gate((gain_d,), gain_far[2], G3)
            gain_near.append(gain_d)
            gain_far.append(neighbour(gain_d))
    filtered, sent = filtered[0], filtered[1:]

    high, low = call(
        functools.partial(gather_kernel, 0, states),
        (*gain_near, *gain_far),
        [((GROUP, rows, states, panel), BF16)] * 2,
    )
    start, packed = last, ()
    for turn in range(groups):
        *packed, first = call(
            functools.partial(smooth_kernel, turn, groups),
            (start, coef, high, low, filtered, *packed),
            [((share, states), F32)] * (GROUP + 1),
            aliases={5 + i: i for i in range(len(packed))},
            flops=BW[min(turn,3)],
        )
        if turn < groups - 1:
            start = hop(first, groups - 1 - turn, groups - 2 - turn)
        if turn == groups - 2:
            filt_near = send_home(gate(sent, first, G4))
    smooth_near = send_home(packed)
    filt = settle(gate(filt_near, smooth_near[1], G5))
    smooth = settle(smooth_near)
    return filt, smooth


def solution(mesh):
    placed = (
        P(),
        P(),
        P("tm", None, None),
        P("tm", None),
        P("tm", "rows", None),
        P("tm", "rows", None),
    )
    return jax.shard_map(
        body,
        mesh=mesh,
        in_specs=placed,
        out_specs=(P("tm", "rows", None), P("tm", "rows", None)),
        check_vma=False,
    )
```

time: 100 us -> 78.6 us (0.79)
  waiting for transfers between devices: 62 us -> 41.8 us
  local copies, waits for them, and re-layouts: 4.41 us -> 1.05 us
  Pallas kernels: 5.81 us -> 7.93 us
    ppermute x6, waiting for transfers between devices: 30.2 us -> 16.4 us  [hop(): return lax.ppermute(value, both, pairs)]
    ppermute x21 -> x28, waiting for transfers between devices: 31.8 us -> 25.4 us  [swap(): return lax.ppermute(value, both, pairs)]
    unnamed x12 -> x4, local copies, waits for them, and re-layouts: 4.41 us -> 1.05 us
    pallas_call x14 -> x21, Pallas kernels: 5.81 us -> 7.93 us  [call(): pl.pallas_call(kernel, out_shape=[jax.ShapeDtypeStruct(shape, dtype) for...]
    ppermute x21 -> x28, starting transfers between devices: 19.7 us -> 19.7 us  [swap(): return lax.ppermute(value, both, pairs)]
  transfers between devices with their start and end apart: 27 -> 34, of which waited for: 10 -> 14; matrix products, arithmetic and copies ran while one was open for 0% -> 0% of each run, Pallas kernels for 2% -> 6%
where the time goes in v2:
time: 78.6 us; the launch traced here: 78.4 us
  waiting for transfers between devices  41.8 us (53%)
  starting transfers between devices  26.7 us (34%)
  Pallas kernels  7.93 us (10%)
  local copies, waits for them, and re-layouts  1.05 us (1%)
  between operations  0.87 us (1%)
    ppermute x28, waiting for transfers between devices, swap(): return lax.ppermute(value, both, pairs)  25.4 us
    ppermute x28, starting transfers between devices, swap(): return lax.ppermute(value, both, pairs)  19.7 us
    ppermute x6, waiting for transfers between devices, hop(): return lax.ppermute(value, both, pairs)  16.4 us
    pallas_call x21, Pallas kernels, call(): pl.pallas_call(kernel, out_shape=[jax.ShapeDtypeStruct(shape, dtype) for...  7.93 us
    ppermute x6, starting transfers between devices, hop(): return lax.ppermute(value, both, pairs)  7.01 us
  transfers between devices with their start and end apart: 34, of which 14 were waited for; matrix products, arithmetic and copies ran while one was open for 0% of the time, Pallas kernels for 6%

profile of v2, /device:TPU:0, one launch (start us, length us, event | category | flops | bytes accessed | tf_op | source)
XLA Modules:
  0.0 78.4 jit_solution(3050585775694454839)
XLA Ops:
  0.6 1.4 %shard_map.77 = (f32[304,256]{1,0:T(8,128)S(1)}, f32[304,256]{1,0:T(8,128)S(1)}, f32[304,256]{1,0:T(8,128)S(1)}, f32[48,256]{1,0:T(8,128)S(1)}, f32[8,256]{1,0:T(8,128)S(1)}) custom-call(f32[1,256]{1,0:T(1,128)} %bitcast.11, s32[1,256]{1,0:T(1,128)} %mask_hbm.1, f32[256,256]{1,0:T(8,128)} %bitcast.10, f32[256,384]{1,0:T(8,128)} %bitcast.7), custom_call_target="tpu_custom_call" | custom-call | bytes 2097152 | tf_op jit(solution)/shard_map/pallas_call | solution.py:23
  2.6 2.6 %collective-permute-start.1 = (f32[304,256]{1,0:T(8,128)S(1)}, f32[304,256]{1,0:T(8,128)S(1)}, u32[]{:S(2)}, u32[]{:S(2)}) collective-permute-start(f32[304,256]{1,0:T(8,128)S(1)} %get-tuple-element.78), channel_id=1, source_target_pairs={{0,4},{1,5},{2,6},{3,7},{4,0},{5,1},{6,2},{7,3},{8,12},{9,13},{10,... | collective-permute-start | bytes 933896 | tf_op jit(solution)/shard_map/ppermute | solution.py:283
  5.2 1.4 %collective-permute-start.2 = (f32[304,256]{1,0:T(8,128)S(1)}, f32[304,256]{1,0:T(8,128)S(1)}, u32[]{:S(2)}, u32[]{:S(2)}) collective-permute-start(f32[304,256]{1,0:T(8,128)S(1)} %get-tuple-element.79), channel_id=1, source_target_pairs={{0,6},{1,7},{2,4},{3,5},{4,2},{5,3},{6,0},{7,1},{8,14},{9,15},{10,... | collective-permute-start | bytes 933896 | tf_op jit(solution)/shard_map/ppermute | solution.py:283
  6.7 1.0 %copy-done.1 = f32[1,256,512]{2,1,0:T(8,128)S(1)} copy-done((f32[1,256,512]{2,1,0:T(8,128)S(1)}, f32[1,256,512]{2,1,0:T(8,128)}, u32[]{:S(2)}) %copy-start.1) | copy-done | bytes 524312
  8.0 2.0 %collective-permute-start.11 = (f32[512,256]{1,0:T(8,128)S(1)}, f32[512,256]{1,0:T(8,128)S(1)}, u32[]{:S(2)}, u32[]{:S(2)}) collective-permute-start(f32[512,256]{1,0:T(8,128)S(1)} %shard_map.79.refs_0_), channel_id=1, source_target_pairs={{0,4},{1,5},{2,6},{3,7},{4,0},{5,1},{6,2},{7,3},{8,12},{9,13},{10,... | collective-permute-start | bytes 1572872 | tf_op jit(solution)/shard_map/ppermute | solution.py:283
  10.1 1.5 %collective-permute-start.10 = (f32[512,256]{1,0:T(8,128)S(1)}, f32[512,256]{1,0:T(8,128)S(1)}, u32[]{:S(2)}, u32[]{:S(2)}) collective-permute-start(f32[512,256]{1,0:T(8,128)S(1)} %shard_map.79.refs_0_), channel_id=1, source_target_pairs={{0,2},{1,3},{2,0},{3,1},{4,6},{5,7},{6,4},{7,5},{8,10},{9,11},{10,... | collective-permute-start | bytes 1572872 | tf_op jit(solution)/shard_map/ppermute | solution.py:283
  11.8 8.2 %collective-permute-done.1.refs_2_ = f32[304,256]{1,0:T(8,128)S(1)} collective-permute-done((f32[304,256]{1,0:T(8,128)S(1)}, f32[304,256]{1,0:T(8,128)S(1)}, u32[]{:S(2)}, u32[]{:S(2)}) %collective-permute-start.1) | collective-permute-done | bytes 311328 | tf_op jit(solution)/shard_map/ppermute | solution.py:283
  20.1 1.5 %collective-permute-done.refs_1_ = f32[304,256]{1,0:T(8,128)S(1)} collective-permute-done((f32[304,256]{1,0:T(8,128)S(1)}, f32[304,256]{1,0:T(8,128)S(1)}, u32[]{:S(2)}, u32[]{:S(2)}) %collective-permute-start) | collective-permute-done | bytes 311328 | tf_op jit(solution)/shard_map/ppermute | solution.py:283
  22.1 1.1 %collective-permute-done.4.refs_5_ = f32[304,256]{1,0:T(8,128)S(1)} collective-permute-done((f32[304,256]{1,0:T(8,128)S(1)}, f32[304,256]{1,0:T(8,128)S(1)}, u32[]{:S(2)}, u32[]{:S(2)}) %collective-permute-start.4) | collective-permute-done | bytes 311328 | tf_op jit(solution)/shard_map/ppermute | solution.py:283
  24.4 0.9 %shard_map.81 = (f32[4,48,512]{2,1,0:T(8,128)S(1)}, f32[48,512]{1,0:T(8,128)S(1)}, f32[48,512]{1,0:T(8,128)S(1)}, f32[48,512]{1,0:T(8,128)S(1)}, f32[48,512]{1,0:T(8,128)S(1)}, /*index=5*/f32[48,512]{1,0:T(8,128)S(1)}) custom-call(f32[48,512]{1,0:T(8,128)S(1)} %shard_map.78.start_ref, f32[8,256]{1,0:T(8,128)S(1)} %get-tuple-element.83.coef_ref, ...), custom_call_target="tpu_custom_call" | custom-call | bytes 2097152 | tf_op jit(solution)/shard_map/pallas_call | solution.py:23
  25.3 3.1 %collective-permute-start.7 = (f32[48,512]{1,0:T(8,128)S(1)}, f32[48,512]{1,0:T(8,128)S(1)}, u32[]{:S(2)}, u32[]{:S(2)}) collective-permute-start(f32[48,512]{1,0:T(8,128)S(1)} %get-tuple-element.92), channel_id=1, source_target_pairs={{0,8},{1,9},{2,10},{3,11},{4,12},{5,13},{6,14},{7,15}} | collective-permute-start | bytes 294920 | tf_op jit(solution)/shard_map/ppermute | solution.py:300
  28.4 2.3 %collective-permute-done.7.start_ref = f32[48,512]{1,0:T(8,128)S(1)} collective-permute-done((f32[48,512]{1,0:T(8,128)S(1)}, f32[48,512]{1,0:T(8,128)S(1)}, u32[]{:S(2)}, u32[]{:S(2)}) %collective-permute-start.7) | collective-permute-done | bytes 98336 | tf_op jit(solution)/shard_map/ppermute | solution.py:300
  31.4 0.9 %collective-permute-done.10.refs_1_ = f32[512,256]{1,0:T(8,128)S(1)} collective-permute-done((f32[512,256]{1,0:T(8,128)S(1)}, f32[512,256]{1,0:T(8,128)S(1)}, u32[]{:S(2)}, u32[]{:S(2)}) %collective-permute-start.10) | collective-permute-done | bytes 524320 | tf_op jit(solution)/shard_map/ppermute | solution.py:283
  32.4 1.8 %collective-permute-start.12 = (f32[512,256]{1,0:T(8,128)S(1)}, f32[512,256]{1,0:T(8,128)S(1)}, u32[]{:S(2)}, u32[]{:S(2)}) collective-permute-start(f32[512,256]{1,0:T(8,128)S(1)} %shard_map.87), channel_id=1, source_target_pairs={{0,4},{1,3},{2,6},{3,1},{4,0},{5,7},{6,2},{7,5},{8,12},{9,11},{10,... | collective-permute-start | bytes 1572872 | tf_op jit(solution)/shard_map/ppermute | solution.py:283
  34.1 0.7 collective-permute-start.9
  35.5 6.1 %collective-permute-done.12.refs_0_ = f32[512,256]{1,0:T(8,128)S(1)} collective-permute-done((f32[512,256]{1,0:T(8,128)S(1)}, f32[512,256]{1,0:T(8,128)S(1)}, u32[]{:S(2)}, u32[]{:S(2)}) %collective-permute-start.12) | collective-permute-done | bytes 524320 | tf_op jit(solution)/shard_map/ppermute | solution.py:283
  41.7 1.9 %collective-permute-done.16.refs_7_ = f32[512,256]{1,0:T(8,128)S(1)} collective-permute-done((f32[512,256]{1,0:T(8,128)S(1)}, f32[512,256]{1,0:T(8,128)S(1)}, u32[]{:S(2)}, u32[]{:S(2)}) %collective-permute-start.16) | collective-permute-done | bytes 524320 | tf_op jit(solution)/shard_map/ppermute | solution.py:283
  43.5 0.8 shard_map.89
  44.3 0.7 collective-permute-start.17
  45.0 0.7 collective-permute-start.18
  45.7 1.3 %collective-permute-start.22 = (f32[48,512]{1,0:T(8,128)S(1)}, f32[48,512]{1,0:T(8,128)S(1)}, u32[]{:S(2)}, u32[]{:S(2)}) collective-permute-start(f32[48,512]{1,0:T(8,128)S(1)} %get-tuple-element.135.refs_4_), channel_id=1, source_target_pairs={{8,0},{9,1},{10,2},{11,3},{12,4},{13,5},{14,6},{15,7}} | collective-permute-start | bytes 294920 | tf_op jit(solution)/shard_map/ppermute | solution.py:300
  47.1 1.8 %collective-permute-start.19 = (f32[48,512]{1,0:T(8,128)S(1)}, f32[48,512]{1,0:T(8,128)S(1)}, u32[]{:S(2)}, u32[]{:S(2)}) collective-permute-start(f32[48,512]{1,0:T(8,128)S(1)} %get-tuple-element.137), channel_id=1, source_target_pairs={{0,2},{1,3},{2,0},{3,1},{4,6},{5,7},{6,4},{7,5},{8,10},{9,11},{10,... | collective-permute-start | bytes 294920 | tf_op jit(solution)/shard_map/ppermute | solution.py:283
  48.8 1.5 %collective-permute-start.20 = (f32[48,512]{1,0:T(8,128)S(1)}, f32[48,512]{1,0:T(8,128)S(1)}, u32[]{:S(2)}, u32[]{:S(2)}) collective-permute-start(f32[48,512]{1,0:T(8,128)S(1)} %get-tuple-element.138), channel_id=1, source_target_pairs={{0,4},{1,5},{2,6},{3,7},{4,0},{5,1},{6,2},{7,3},{8,12},{9,13},{10,... | collective-permute-start | bytes 294920 | tf_op jit(solution)/shard_map/ppermute | solution.py:283
  50.6 14.1 %collective-permute-done.22.start_ref = f32[48,512]{1,0:T(8,128)S(1)} collective-permute-done((f32[48,512]{1,0:T(8,128)S(1)}, f32[48,512]{1,0:T(8,128)S(1)}, u32[]{:S(2)}, u32[]{:S(2)}) %collective-permute-start.22) | collective-permute-done | bytes 98336 | tf_op jit(solution)/shard_map/ppermute | solution.py:300
  64.7 1.8 %shard_map.94 = (f32[48,512]{1,0:T(8,128)S(1)}, f32[48,512]{1,0:T(8,128)S(1)}, f32[48,512]{1,0:T(8,128)S(1)}, f32[48,512]{1,0:T(8,128)S(1)}, f32[48,512]{1,0:T(8,128)}) custom-call(f32[48,512]{1,0:T(8,128)S(1)} %collective-permute-done.22.start_ref, ...), custom_call_target="tpu_custom_call", output_to_operand_aliasing={{0}: (5, {}), {1}: (6, {}), {2}: (7, {}), {3}: (8, {})} | custom-call | flops 10000000000 | bytes 2097152 | tf_op jit(solution)/shard_map/pallas_call | solution.py:23
  66.5 1.5 %collective-permute-start.23 = (f32[48,512]{1,0:T(8,128)S(1)}, f32[48,512]{1,0:T(8,128)S(1)}, u32[]{:S(2)}, u32[]{:S(2)}) collective-permute-start(f32[48,512]{1,0:T(8,128)S(1)} %get-tuple-element.144), channel_id=1, source_target_pairs={{0,2},{1,3},{2,0},{3,1},{4,6},{5,7},{6,4},{7,5},{8,10},{9,11},{10,... | collective-permute-start | bytes 294920 | tf_op jit(solution)/shard_map/ppermute | solution.py:283
  68.0 1.5 %collective-permute-start.28 = (f32[48,512]{1,0:T(8,128)S(1)}, f32[48,512]{1,0:T(8,128)S(1)}, u32[]{:S(2)}, u32[]{:S(2)}) collective-permute-start(f32[48,512]{1,0:T(8,128)S(1)} %get-tuple-element.150), channel_id=1, source_target_pairs={{0,4},{1,5},{2,6},{3,7},{4,0},{5,1},{6,2},{7,3},{8,12},{9,13},{10,... | collective-permute-start | bytes 294920 | tf_op jit(solution)/shard_map/ppermute | solution.py:283
  70.0 1.3 %collective-permute-done.23.refs_4_.refs_1_ = f32[48,512]{1,0:T(8,128)S(1)} collective-permute-done((f32[48,512]{1,0:T(8,128)S(1)}, f32[48,512]{1,0:T(8,128)S(1)}, u32[]{:S(2)}, u32[]{:S(2)}) %collective-permute-start.23) | collective-permute-done | bytes 98336 | tf_op jit(solution)/shard_map/ppermute | solution.py:283
  71.8 0.8 collective-permute-done.28.refs_2_
  72.6 2.4 %collective-permute-done.29.refs_3_ = f32[48,512]{1,0:T(8,128)S(1)} collective-permute-done((f32[48,512]{1,0:T(8,128)S(1)}, f32[48,512]{1,0:T(8,128)S(1)}, u32[]{:S(2)}, u32[]{:S(2)}) %collective-permute-start.29) | collective-permute-done | bytes 98336 | tf_op jit(solution)/shard_map/ppermute | solution.py:283
  76.3 1.0 %shard_map.96 = f32[256,384]{1,0:T(8,128)} custom-call(f32[48,512]{1,0:T(8,128)S(1)} %get-tuple-element.145.refs_0_, f32[48,512]{1,0:T(8,128)S(1)} %get-tuple-element.146.refs_1_, f32[48,512]{1,0:T(8,128)S(1)} %get-tuple-element.147.refs_2_, f32[48,512]{1,0:T(8,128)S(1)} %get-tuple-element.148.refs_3_, f32[48,512]{1,0:T(8,128)S(1)} %collective-permute-done.24.refs_4_, ...), custom_call_target="tpu_custom_call" | custom-call | bytes 2097152 | tf_op jit(solution)/shard_map/pallas_call | solution.py:23
  77.4 1.0 %shard_map.97 = f32[256,384]{1,0:T(8,128)} custom-call(f32[48,512]{1,0:T(8,128)S(1)} %get-tuple-element.149.refs_0_, f32[48,512]{1,0:T(8,128)S(1)} %collective-permute-done.23.refs_4_.refs_1_, f32[48,512]{1,0:T(8,128)S(1)} %collective-permute-done.28.refs_2_, f32[48,512]{1,0:T(8,128)S(1)} %collective-permute-done.29.refs_3_, ...), custom_call_target="tpu_custom_call" | custom-call | bytes 2097152 | tf_op jit(solution)/shard_map/pallas_call | solution.py:23
  (61 shorter events, 7.0 us)
Async XLA Ops:
  2.1 8.0 %collective-permute-start.3 = (f32[304,256]{1,0:T(8,128)S(1)}, f32[304,256]{1,0:T(8,128)S(1)}, u32[]{:S(2)}, u32[]{:S(2)}) collective-permute-start(f32[304,256]{1,0:T(8,128)S(1)} %get-tuple-element.77.refs_0_), channel_id=1, source_target_pairs={{0,1},{1,0},{2,3},{3,2},{4,5},{5,4},{6,7},{7,6},{8,9},{9,8},{10,11... | collective-permute-start | bytes 933896 | tf_op jit(solution)/shard_map/ppermute | solution.py:283
  2.6 17.5 %collective-permute-start.1 = (f32[304,256]{1,0:T(8,128)S(1)}, f32[304,256]{1,0:T(8,128)S(1)}, u32[]{:S(2)}, u32[]{:S(2)}) collective-permute-start(f32[304,256]{1,0:T(8,128)S(1)} %get-tuple-element.78), channel_id=1, source_target_pairs={{0,4},{1,5},{2,6},{3,7},{4,0},{5,1},{6,2},{7,3},{8,12},{9,13},{10,... | collective-permute-start | bytes 933896 | tf_op jit(solution)/shard_map/ppermute | solution.py:283
  5.2 14.9 %collective-permute-start.2 = (f32[304,256]{1,0:T(8,128)S(1)}, f32[304,256]{1,0:T(8,128)S(1)}, u32[]{:S(2)}, u32[]{:S(2)}) collective-permute-start(f32[304,256]{1,0:T(8,128)S(1)} %get-tuple-element.79), channel_id=1, source_target_pairs={{0,6},{1,7},{2,4},{3,5},{4,2},{5,3},{6,0},{7,1},{8,14},{9,15},{10,... | collective-permute-start | bytes 933896 | tf_op jit(solution)/shard_map/ppermute | solution.py:283
  6.6 15.0 %collective-permute-start = (f32[304,256]{1,0:T(8,128)S(1)}, f32[304,256]{1,0:T(8,128)S(1)}, u32[]{:S(2)}, u32[]{:S(2)}) collective-permute-start(f32[304,256]{1,0:T(8,128)S(1)} %get-tuple-element.77.refs_0_), channel_id=1, source_target_pairs={{0,2},{1,3},{2,0},{3,1},{4,6},{5,7},{6,4},{7,5},{8,10},{9,11},{10,... | collective-permute-start | bytes 933896 | tf_op jit(solution)/shard_map/ppermute | solution.py:283
  8.0 23.4 %collective-permute-start.11 = (f32[512,256]{1,0:T(8,128)S(1)}, f32[512,256]{1,0:T(8,128)S(1)}, u32[]{:S(2)}, u32[]{:S(2)}) collective-permute-start(f32[512,256]{1,0:T(8,128)S(1)} %shard_map.79.refs_0_), channel_id=1, source_target_pairs={{0,4},{1,5},{2,6},{3,7},{4,0},{5,1},{6,2},{7,3},{8,12},{9,13},{10,... | collective-permute-start | bytes 1572872 | tf_op jit(solution)/shard_map/ppermute | solution.py:283
  10.1 22.3 %collective-permute-start.10 = (f32[512,256]{1,0:T(8,128)S(1)}, f32[512,256]{1,0:T(8,128)S(1)}, u32[]{:S(2)}, u32[]{:S(2)}) collective-permute-start(f32[512,256]{1,0:T(8,128)S(1)} %shard_map.79.refs_0_), channel_id=1, source_target_pairs={{0,2},{1,3},{2,0},{3,1},{4,6},{5,7},{6,4},{7,5},{8,10},{9,11},{10,... | collective-permute-start | bytes 1572872 | tf_op jit(solution)/shard_map/ppermute | solution.py:283
  21.6 1.6 %collective-permute-start.4 = (f32[304,256]{1,0:T(8,128)S(1)}, f32[304,256]{1,0:T(8,128)S(1)}, u32[]{:S(2)}, u32[]{:S(2)}) collective-permute-start(f32[304,256]{1,0:T(8,128)S(1)} %collective-permute-done.refs_1_), channel_id=1, source_target_pairs={{0,1},{1,0},{2,3},{3,2},{4,5},{5,4},{6,7},{7,6},{8,9},{9,8},{10,11... | collective-permute-start | bytes 933896 | tf_op jit(solution)/shard_map/ppermute | solution.py:283
  21.6 2.0 %collective-permute-start.5 = (f32[304,256]{1,0:T(8,128)S(1)}, f32[304,256]{1,0:T(8,128)S(1)}, u32[]{:S(2)}, u32[]{:S(2)}) collective-permute-start(f32[304,256]{1,0:T(8,128)S(1)} %collective-permute-done.1.refs_2_), channel_id=1, source_target_pairs={{0,1},{1,0},{2,3},{3,2},{4,5},{5,4},{6,7},{7,6},{8,9},{9,8},{10,11... | collective-permute-start | bytes 933896 | tf_op jit(solution)/shard_map/ppermute | solution.py:283
  22.1 2.0 %collective-permute-start.6 = (f32[304,256]{1,0:T(8,128)S(1)}, f32[304,256]{1,0:T(8,128)S(1)}, u32[]{:S(2)}, u32[]{:S(2)}) collective-permute-start(f32[304,256]{1,0:T(8,128)S(1)} %collective-permute-done.2.refs_3_), channel_id=1, source_target_pairs={{0,1},{1,0},{2,3},{3,2},{4,5},{5,4},{6,7},{7,6},{8,9},{9,8},{10,11... | collective-permute-start | bytes 933896 | tf_op jit(solution)/shard_map/ppermute | solution.py:283
  25.3 5.4 %collective-permute-start.7 = (f32[48,512]{1,0:T(8,128)S(1)}, f32[48,512]{1,0:T(8,128)S(1)}, u32[]{:S(2)}, u32[]{:S(2)}) collective-permute-start(f32[48,512]{1,0:T(8,128)S(1)} %get-tuple-element.92), channel_id=1, source_target_pairs={{0,8},{1,9},{2,10},{3,11},{4,12},{5,13},{6,14},{7,15}} | collective-permute-start | bytes 294920 | tf_op jit(solution)/shard_map/ppermute | solution.py:300
  30.7 3.4 %collective-permute-start.8 = (f32[48,512]{1,0:T(8,128)S(1)}, f32[48,512]{1,0:T(8,128)S(1)}, u32[]{:S(2)}, u32[]{:S(2)}) collective-permute-start(f32[48,512]{1,0:T(8,128)S(1)} %get-tuple-element.98.refs_3_), channel_id=1, source_target_pairs={{8,16},{9,17},{10,18},{11,19},{12,20},{13,21},{14,22},{15,23}} | collective-permute-start | bytes 294920 | tf_op jit(solution)/shard_map/ppermute | solution.py:300
  32.4 9.2 %collective-permute-start.12 = (f32[512,256]{1,0:T(8,128)S(1)}, f32[512,256]{1,0:T(8,128)S(1)}, u32[]{:S(2)}, u32[]{:S(2)}) collective-permute-start(f32[512,256]{1,0:T(8,128)S(1)} %shard_map.87), channel_id=1, source_target_pairs={{0,4},{1,3},{2,6},{3,1},{4,0},{5,7},{6,2},{7,5},{8,12},{9,11},{10,... | collective-permute-start | bytes 1572872 | tf_op jit(solution)/shard_map/ppermute | solution.py:283
  34.1 7.5 %collective-permute-start.13 = (f32[512,256]{1,0:T(8,128)S(1)}, f32[512,256]{1,0:T(8,128)S(1)}, u32[]{:S(2)}, u32[]{:S(2)}) collective-permute-start(f32[512,256]{1,0:T(8,128)S(1)} %get-tuple-element.121.refs_2_), channel_id=1, source_target_pairs={{0,1},{1,0},{2,3},{3,2},{4,5},{5,4},{6,7},{7,6},{8,9},{9,8},{10,11... | collective-permute-start | bytes 1572872 | tf_op jit(solution)/shard_map/ppermute | solution.py:283
  34.1 7.5 %collective-permute-start.9 = (f32[48,512]{1,0:T(8,128)S(1)}, f32[48,512]{1,0:T(8,128)S(1)}, u32[]{:S(2)}, u32[]{:S(2)}) collective-permute-start(f32[48,512]{1,0:T(8,128)S(1)} %get-tuple-element.104), channel_id=1, source_target_pairs={{16,24},{17,25},{18,26},{19,27},{20,28},{21,29},{22,30},{23,31}} | collective-permute-start | bytes 294920 | tf_op jit(solution)/shard_map/ppermute | solution.py:300
  34.8 6.8 %collective-permute-start.14 = (f32[512,256]{1,0:T(8,128)S(1)}, f32[512,256]{1,0:T(8,128)S(1)}, u32[]{:S(2)}, u32[]{:S(2)}) collective-permute-start(f32[512,256]{1,0:T(8,128)S(1)} %get-tuple-element.119.refs_0_), channel_id=1, source_target_pairs={{0,1},{1,0},{2,3},{3,2},{4,5},{5,4},{6,7},{7,6},{8,9},{9,8},{10,11... | collective-permute-start | bytes 1572872 | tf_op jit(solution)/shard_map/ppermute | solution.py:283
  35.4 6.3 %collective-permute-start.15 = (f32[512,256]{1,0:T(8,128)S(1)}, f32[512,256]{1,0:T(8,128)S(1)}, u32[]{:S(2)}, u32[]{:S(2)}) collective-permute-start(f32[512,256]{1,0:T(8,128)S(1)} %get-tuple-element.120.refs_1_), channel_id=1, source_target_pairs={{0,1},{1,0},{2,3},{3,2},{4,5},{5,4},{6,7},{7,6},{8,9},{9,8},{10,11... | collective-permute-start | bytes 1572872 | tf_op jit(solution)/shard_map/ppermute | solution.py:283
  41.6 1.9 %collective-permute-start.16 = (f32[512,256]{1,0:T(8,128)S(1)}, f32[512,256]{1,0:T(8,128)S(1)}, u32[]{:S(2)}, u32[]{:S(2)}) collective-permute-start(f32[512,256]{1,0:T(8,128)S(1)} %shard_map.88.refs_3_), channel_id=1, source_target_pairs={{0,1},{1,0},{2,3},{3,2},{4,5},{5,4},{6,7},{7,6},{8,9},{9,8},{10,11... | collective-permute-start | bytes 1572872 | tf_op jit(solution)/shard_map/ppermute | solution.py:283
  45.7 18.9 %collective-permute-start.22 = (f32[48,512]{1,0:T(8,128)S(1)}, f32[48,512]{1,0:T(8,128)S(1)}, u32[]{:S(2)}, u32[]{:S(2)}) collective-permute-start(f32[48,512]{1,0:T(8,128)S(1)} %get-tuple-element.135.refs_4_), channel_id=1, source_target_pairs={{8,0},{9,1},{10,2},{11,3},{12,4},{13,5},{14,6},{15,7}} | collective-permute-start | bytes 294920 | tf_op jit(solution)/shard_map/ppermute | solution.py:300
  47.1 22.5 %collective-permute-start.19 = (f32[48,512]{1,0:T(8,128)S(1)}, f32[48,512]{1,0:T(8,128)S(1)}, u32[]{:S(2)}, u32[]{:S(2)}) collective-permute-start(f32[48,512]{1,0:T(8,128)S(1)} %get-tuple-element.137), channel_id=1, source_target_pairs={{0,2},{1,3},{2,0},{3,1},{4,6},{5,7},{6,4},{7,5},{8,10},{9,11},{10,... | collective-permute-start | bytes 294920 | tf_op jit(solution)/shard_map/ppermute | solution.py:283
  48.8 21.2 %collective-permute-start.20 = (f32[48,512]{1,0:T(8,128)S(1)}, f32[48,512]{1,0:T(8,128)S(1)}, u32[]{:S(2)}, u32[]{:S(2)}) collective-permute-start(f32[48,512]{1,0:T(8,128)S(1)} %get-tuple-element.138), channel_id=1, source_target_pairs={{0,4},{1,5},{2,6},{3,7},{4,0},{5,1},{6,2},{7,3},{8,12},{9,13},{10,... | collective-permute-start | bytes 294920 | tf_op jit(solution)/shard_map/ppermute | solution.py:283
  50.3 19.7 %collective-permute-start.21 = (f32[48,512]{1,0:T(8,128)S(1)}, f32[48,512]{1,0:T(8,128)S(1)}, u32[]{:S(2)}, u32[]{:S(2)}) collective-permute-start(f32[48,512]{1,0:T(8,128)S(1)} %get-tuple-element.139), channel_id=1, source_target_pairs={{0,6},{1,7},{2,4},{3,5},{4,2},{5,3},{6,0},{7,1},{8,14},{9,15},{10,... | collective-permute-start | bytes 294920 | tf_op jit(solution)/shard_map/ppermute | solution.py:283
  66.5 4.8 %collective-permute-start.23 = (f32[48,512]{1,0:T(8,128)S(1)}, f32[48,512]{1,0:T(8,128)S(1)}, u32[]{:S(2)}, u32[]{:S(2)}) collective-permute-start(f32[48,512]{1,0:T(8,128)S(1)} %get-tuple-element.144), channel_id=1, source_target_pairs={{0,2},{1,3},{2,0},{3,1},{4,6},{5,7},{6,4},{7,5},{8,10},{9,11},{10,... | collective-permute-start | bytes 294920 | tf_op jit(solution)/shard_map/ppermute | solution.py:283
  68.0 4.6 %collective-permute-start.28 = (f32[48,512]{1,0:T(8,128)S(1)}, f32[48,512]{1,0:T(8,128)S(1)}, u32[]{:S(2)}, u32[]{:S(2)}) collective-permute-start(f32[48,512]{1,0:T(8,128)S(1)} %get-tuple-element.150), channel_id=1, source_target_pairs={{0,4},{1,5},{2,6},{3,7},{4,0},{5,1},{6,2},{7,3},{8,12},{9,13},{10,... | collective-permute-start | bytes 294920 | tf_op jit(solution)/shard_map/ppermute | solution.py:283
  69.5 5.5 %collective-permute-start.29 = (f32[48,512]{1,0:T(8,128)S(1)}, f32[48,512]{1,0:T(8,128)S(1)}, u32[]{:S(2)}, u32[]{:S(2)}) collective-permute-start(f32[48,512]{1,0:T(8,128)S(1)} %get-tuple-element.151), channel_id=1, source_target_pairs={{0,6},{1,7},{2,4},{3,5},{4,2},{5,3},{6,0},{7,1},{8,14},{9,15},{10,... | collective-permute-start | bytes 294920 | tf_op jit(solution)/shard_map/ppermute | solution.py:283
  71.3 3.7 %collective-permute-start.24 = (f32[48,512]{1,0:T(8,128)S(1)}, f32[48,512]{1,0:T(8,128)S(1)}, u32[]{:S(2)}, u32[]{:S(2)}) collective-permute-start(f32[48,512]{1,0:T(8,128)S(1)} %get-tuple-element.145.refs_0_), channel_id=1, source_target_pairs={{0,1},{1,0},{2,3},{3,2},{4,5},{5,4},{6,7},{7,6},{8,9},{9,8},{10,11... | collective-permute-start | bytes 294920 | tf_op jit(solution)/shard_map/ppermute | solution.py:283
  71.3 4.2 %collective-permute-start.25 = (f32[48,512]{1,0:T(8,128)S(1)}, f32[48,512]{1,0:T(8,128)S(1)}, u32[]{:S(2)}, u32[]{:S(2)}) collective-permute-start(f32[48,512]{1,0:T(8,128)S(1)} %get-tuple-element.146.refs_1_), channel_id=1, source_target_pairs={{0,1},{1,0},{2,3},{3,2},{4,5},{5,4},{6,7},{7,6},{8,9},{9,8},{10,11... | collective-permute-start | bytes 294920 | tf_op jit(solution)/shard_map/ppermute | solution.py:283
  71.8 3.8 %collective-permute-start.26 = (f32[48,512]{1,0:T(8,128)S(1)}, f32[48,512]{1,0:T(8,128)S(1)}, u32[]{:S(2)}, u32[]{:S(2)}) collective-permute-start(f32[48,512]{1,0:T(8,128)S(1)} %get-tuple-element.147.refs_2_), channel_id=1, source_target_pairs={{0,1},{1,0},{2,3},{3,2},{4,5},{5,4},{6,7},{7,6},{8,9},{9,8},{10,11... | collective-permute-start | bytes 294920 | tf_op jit(solution)/shard_map/ppermute | solution.py:283
  72.6 4.7 %collective-permute-start.30 = (f32[48,512]{1,0:T(8,128)S(1)}, f32[48,512]{1,0:T(8,128)S(1)}, u32[]{:S(2)}, u32[]{:S(2)}) collective-permute-start(f32[48,512]{1,0:T(8,128)S(1)} %get-tuple-element.149.refs_0_), channel_id=1, source_target_pairs={{0,1},{1,0},{2,3},{3,2},{4,5},{5,4},{6,7},{7,6},{8,9},{9,8},{10,11... | collective-permute-start | bytes 294920 | tf_op jit(solution)/shard_map/ppermute | solution.py:283
  75.0 1.3 %collective-permute-start.27 = (f32[48,512]{1,0:T(8,128)S(1)}, f32[48,512]{1,0:T(8,128)S(1)}, u32[]{:S(2)}, u32[]{:S(2)}) collective-permute-start(f32[48,512]{1,0:T(8,128)S(1)} %get-tuple-element.148.refs_3_), channel_id=1, source_target_pairs={{0,1},{1,0},{2,3},{3,2},{4,5},{5,4},{6,7},{7,6},{8,9},{9,8},{10,11... | collective-permute-start | bytes 294920 | tf_op jit(solution)/shard_map/ppermute | solution.py:283
  75.0 2.3 %collective-permute-start.31 = (f32[48,512]{1,0:T(8,128)S(1)}, f32[48,512]{1,0:T(8,128)S(1)}, u32[]{:S(2)}, u32[]{:S(2)}) collective-permute-start(f32[48,512]{1,0:T(8,128)S(1)} %collective-permute-done.23.refs_4_.refs_1_), channel_id=1, source_target_pairs={{0,1},{1,0},{2,3},{3,2},{4,5},{5,4},{6,7},{7,6},{8,9},{9,8},{10,11... | collective-permute-start | bytes 294920 | tf_op jit(solution)/shard_map/ppermute | solution.py:283
  75.6 1.8 %collective-permute-start.32 = (f32[48,512]{1,0:T(8,128)S(1)}, f32[48,512]{1,0:T(8,128)S(1)}, u32[]{:S(2)}, u32[]{:S(2)}) collective-permute-start(f32[48,512]{1,0:T(8,128)S(1)} %collective-permute-done.28.refs_2_), channel_id=1, source_target_pairs={{0,1},{1,0},{2,3},{3,2},{4,5},{5,4},{6,7},{7,6},{8,9},{9,8},{10,11... | collective-permute-start | bytes 294920 | tf_op jit(solution)/shard_map/ppermute | solution.py:283
  75.6 1.7 %collective-permute-start.33 = (f32[48,512]{1,0:T(8,128)S(1)}, f32[48,512]{1,0:T(8,128)S(1)}, u32[]{:S(2)}, u32[]{:S(2)}) collective-permute-start(f32[48,512]{1,0:T(8,128)S(1)} %collective-permute-done.29.refs_3_), channel_id=1, source_target_pairs={{0,1},{1,0},{2,3},{3,2},{4,5},{5,4},{6,7},{7,6},{8,9},{9,8},{10,11... | collective-permute-start | bytes 294920 | tf_op jit(solution)/shard_map/ppermute | solution.py:283
  (4 other events, 13.3 us)

commit v3 on v2

--- a/solution.py
+++ b/solution.py
@@ -11,9 +11,11 @@
 LANES = 128
 PIECES = 1
 FW = (0, 0, 10**11, 10**11)
-BW = (0, 0, 10**10, 10**10)
+BW = (0, 10**10)
+JF = 10**11
 G1 = G2 = G3 = 10**9
 G4 = 10**9
+G6 = 10**9
 G5 = 10**10
 BF16 = jnp.bfloat16
 F32 = jnp.float32
@@ -219,44 +221,87 @@
         last_ref[...] = state
 
 
+def smooth_steps(state, coef_ref, high_ref, low_ref, filt_ref, keep, last_group=False):
+    half = high_ref.shape[3] // 2
+    for step in range(GROUP - 1, -1, -1):
+        filt = filt_ref[step]
+        if last_group and step == GROUP - 1:
+            state = filt
+        else:
+            change = state - transition(filt, coef_ref, half)[0]
+            update = [
+                multiply(change, high_ref[step, block], low_ref[step, block]) for block in range(high_ref.shape[1])
+            ]
+            state = filt + jnp.concatenate(update, 1)
+        keep(step, state)
+    return state
+
+
 def smooth_kernel(turn, groups, start_ref, coef_ref, high_ref, low_ref, filt_ref, *rest):
-    sent, first_ref = rest[-GROUP - 1 : -1], rest[-1]
+    sent, first = (rest[-GROUP - 1 : -1], rest[-1:]) if turn == 0 else (rest[-GROUP:], ())
     group, spot, _ = place()
-    half = high_ref.shape[3] // 2
 
     @pl.when(group == groups - 1 - turn)
     def _():
-        state = start_ref[...]
-        for step in range(GROUP - 1, -1, -1):
-            filt = filt_ref[step]
-            if turn == 0 and step == GROUP - 1:
-                state = filt
-            else:
-                change = state - transition(filt, coef_ref, half)[0]
-                update = [
-                    multiply(change, high_ref[step, block], low_ref[step, block])
-                    for block in range(high_ref.shape[1])
-                ]
-                state = filt + jnp.concatenate(update, 1)
-            pack(spot, step, sent, state)
-        first_ref[...] = state
+        keep = lambda step, state: pack(spot, step, sent, state)
+        state = smooth_steps(start_ref[...], coef_ref, high_ref, low_ref, filt_ref, keep, turn == 0)
+        for ref in first:
+            ref[...] = state
+
+
+def joined_kernel(groups, coef_ref, high_ref, low_ref, filt_ref, map_high_ref, map_low_ref, offset_ref):
+    group, _, _ = place()
+
+    @pl.when(jnp.logical_and(group > 0, group < groups - 1))
+    def _():
+        blocks, lanes = high_ref.shape[1], high_ref.shape[3]
+        nothing = jnp.zeros(offset_ref.shape, F32)
+        offset_ref[...] = smooth_steps(nothing, coef_ref, high_ref, low_ref, filt_ref, lambda *_: None)
+        last = GROUP - 1
+        joined = [high_ref[last, block].astype(F32) + low_ref[last, block].astype(F32) for block in range(blocks)]
+        for step in range(GROUP - 2, -1, -1):
+            whole = jnp.concatenate(joined, 1)
+            joined = [multiply(whole, high_ref[step, block], low_ref[step, block]) for block in range(blocks)]
+        for block in range(blocks):
+            map_high_ref[block], map_low_ref[block] = split(joined[block])
+
+
+def jump_kernel(turn, groups, start_ref, map_high_ref, map_low_ref, offset_ref, first_ref):
+    group, _, _ = place()
+
+    @pl.when(group == groups - 1 - turn)
+    def _():
+        start = start_ref[...]
+        moved = [multiply(start, map_high_ref[block], map_low_ref[block]) for block in range(map_high_ref.shape[0])]
+        first_ref[...] = offset_ref[...] + jnp.concatenate(moved, 1)
+
+
+def across_kernel(*refs):
+    _, _, row = place()
+    lanes = refs[-1].shape[2]
+    for at, ref in enumerate(refs[:-1]):
+        refs[-1][at] = ref[:, pl.ds(pl.multiple_of((1 - row) * lanes, LANES), lanes)]
 
 
 def home_kernel(share, *refs):
-    near, far, (out_ref, turned, tiles) = refs[:GROUP], refs[GROUP : 2 * GROUP], refs[2 * GROUP :]
+    near, (far_ref, *outs, turned, tiles) = refs[: 2 * GROUP], refs[2 * GROUP :]
     _, spot, row = place()
     rows = lax.axis_size("rows")
-    half = out_ref.shape[0] // 2
-    lanes = pl.ds(pl.multiple_of(row * 2 * half, LANES), 2 * half)
-    for flip in range(GROUP):
-        start = jnp.bitwise_xor(spot, flip) * rows
-        turned[pl.ds(pl.multiple_of((start + row) * share, 8), share), :] = near[flip][:, lanes]
-        turned[pl.ds(pl.multiple_of((start + 1 - row) * share, 8), share), :] = far[flip][:, lanes]
-    for at in range(out_ref.shape[1] // LANES):
-        lines = slice(at * LANES, (at + 1) * LANES)
-        for part in range(2):
-            tiles[at, pl.ds(part, half, stride=2), :] = turned[lines, part * half : (part + 1) * half].T
-        out_ref[:, lines] = tiles[at]
+    panel, paths = outs[0].shape
+    half = panel // 2
+    lanes = pl.ds(pl.multiple_of(row * panel, LANES), panel)
+    for kind, out_ref in enumerate(outs):
+        for flip in range(GROUP):
+            at = kind * GROUP + flip
+            start = jnp.bitwise_xor(spot, flip) * rows
+            turned[kind, pl.ds(pl.multiple_of((start + row) * share, 8), share), :] = near[at][:, lanes]
+            turned[kind, pl.ds(pl.multiple_of((start + 1 - row) * share, 8), share), :] = far_ref[at]
+        for at in range(paths // LANES):
+            lines = slice(at * LANES, (at + 1) * LANES)
+            for part in range(2):
+                piece = turned[kind, lines, part * half : (part + 1) * half].T
+                tiles[kind, at, pl.ds(part, half, stride=2), :] = piece
+            out_ref[:, lines] = tiles[kind, at]
 
 
 def gate(values, token, flops):
@@ -282,14 +327,14 @@
         pairs = [(t * rows + r, target(t, r)) for t in range(count) for r in range(rows)]
         return lax.ppermute(value, both, pairs)
 
-    def across(value, flip, core=0):
-        return swap(value, lambda t, r: (t ^ flip) * rows + (r ^ core))
+    def across(value, flip):
+        return swap(value, lambda t, r: (t ^ flip) * rows + r)
 
     def forward(value):
         return swap(value, lambda t, r: (t ^ (2 - r)) * rows + r)
 
     def neighbour(value):
-        return across(value, 0, 1)
+        return swap(value, lambda t, r: t * rows + 1 - r)
 
     def hop(value, source, target):
         pairs = [
@@ -300,16 +345,7 @@
         return lax.ppermute(value, both, pairs)
 
     def send_home(sent):
-        return [sent[0]] + [across(sent[flip], flip) for flip in range(1, GROUP)]
-
-    def settle(near):
-        (out,) = call(
-            functools.partial(home_kernel, share),
-            (*near, *[neighbour(value) for value in near]),
-            [((panel, paths), F32)],
-            [pltpu.VMEM((paths, panel), F32), pltpu.VMEM((paths // LANES, panel, LANES), F32)],
-        )
-        return out[None]
+        return [across(sent[flip], flip) for flip in reversed(range(1, GROUP))][::-1]
 
     *messages, own_obs, coef = call(
         functools.partial(gain_kernel, share),
@@ -379,22 +415,43 @@
         [((GROUP, rows, states, panel), BF16)] * 2,
     )
     start, packed = last, ()
+    *joined, offset = call(
+        functools.partial(joined_kernel, groups),
+        (coef, high, low, filtered),
+        [((rows, states, panel), BF16)] * 2 + [((share, states), F32)],
+        flops=JF,
+    )
     for turn in range(groups):
-        *packed, first = call(
+        middle = 0 < turn < groups - 1
+        if middle:
+            (first,) = call(
+                functools.partial(jump_kernel, turn, groups), (start, *joined, offset), [((share, states), F32)]
+            )
+            here = hop(first, groups - 1 - turn, groups - 2 - turn)
+        packed = call(
             functools.partial(smooth_kernel, turn, groups),
             (start, coef, high, low, filtered, *packed),
-            [((share, states), F32)] * (GROUP + 1),
+            [((share, states), F32)] * (GROUP + (turn == 0)),
             aliases={5 + i: i for i in range(len(packed))},
-            flops=BW[min(turn,3)],
+            flops=BW[1] if middle else BW[0],
         )
+        if turn == 0:
+            *packed, first = packed
+            here = hop(first, groups - 1, groups - 2)
+        if turn == groups - 2:
+            sent = gate(sent, first, G4)
+            sent = [sent[0], *send_home(sent)]
         if turn < groups - 1:
-            start = hop(first, groups - 1 - turn, groups - 2 - turn)
-        if turn == groups - 2:
-            filt_near = send_home(gate(sent, first, G4))
-    smooth_near = send_home(packed)
-    filt = settle(gate(filt_near, smooth_near[1], G5))
-    smooth = settle(smooth_near)
-    return filt, smooth
+            start = here
+    near = (*sent, packed[0], *send_home(packed))
+    (far,) = call(across_kernel, near, [((2 * GROUP, share, panel), F32)])
+    filt, smooth = call(
+        functools.partial(home_kernel, share),
+        (*near, neighbour(far)),
+        [((panel, paths), F32)] * 2,
+        [pltpu.VMEM((2, paths, panel), F32), pltpu.VMEM((2, paths // LANES, panel, LANES), F32)],
+    )
+    return filt[None], smooth[None]
 
 
 def solution(mesh):

time: 78.6 us -> 75.9 us (0.966)
  Pallas kernels: 7.93 us -> 6.5 us
  starting transfers between devices: 26.7 us -> 25.3 us
    ppermute x28 -> x21, waiting for transfers between devices: 25.4 us -> 27.4 us  [swap(): return lax.ppermute(value, both, pairs)]
    ppermute x6, waiting for transfers between devices: 16.4 us -> 14.5 us  [hop(): return lax.ppermute(value, both, pairs)]
    pallas_call x21 -> x23, Pallas kernels: 7.93 us -> 6.5 us  [call(): pl.pallas_call(kernel, out_shape=[jax.ShapeDtypeStruct(shape, dtype) for...]
    ppermute x28 -> x21, starting transfers between devices: 19.7 us -> 18.3 us  [swap(): return lax.ppermute(value, both, pairs)]
  transfers between devices with their start and end apart: 34 -> 27, of which waited for: 14 -> 14; matrix products, arithmetic and copies ran while one was open for 0% -> 0% of each run, Pallas kernels for 6% -> 4%
where the time goes in v3:
time: 75.9 us; the launch traced here: 75.6 us
  waiting for transfers between devices  41.9 us (55%)
  starting transfers between devices  25.3 us (33%)
  Pallas kernels  6.5 us (9%)
  local copies, waits for them, and re-layouts  1.05 us (1%)
  between operations  0.88 us (1%)
    ppermute x21, waiting for transfers between devices, swap(): return lax.ppermute(value, both, pairs)  27.4 us
    ppermute x21, starting transfers between devices, swap(): return lax.ppermute(value, both, pairs)  18.3 us
    ppermute x6, waiting for transfers between devices, hop(): return lax.ppermute(value, both, pairs)  14.5 us
    ppermute x6, starting transfers between devices, hop(): return lax.ppermute(value, both, pairs)  7.01 us
    pallas_call x23, Pallas kernels, call(): pl.pallas_call(kernel, out_shape=[jax.ShapeDtypeStruct(shape, dtype) for...  6.5 us
  transfers between devices with their start and end apart: 27, of which 14 were waited for; matrix products, arithmetic and copies ran while one was open for 0% of the time, Pallas kernels for 4%

profile of v3, /device:TPU:0, one launch (start us, length us, event | category | flops | bytes accessed | tf_op | source)
XLA Modules:
  0.0 75.6 jit_solution(5910981001991563764)
XLA Ops:
  0.6 1.4 %shard_map.77 = (f32[304,256]{1,0:T(8,128)S(1)}, f32[304,256]{1,0:T(8,128)S(1)}, f32[304,256]{1,0:T(8,128)S(1)}, f32[48,256]{1,0:T(8,128)S(1)}, f32[8,256]{1,0:T(8,128)S(1)}) custom-call(f32[1,256]{1,0:T(1,128)} %bitcast.9, s32[1,256]{1,0:T(1,128)} %mask_hbm.1, f32[256,256]{1,0:T(8,128)} %bitcast.8, f32[256,384]{1,0:T(8,128)} %bitcast.7), custom_call_target="tpu_custom_call" | custom-call | bytes 2097152 | tf_op jit(solution)/shard_map/pallas_call | solution.py:25
  2.6 2.6 %collective-permute-start.1 = (f32[304,256]{1,0:T(8,128)S(1)}, f32[304,256]{1,0:T(8,128)S(1)}, u32[]{:S(2)}, u32[]{:S(2)}) collective-permute-start(f32[304,256]{1,0:T(8,128)S(1)} %get-tuple-element.77), channel_id=1, source_target_pairs={{0,4},{1,5},{2,6},{3,7},{4,0},{5,1},{6,2},{7,3},{8,12},{9,13},{10,... | collective-permute-start | bytes 933896 | tf_op jit(solution)/shard_map/ppermute | solution.py:328
  5.2 1.4 %collective-permute-start.2 = (f32[304,256]{1,0:T(8,128)S(1)}, f32[304,256]{1,0:T(8,128)S(1)}, u32[]{:S(2)}, u32[]{:S(2)}) collective-permute-start(f32[304,256]{1,0:T(8,128)S(1)} %get-tuple-element.78), channel_id=1, source_target_pairs={{0,6},{1,7},{2,4},{3,5},{4,2},{5,3},{6,0},{7,1},{8,14},{9,15},{10,... | collective-permute-start | bytes 933896 | tf_op jit(solution)/shard_map/ppermute | solution.py:328
  6.7 1.0 %copy-done.1 = f32[1,256,512]{2,1,0:T(8,128)S(1)} copy-done((f32[1,256,512]{2,1,0:T(8,128)S(1)}, f32[1,256,512]{2,1,0:T(8,128)}, u32[]{:S(2)}) %copy-start.1) | copy-done | bytes 524312
  8.0 2.0 %collective-permute-start.11 = (f32[512,256]{1,0:T(8,128)S(1)}, f32[512,256]{1,0:T(8,128)S(1)}, u32[]{:S(2)}, u32[]{:S(2)}) collective-permute-start(f32[512,256]{1,0:T(8,128)S(1)} %shard_map.79.refs_0_), channel_id=1, source_target_pairs={{0,4},{1,5},{2,6},{3,7},{4,0},{5,1},{6,2},{7,3},{8,12},{9,13},{10,... | collective-permute-start | bytes 1572872 | tf_op jit(solution)/shard_map/ppermute | solution.py:328
  10.0 1.5 %collective-permute-start.10 = (f32[512,256]{1,0:T(8,128)S(1)}, f32[512,256]{1,0:T(8,128)S(1)}, u32[]{:S(2)}, u32[]{:S(2)}) collective-permute-start(f32[512,256]{1,0:T(8,128)S(1)} %shard_map.79.refs_0_), channel_id=1, source_target_pairs={{0,2},{1,3},{2,0},{3,1},{4,6},{5,7},{6,4},{7,5},{8,10},{9,11},{10,... | collective-permute-start | bytes 1572872 | tf_op jit(solution)/shard_map/ppermute | solution.py:328
  11.8 8.2 %collective-permute-done.1.refs_2_ = f32[304,256]{1,0:T(8,128)S(1)} collective-permute-done((f32[304,256]{1,0:T(8,128)S(1)}, f32[304,256]{1,0:T(8,128)S(1)}, u32[]{:S(2)}, u32[]{:S(2)}) %collective-permute-start.1) | collective-permute-done | bytes 311328 | tf_op jit(solution)/shard_map/ppermute | solution.py:328
  20.1 1.5 %collective-permute-done.refs_1_ = f32[304,256]{1,0:T(8,128)S(1)} collective-permute-done((f32[304,256]{1,0:T(8,128)S(1)}, f32[304,256]{1,0:T(8,128)S(1)}, u32[]{:S(2)}, u32[]{:S(2)}) %collective-permute-start) | collective-permute-done | bytes 311328 | tf_op jit(solution)/shard_map/ppermute | solution.py:328
  22.1 1.1 %collective-permute-done.4.refs_5_ = f32[304,256]{1,0:T(8,128)S(1)} collective-permute-done((f32[304,256]{1,0:T(8,128)S(1)}, f32[304,256]{1,0:T(8,128)S(1)}, u32[]{:S(2)}, u32[]{:S(2)}) %collective-permute-start.4) | collective-permute-done | bytes 311328 | tf_op jit(solution)/shard_map/ppermute | solution.py:328
  24.4 0.9 %shard_map.81 = (f32[4,48,512]{2,1,0:T(8,128)S(1)}, f32[48,512]{1,0:T(8,128)S(1)}, f32[48,512]{1,0:T(8,128)S(1)}, f32[48,512]{1,0:T(8,128)S(1)}, f32[48,512]{1,0:T(8,128)S(1)}, /*index=5*/f32[48,512]{1,0:T(8,128)S(1)}) custom-call(f32[48,512]{1,0:T(8,128)S(1)} %shard_map.78.start_ref, f32[8,256]{1,0:T(8,128)S(1)} %get-tuple-element.82.coef_ref, ...), custom_call_target="tpu_custom_call" | custom-call | bytes 2097152 | tf_op jit(solution)/shard_map/pallas_call | solution.py:25
  25.3 3.1 %collective-permute-start.7 = (f32[48,512]{1,0:T(8,128)S(1)}, f32[48,512]{1,0:T(8,128)S(1)}, u32[]{:S(2)}, u32[]{:S(2)}) collective-permute-start(f32[48,512]{1,0:T(8,128)S(1)} %get-tuple-element.91), channel_id=1, source_target_pairs={{0,8},{1,9},{2,10},{3,11},{4,12},{5,13},{6,14},{7,15}} | collective-permute-start | bytes 294920 | tf_op jit(solution)/shard_map/ppermute | solution.py:345
  28.4 2.3 %collective-permute-done.7.start_ref = f32[48,512]{1,0:T(8,128)S(1)} collective-permute-done((f32[48,512]{1,0:T(8,128)S(1)}, f32[48,512]{1,0:T(8,128)S(1)}, u32[]{:S(2)}, u32[]{:S(2)}) %collective-permute-start.7) | collective-permute-done | bytes 98336 | tf_op jit(solution)/shard_map/ppermute | solution.py:345
  31.4 0.9 %collective-permute-done.10.refs_1_ = f32[512,256]{1,0:T(8,128)S(1)} collective-permute-done((f32[512,256]{1,0:T(8,128)S(1)}, f32[512,256]{1,0:T(8,128)S(1)}, u32[]{:S(2)}, u32[]{:S(2)}) %collective-permute-start.10) | collective-permute-done | bytes 524320 | tf_op jit(solution)/shard_map/ppermute | solution.py:328
  32.4 1.8 %collective-permute-start.12 = (f32[512,256]{1,0:T(8,128)S(1)}, f32[512,256]{1,0:T(8,128)S(1)}, u32[]{:S(2)}, u32[]{:S(2)}) collective-permute-start(f32[512,256]{1,0:T(8,128)S(1)} %shard_map.87), channel_id=1, source_target_pairs={{0,4},{1,3},{2,6},{3,1},{4,0},{5,7},{6,2},{7,5},{8,12},{9,11},{10,... | collective-permute-start | bytes 1572872 | tf_op jit(solution)/shard_map/ppermute | solution.py:328
  34.1 0.7 collective-permute-start.9
  35.5 6.1 %collective-permute-done.12.refs_0_ = f32[512,256]{1,0:T(8,128)S(1)} collective-permute-done((f32[512,256]{1,0:T(8,128)S(1)}, f32[512,256]{1,0:T(8,128)S(1)}, u32[]{:S(2)}, u32[]{:S(2)}) %collective-permute-start.12) | collective-permute-done | bytes 524320 | tf_op jit(solution)/shard_map/ppermute | solution.py:328
  41.7 1.9 %collective-permute-done.16.refs_7_ = f32[512,256]{1,0:T(8,128)S(1)} collective-permute-done((f32[512,256]{1,0:T(8,128)S(1)}, f32[512,256]{1,0:T(8,128)S(1)}, u32[]{:S(2)}, u32[]{:S(2)}) %collective-permute-start.16) | collective-permute-done | bytes 524320 | tf_op jit(solution)/shard_map/ppermute | solution.py:328
  43.5 0.8 %shard_map.89 = (bf16[4,2,512,256]{3,2,1,0:T(8,128)(2,1)S(1)}, bf16[4,2,512,256]{3,2,1,0:T(8,128)(2,1)S(1)}) custom-call(f32[512,256]{1,0:T(8,128)S(1)} %get-tuple-element.118.refs_0_, f32[512,256]{1,0:T(8,128)S(1)} %get-tuple-element.119.refs_1_, f32[512,256]{1,0:T(8,128)S(1)} %get-tuple-element.120.refs_2_, f32[512,256]{1,0:T(8,128)S(1)} %shard_map.88.refs_3_, ...), custom_call_target="tpu_custom_call" | custom-call | bytes 2097152 | tf_op jit(solution)/shard_map/pallas_call | solution.py:25
  44.3 0.7 collective-permute-start.17
  45.1 0.7 collective-permute-start.18
  45.8 1.3 %collective-permute-start.22 = (f32[48,512]{1,0:T(8,128)S(1)}, f32[48,512]{1,0:T(8,128)S(1)}, u32[]{:S(2)}, u32[]{:S(2)}) collective-permute-start(f32[48,512]{1,0:T(8,128)S(1)} %shard_map.93.refs_4_), channel_id=1, source_target_pairs={{8,0},{9,1},{10,2},{11,3},{12,4},{13,5},{14,6},{15,7}} | collective-permute-start | bytes 294920 | tf_op jit(solution)/shard_map/ppermute | solution.py:345
  47.1 1.8 %collective-permute-start.19 = (f32[48,512]{1,0:T(8,128)S(1)}, f32[48,512]{1,0:T(8,128)S(1)}, u32[]{:S(2)}, u32[]{:S(2)}) collective-permute-start(f32[48,512]{1,0:T(8,128)S(1)} %get-tuple-element.129), channel_id=1, source_target_pairs={{0,2},{1,3},{2,0},{3,1},{4,6},{5,7},{6,4},{7,5},{8,10},{9,11},{10,... | collective-permute-start | bytes 294920 | tf_op jit(solution)/shard_map/ppermute | solution.py:328
  48.9 1.5 %collective-permute-start.20 = (f32[48,512]{1,0:T(8,128)S(1)}, f32[48,512]{1,0:T(8,128)S(1)}, u32[]{:S(2)}, u32[]{:S(2)}) collective-permute-start(f32[48,512]{1,0:T(8,128)S(1)} %get-tuple-element.130), channel_id=1, source_target_pairs={{0,4},{1,5},{2,6},{3,7},{4,0},{5,1},{6,2},{7,3},{8,12},{9,13},{10,... | collective-permute-start | bytes 294920 | tf_op jit(solution)/shard_map/ppermute | solution.py:328
  50.7 12.2 %collective-permute-done.22.start_ref = f32[48,512]{1,0:T(8,128)S(1)} collective-permute-done((f32[48,512]{1,0:T(8,128)S(1)}, f32[48,512]{1,0:T(8,128)S(1)}, u32[]{:S(2)}, u32[]{:S(2)}) %collective-permute-start.22) | collective-permute-done | bytes 98336 | tf_op jit(solution)/shard_map/ppermute | solution.py:345
  62.9 1.2 %shard_map.97 = (f32[48,512]{1,0:T(8,128)S(1)}, f32[48,512]{1,0:T(8,128)S(1)}, f32[48,512]{1,0:T(8,128)S(1)}, f32[48,512]{1,0:T(8,128)S(1)}) custom-call(f32[48,512]{1,0:T(8,128)S(1)} %collective-permute-done.22.start_ref, f32[8,256]{1,0:T(8,128)S(1)} %get-tuple-element.82.coef_ref, ...), custom_call_target="tpu_custom_call", output_to_operand_aliasing={{0}: (5, {}), {1}: (6, {}), {2}: (7, {}), {3}: (8, {})} | custom-call | bytes 2097152 | tf_op jit(solution)/shard_map/pallas_call | solution.py:25
  64.1 1.6 %collective-permute-start.23 = (f32[48,512]{1,0:T(8,128)S(1)}, f32[48,512]{1,0:T(8,128)S(1)}, u32[]{:S(2)}, u32[]{:S(2)}) collective-permute-start(f32[48,512]{1,0:T(8,128)S(1)} %get-tuple-element.145), channel_id=1, source_target_pairs={{0,2},{1,3},{2,0},{3,1},{4,6},{5,7},{6,4},{7,5},{8,10},{9,11},{10,... | collective-permute-start | bytes 294920 | tf_op jit(solution)/shard_map/ppermute | solution.py:328
  65.6 1.5 %collective-permute-start.24 = (f32[48,512]{1,0:T(8,128)S(1)}, f32[48,512]{1,0:T(8,128)S(1)}, u32[]{:S(2)}, u32[]{:S(2)}) collective-permute-start(f32[48,512]{1,0:T(8,128)S(1)} %get-tuple-element.146), channel_id=1, source_target_pairs={{0,4},{1,5},{2,6},{3,7},{4,0},{5,1},{6,2},{7,3},{8,12},{9,13},{10,... | collective-permute-start | bytes 294920 | tf_op jit(solution)/shard_map/ppermute | solution.py:328
  67.6 1.3 %collective-permute-done.23.refs_5_ = f32[48,512]{1,0:T(8,128)S(1)} collective-permute-done((f32[48,512]{1,0:T(8,128)S(1)}, f32[48,512]{1,0:T(8,128)S(1)}, u32[]{:S(2)}, u32[]{:S(2)}) %collective-permute-start.23) | collective-permute-done | bytes 98336 | tf_op jit(solution)/shard_map/ppermute | solution.py:328
  68.9 1.3 %collective-permute-done.24.refs_6_ = f32[48,512]{1,0:T(8,128)S(1)} collective-permute-done((f32[48,512]{1,0:T(8,128)S(1)}, f32[48,512]{1,0:T(8,128)S(1)}, u32[]{:S(2)}, u32[]{:S(2)}) %collective-permute-start.24) | collective-permute-done | bytes 98336 | tf_op jit(solution)/shard_map/ppermute | solution.py:328
  70.2 2.4 %collective-permute-done.25.refs_7_ = f32[48,512]{1,0:T(8,128)S(1)} collective-permute-done((f32[48,512]{1,0:T(8,128)S(1)}, f32[48,512]{1,0:T(8,128)S(1)}, u32[]{:S(2)}, u32[]{:S(2)}) %collective-permute-start.25) | collective-permute-done | bytes 98336 | tf_op jit(solution)/shard_map/ppermute | solution.py:328
  72.8 1.7 %collective-permute-done.26.refs_8_ = f32[8,48,256]{2,1,0:T(8,128)S(1)} collective-permute-done((f32[8,48,256]{2,1,0:T(8,128)S(1)}, f32[8,48,256]{2,1,0:T(8,128)S(1)}, u32[]{:S(2)}, u32[]{:S(2)}) %collective-permute-start.26) | collective-permute-done | bytes 393248 | tf_op jit(solution)/shard_map/ppermute | solution.py:328
  74.5 1.1 %shard_map.99 = (f32[256,384]{1,0:T(8,128)}, f32[256,384]{1,0:T(8,128)}) custom-call(f32[48,512]{1,0:T(8,128)S(1)} %get-tuple-element.128.refs_0_, f32[48,512]{1,0:T(8,128)S(1)} %collective-permute-done.19.refs_1_, f32[48,512]{1,0:T(8,128)S(1)} %collective-permute-done.20.refs_2_, f32[48,512]{1,0:T(8,128)S(1)} %collective-permute-done.21.refs_3_, ...), custom_call_target="tpu_custom_call" | custom-call | bytes 2097152 | tf_op jit(solution)/shard_map/pallas_call | solution.py:25
  (49 shorter events, 5.3 us)
Async XLA Ops:
  0.6 10.9 %copy-start = (f32[512,384]{1,0:T(8,128)S(1)}, f32[512,384]{1,0:T(8,128)}, u32[]{:S(2)}) copy-start(f32[512,384]{1,0:T(8,128)} %prior_ref.1) | copy-start | bytes 2359300
  2.1 8.0 %collective-permute-start.3 = (f32[304,256]{1,0:T(8,128)S(1)}, f32[304,256]{1,0:T(8,128)S(1)}, u32[]{:S(2)}, u32[]{:S(2)}) collective-permute-start(f32[304,256]{1,0:T(8,128)S(1)} %get-tuple-element.76.refs_0_), channel_id=1, source_target_pairs={{0,1},{1,0},{2,3},{3,2},{4,5},{5,4},{6,7},{7,6},{8,9},{9,8},{10,11... | collective-permute-start | bytes 933896 | tf_op jit(solution)/shard_map/ppermute | solution.py:328
  2.6 17.5 %collective-permute-start.1 = (f32[304,256]{1,0:T(8,128)S(1)}, f32[304,256]{1,0:T(8,128)S(1)}, u32[]{:S(2)}, u32[]{:S(2)}) collective-permute-start(f32[304,256]{1,0:T(8,128)S(1)} %get-tuple-element.77), channel_id=1, source_target_pairs={{0,4},{1,5},{2,6},{3,7},{4,0},{5,1},{6,2},{7,3},{8,12},{9,13},{10,... | collective-permute-start | bytes 933896 | tf_op jit(solution)/shard_map/ppermute | solution.py:328
  5.2 14.9 %collective-permute-start.2 = (f32[304,256]{1,0:T(8,128)S(1)}, f32[304,256]{1,0:T(8,128)S(1)}, u32[]{:S(2)}, u32[]{:S(2)}) collective-permute-start(f32[304,256]{1,0:T(8,128)S(1)} %get-tuple-element.78), channel_id=1, source_target_pairs={{0,6},{1,7},{2,4},{3,5},{4,2},{5,3},{6,0},{7,1},{8,14},{9,15},{10,... | collective-permute-start | bytes 933896 | tf_op jit(solution)/shard_map/ppermute | solution.py:328
  6.6 15.0 %collective-permute-start = (f32[304,256]{1,0:T(8,128)S(1)}, f32[304,256]{1,0:T(8,128)S(1)}, u32[]{:S(2)}, u32[]{:S(2)}) collective-permute-start(f32[304,256]{1,0:T(8,128)S(1)} %get-tuple-element.76.refs_0_), channel_id=1, source_target_pairs={{0,2},{1,3},{2,0},{3,1},{4,6},{5,7},{6,4},{7,5},{8,10},{9,11},{10,... | collective-permute-start | bytes 933896 | tf_op jit(solution)/shard_map/ppermute | solution.py:328
  6.7 1.0 %copy-start.1 = (f32[1,256,512]{2,1,0:T(8,128)S(1)}, f32[1,256,512]{2,1,0:T(8,128)}, u32[]{:S(2)}) copy-start(f32[1,256,512]{2,1,0:T(8,128)} %param.11) | copy-start | bytes 1572868
  8.0 23.4 %collective-permute-start.11 = (f32[512,256]{1,0:T(8,128)S(1)}, f32[512,256]{1,0:T(8,128)S(1)}, u32[]{:S(2)}, u32[]{:S(2)}) collective-permute-start(f32[512,256]{1,0:T(8,128)S(1)} %shard_map.79.refs_0_), channel_id=1, source_target_pairs={{0,4},{1,5},{2,6},{3,7},{4,0},{5,1},{6,2},{7,3},{8,12},{9,13},{10,... | collective-permute-start | bytes 1572872 | tf_op jit(solution)/shard_map/ppermute | solution.py:328
  10.0 22.3 %collective-permute-start.10 = (f32[512,256]{1,0:T(8,128)S(1)}, f32[512,256]{1,0:T(8,128)S(1)}, u32[]{:S(2)}, u32[]{:S(2)}) collective-permute-start(f32[512,256]{1,0:T(8,128)S(1)} %shard_map.79.refs_0_), channel_id=1, source_target_pairs={{0,2},{1,3},{2,0},{3,1},{4,6},{5,7},{6,4},{7,5},{8,10},{9,11},{10,... | collective-permute-start | bytes 1572872 | tf_op jit(solution)/shard_map/ppermute | solution.py:328
  21.6 1.6 %collective-permute-start.4 = (f32[304,256]{1,0:T(8,128)S(1)}, f32[304,256]{1,0:T(8,128)S(1)}, u32[]{:S(2)}, u32[]{:S(2)}) collective-permute-start(f32[304,256]{1,0:T(8,128)S(1)} %collective-permute-done.refs_1_), channel_id=1, source_target_pairs={{0,1},{1,0},{2,3},{3,2},{4,5},{5,4},{6,7},{7,6},{8,9},{9,8},{10,11... | collective-permute-start | bytes 933896 | tf_op jit(solution)/shard_map/ppermute | solution.py:328
  21.6 2.0 %collective-permute-start.5 = (f32[304,256]{1,0:T(8,128)S(1)}, f32[304,256]{1,0:T(8,128)S(1)}, u32[]{:S(2)}, u32[]{:S(2)}) collective-permute-start(f32[304,256]{1,0:T(8,128)S(1)} %collective-permute-done.1.refs_2_), channel_id=1, source_target_pairs={{0,1},{1,0},{2,3},{3,2},{4,5},{5,4},{6,7},{7,6},{8,9},{9,8},{10,11... | collective-permute-start | bytes 933896 | tf_op jit(solution)/shard_map/ppermute | solution.py:328
  22.1 2.0 %collective-permute-start.6 = (f32[304,256]{1,0:T(8,128)S(1)}, f32[304,256]{1,0:T(8,128)S(1)}, u32[]{:S(2)}, u32[]{:S(2)}) collective-permute-start(f32[304,256]{1,0:T(8,128)S(1)} %collective-permute-done.2.refs_3_), channel_id=1, source_target_pairs={{0,1},{1,0},{2,3},{3,2},{4,5},{5,4},{6,7},{7,6},{8,9},{9,8},{10,11... | collective-permute-start | bytes 933896 | tf_op jit(solution)/shard_map/ppermute | solution.py:328
  25.3 5.4 %collective-permute-start.7 = (f32[48,512]{1,0:T(8,128)S(1)}, f32[48,512]{1,0:T(8,128)S(1)}, u32[]{:S(2)}, u32[]{:S(2)}) collective-permute-start(f32[48,512]{1,0:T(8,128)S(1)} %get-tuple-element.91), channel_id=1, source_target_pairs={{0,8},{1,9},{2,10},{3,11},{4,12},{5,13},{6,14},{7,15}} | collective-permute-start | bytes 294920 | tf_op jit(solution)/shard_map/ppermute | solution.py:345
  30.7 3.4 %collective-permute-start.8 = (f32[48,512]{1,0:T(8,128)S(1)}, f32[48,512]{1,0:T(8,128)S(1)}, u32[]{:S(2)}, u32[]{:S(2)}) collective-permute-start(f32[48,512]{1,0:T(8,128)S(1)} %get-tuple-element.97.refs_3_), channel_id=1, source_target_pairs={{8,16},{9,17},{10,18},{11,19},{12,20},{13,21},{14,22},{15,23}} | collective-permute-start | bytes 294920 | tf_op jit(solution)/shard_map/ppermute | solution.py:345
  32.4 9.2 %collective-permute-start.12 = (f32[512,256]{1,0:T(8,128)S(1)}, f32[512,256]{1,0:T(8,128)S(1)}, u32[]{:S(2)}, u32[]{:S(2)}) collective-permute-start(f32[512,256]{1,0:T(8,128)S(1)} %shard_map.87), channel_id=1, source_target_pairs={{0,4},{1,3},{2,6},{3,1},{4,0},{5,7},{6,2},{7,5},{8,12},{9,11},{10,... | collective-permute-start | bytes 1572872 | tf_op jit(solution)/shard_map/ppermute | solution.py:328
  34.1 7.5 %collective-permute-start.13 = (f32[512,256]{1,0:T(8,128)S(1)}, f32[512,256]{1,0:T(8,128)S(1)}, u32[]{:S(2)}, u32[]{:S(2)}) collective-permute-start(f32[512,256]{1,0:T(8,128)S(1)} %get-tuple-element.120.refs_2_), channel_id=1, source_target_pairs={{0,1},{1,0},{2,3},{3,2},{4,5},{5,4},{6,7},{7,6},{8,9},{9,8},{10,11... | collective-permute-start | bytes 1572872 | tf_op jit(solution)/shard_map/ppermute | solution.py:328
  34.1 7.5 %collective-permute-start.9 = (f32[48,512]{1,0:T(8,128)S(1)}, f32[48,512]{1,0:T(8,128)S(1)}, u32[]{:S(2)}, u32[]{:S(2)}) collective-permute-start(f32[48,512]{1,0:T(8,128)S(1)} %get-tuple-element.103), channel_id=1, source_target_pairs={{16,24},{17,25},{18,26},{19,27},{20,28},{21,29},{22,30},{23,31}} | collective-permute-start | bytes 294920 | tf_op jit(solution)/shard_map/ppermute | solution.py:345
  34.8 6.8 %collective-permute-start.14 = (f32[512,256]{1,0:T(8,128)S(1)}, f32[512,256]{1,0:T(8,128)S(1)}, u32[]{:S(2)}, u32[]{:S(2)}) collective-permute-start(f32[512,256]{1,0:T(8,128)S(1)} %get-tuple-element.118.refs_0_), channel_id=1, source_target_pairs={{0,1},{1,0},{2,3},{3,2},{4,5},{5,4},{6,7},{7,6},{8,9},{9,8},{10,11... | collective-permute-start | bytes 1572872 | tf_op jit(solution)/shard_map/ppermute | solution.py:328
  35.4 6.3 %collective-permute-start.15 = (f32[512,256]{1,0:T(8,128)S(1)}, f32[512,256]{1,0:T(8,128)S(1)}, u32[]{:S(2)}, u32[]{:S(2)}) collective-permute-start(f32[512,256]{1,0:T(8,128)S(1)} %get-tuple-element.119.refs_1_), channel_id=1, source_target_pairs={{0,1},{1,0},{2,3},{3,2},{4,5},{5,4},{6,7},{7,6},{8,9},{9,8},{10,11... | collective-permute-start | bytes 1572872 | tf_op jit(solution)/shard_map/ppermute | solution.py:328
  41.6 1.9 %collective-permute-start.16 = (f32[512,256]{1,0:T(8,128)S(1)}, f32[512,256]{1,0:T(8,128)S(1)}, u32[]{:S(2)}, u32[]{:S(2)}) collective-permute-start(f32[512,256]{1,0:T(8,128)S(1)} %shard_map.88.refs_3_), channel_id=1, source_target_pairs={{0,1},{1,0},{2,3},{3,2},{4,5},{5,4},{6,7},{7,6},{8,9},{9,8},{10,11... | collective-permute-start | bytes 1572872 | tf_op jit(solution)/shard_map/ppermute | solution.py:328
  44.3 0.7 collective-permute-start.17
  45.1 0.7 collective-permute-start.18
  45.8 17.1 %collective-permute-start.22 = (f32[48,512]{1,0:T(8,128)S(1)}, f32[48,512]{1,0:T(8,128)S(1)}, u32[]{:S(2)}, u32[]{:S(2)}) collective-permute-start(f32[48,512]{1,0:T(8,128)S(1)} %shard_map.93.refs_4_), channel_id=1, source_target_pairs={{8,0},{9,1},{10,2},{11,3},{12,4},{13,5},{14,6},{15,7}} | collective-permute-start | bytes 294920 | tf_op jit(solution)/shard_map/ppermute | solution.py:345
  47.1 20.0 %collective-permute-start.19 = (f32[48,512]{1,0:T(8,128)S(1)}, f32[48,512]{1,0:T(8,128)S(1)}, u32[]{:S(2)}, u32[]{:S(2)}) collective-permute-start(f32[48,512]{1,0:T(8,128)S(1)} %get-tuple-element.129), channel_id=1, source_target_pairs={{0,2},{1,3},{2,0},{3,1},{4,6},{5,7},{6,4},{7,5},{8,10},{9,11},{10,... | collective-permute-start | bytes 294920 | tf_op jit(solution)/shard_map/ppermute | solution.py:328
  48.9 18.8 %collective-permute-start.20 = (f32[48,512]{1,0:T(8,128)S(1)}, f32[48,512]{1,0:T(8,128)S(1)}, u32[]{:S(2)}, u32[]{:S(2)}) collective-permute-start(f32[48,512]{1,0:T(8,128)S(1)} %get-tuple-element.130), channel_id=1, source_target_pairs={{0,4},{1,5},{2,6},{3,7},{4,0},{5,1},{6,2},{7,3},{8,12},{9,13},{10,... | collective-permute-start | bytes 294920 | tf_op jit(solution)/shard_map/ppermute | solution.py:328
  50.4 17.2 %collective-permute-start.21 = (f32[48,512]{1,0:T(8,128)S(1)}, f32[48,512]{1,0:T(8,128)S(1)}, u32[]{:S(2)}, u32[]{:S(2)}) collective-permute-start(f32[48,512]{1,0:T(8,128)S(1)} %get-tuple-element.131), channel_id=1, source_target_pairs={{0,6},{1,7},{2,4},{3,5},{4,2},{5,3},{6,0},{7,1},{8,14},{9,15},{10,... | collective-permute-start | bytes 294920 | tf_op jit(solution)/shard_map/ppermute | solution.py:328
  64.1 4.9 %collective-permute-start.23 = (f32[48,512]{1,0:T(8,128)S(1)}, f32[48,512]{1,0:T(8,128)S(1)}, u32[]{:S(2)}, u32[]{:S(2)}) collective-permute-start(f32[48,512]{1,0:T(8,128)S(1)} %get-tuple-element.145), channel_id=1, source_target_pairs={{0,2},{1,3},{2,0},{3,1},{4,6},{5,7},{6,4},{7,5},{8,10},{9,11},{10,... | collective-permute-start | bytes 294920 | tf_op jit(solution)/shard_map/ppermute | solution.py:328
  65.6 4.6 %collective-permute-start.24 = (f32[48,512]{1,0:T(8,128)S(1)}, f32[48,512]{1,0:T(8,128)S(1)}, u32[]{:S(2)}, u32[]{:S(2)}) collective-permute-start(f32[48,512]{1,0:T(8,128)S(1)} %get-tuple-element.146), channel_id=1, source_target_pairs={{0,4},{1,5},{2,6},{3,7},{4,0},{5,1},{6,2},{7,3},{8,12},{9,13},{10,... | collective-permute-start | bytes 294920 | tf_op jit(solution)/shard_map/ppermute | solution.py:328
  67.1 5.5 %collective-permute-start.25 = (f32[48,512]{1,0:T(8,128)S(1)}, f32[48,512]{1,0:T(8,128)S(1)}, u32[]{:S(2)}, u32[]{:S(2)}) collective-permute-start(f32[48,512]{1,0:T(8,128)S(1)} %get-tuple-element.147), channel_id=1, source_target_pairs={{0,6},{1,7},{2,4},{3,5},{4,2},{5,3},{6,0},{7,1},{8,14},{9,15},{10,... | collective-permute-start | bytes 294920 | tf_op jit(solution)/shard_map/ppermute | solution.py:328
  72.7 1.8 %collective-permute-start.26 = (f32[8,48,256]{2,1,0:T(8,128)S(1)}, f32[8,48,256]{2,1,0:T(8,128)S(1)}, u32[]{:S(2)}, u32[]{:S(2)}) collective-permute-start(f32[8,48,256]{2,1,0:T(8,128)S(1)} %shard_map.98), channel_id=1, source_target_pairs={{0,1},{1,0},{2,3},{3,2},{4,5},{5,4},{6,7},{7,6},{8,9},{9,8},{10,11... | collective-permute-start | bytes 1179656 | tf_op jit(solution)/shard_map/ppermute | solution.py:328

commit v4 on v3

--- a/solution.py
+++ b/solution.py
@@ -13,6 +13,10 @@
 FW = (0, 0, 10**11, 10**11)
 BW = (0, 10**10)
 JF = 10**11
+JP = 0
+JJ = 0
+GA = 10**10
+AF = 0
 G1 = G2 = G3 = 10**9
 G4 = 10**9
 G6 = 10**9
@@ -164,13 +168,13 @@
             parts[block * half // depth][at : at + half, part * half : (part + 1) * half] = piece
 
 
-def gather_kernel(share, depth, *refs):
+def gather_kernel(flips, share, depth, *refs):
     _, spot, row = place()
-    near, far, rest = refs[:GROUP], refs[GROUP : 2 * GROUP], refs[2 * GROUP :]
+    near, far, rest = refs[: len(flips)], refs[len(flips) : 2 * len(flips)], refs[2 * len(flips) :]
     high_ref, low_ref = rest[-2 - (share > 0)], rest[-1 - (share > 0)]
-    for flip in range(GROUP):
+    for index, flip in enumerate(flips):
         at = jnp.bitwise_xor(spot, flip)
-        for ref, block in ((near[flip], row), (far[flip], 1 - row)):
+        for ref, block in ((near[index], row), (far[index], 1 - row)):
             high, low = split(ref[0:depth, :])
             high_ref[at, block] = high
             low_ref[at, block] = low
@@ -200,25 +204,51 @@
             ref[...] = state
 
 
-def filter_kernel(turn, start_ref, coef_ref, high_ref, low_ref, obs_ref, *rest):
-    out_ref, sent, last_ref = rest[-GROUP - 2], rest[-GROUP - 1 : -1], rest[-1]
+def filter_steps(state, coef_ref, high_ref, low_ref, obs_ref, keep):
+    half = high_ref.shape[3] // 2
+    for step in range(GROUP):
+        moved, values = transition(state, coef_ref, half)
+        innovation = -values if obs_ref is None else obs_ref[step] - values
+        update = [
+            multiply(innovation, high_ref[step, block], low_ref[step, block]) for block in range(high_ref.shape[1])
+        ]
+        state = moved + jnp.concatenate(update, 1)
+        keep(step, state)
+    return state
+
+
+def filter_kernel(turn, middle, start_ref, coef_ref, high_ref, low_ref, obs_ref, *rest):
+    lasts = () if middle else rest[-1:]
+    outs = rest[-GROUP - 1 :] if middle else rest[-GROUP - 2 : -1]
+    out_ref, sent = outs[0], outs[1:]
     group, spot, _ = place()
-    half = high_ref.shape[3] // 2
 
     @pl.when(group == turn)
     def _():
-        state = start_ref[...]
-        for step in range(GROUP):
-            moved, values = transition(state, coef_ref, half)
-            innovation = obs_ref[step] - values
-            update = [
-                multiply(innovation, high_ref[step, block], low_ref[step, block])
-                for block in range(high_ref.shape[1])
-            ]
-            state = moved + jnp.concatenate(update, 1)
+        def keep(step, state):
             out_ref[step] = state
             pack(spot, step, sent, state)
-        last_ref[...] = state
+
+        state = filter_steps(start_ref[...], coef_ref, high_ref, low_ref, obs_ref, keep)
+        for ref in lasts:
+            ref[...] = state
+
+
+def joined_filter_kernel(groups, coef_ref, high_ref, low_ref, obs_ref, map_high_ref, map_low_ref, offset_ref):
+    group, _, _ = place()
+
+    @pl.when(jnp.logical_and(group > 0, group < groups - 1))
+    def _():
+        blocks, states, lanes = map_high_ref.shape
+        nothing = jnp.zeros(offset_ref.shape, F32)
+        offset_ref[...] = filter_steps(nothing, coef_ref, high_ref, low_ref, obs_ref, lambda *_: None)
+        rows = lax.broadcasted_iota(jnp.int32, (states, states), 0)
+        columns = lax.broadcasted_iota(jnp.int32, (states, states), 1)
+        unit = jnp.where(rows == columns, 1.0, 0.0)
+        joined = filter_steps(unit, coef_ref, high_ref, low_ref, None, lambda *_: None)
+        for block in range(blocks):
+            part = joined[:, block * lanes : (block + 1) * lanes]
+            map_high_ref[block], map_low_ref[block] = split(part)
 
 
 def smooth_steps(state, coef_ref, high_ref, low_ref, filt_ref, keep, last_group=False):
@@ -266,21 +296,21 @@
             map_high_ref[block], map_low_ref[block] = split(joined[block])
 
 
-def jump_kernel(turn, groups, start_ref, map_high_ref, map_low_ref, offset_ref, first_ref):
+def jump_kernel(active, start_ref, map_high_ref, map_low_ref, offset_ref, first_ref):
     group, _, _ = place()
 
-    @pl.when(group == groups - 1 - turn)
+    @pl.when(group == active)
     def _():
         start = start_ref[...]
         moved = [multiply(start, map_high_ref[block], map_low_ref[block]) for block in range(map_high_ref.shape[0])]
         first_ref[...] = offset_ref[...] + jnp.concatenate(moved, 1)
 
 
-def across_kernel(*refs):
+def across_kernel(slots, *refs):
     _, _, row = place()
     lanes = refs[-1].shape[2]
-    for at, ref in enumerate(refs[:-1]):
-        refs[-1][at] = ref[:, pl.ds(pl.multiple_of((1 - row) * lanes, LANES), lanes)]
+    for slot, ref in zip(slots, refs):
+        refs[-1][slot] = ref[:, pl.ds(pl.multiple_of((1 - row) * lanes, LANES), lanes)]
 
 
 def home_kernel(share, *refs):
@@ -382,21 +412,37 @@
     far = [own_far] + [neighbour(value) for value in near]
     near = [messages[0], *near]
     high, low, obs = call(
-        functools.partial(gather_kernel, share, sites),
+        functools.partial(gather_kernel, range(GROUP), share, sites),
         (*near, *far, own_obs),
         [((GROUP, rows, sites, panel), BF16)] * 2 + [((GROUP, share, sites), F32)],
     )
     start, filtered = prior, ()
+    *joined, offset = call(
+        functools.partial(joined_filter_kernel, groups),
+        (coef, high, low, obs),
+        [((rows, states, panel), BF16)] * 2 + [((share, states), F32)],
+        flops=JP,
+    )
     for turn in range(groups):
-        *filtered, last = call(
-            functools.partial(filter_kernel, turn),
+        middle = 0 < turn < groups - 1
+        if middle:
+            (last,) = call(
+                functools.partial(jump_kernel, turn), (start, *joined, offset), [((share, states), F32)], flops=JJ
+            )
+            there = hop(last, turn, turn + 1)
+        filtered = call(
+            functools.partial(filter_kernel, turn, middle),
             (start, coef, high, low, obs, *filtered),
-            [((GROUP, share, states), F32)] + [((share, states), F32)] * (GROUP + 1),
+            [((GROUP, share, states), F32)] + [((share, states), F32)] * (GROUP + 1 - middle),
             aliases={5 + i: i for i in range(len(filtered))},
             flops=FW[min(turn,3)],
         )
+        if not middle:
+            *filtered, last = filtered
+        if turn == 0:
+            there = hop(last, 0, 1)
         if turn < groups - 1:
-            start = hop(last, turn, turn + 1)
+            start = there
         if turn == groups - 3:
             turned_gain, gain_x, gain_y = gate((turned_gain, gain_x, gain_y), last, G1)
             (gain_d,) = call(choose_kernel, (gain_x, gain_y), [((states, panel), F32)], flops=G1)
@@ -404,16 +450,22 @@
             gain_near = list(gate((turned_gain, gain_x, gain_y), start, G2))
             gain_far = [neighbour(value) for value in gain_near]
         if turn == groups - 2:
-            (gain_d,) = gate((gain_d,), gain_far[2], G3)
-            gain_near.append(gain_d)
-            gain_far.append(neighbour(gain_d))
+            parts = call(
+                functools.partial(gather_kernel, range(GROUP - 1), 0, states),
+                (*gain_near, *gain_far),
+                [((GROUP, rows, states, panel), BF16)] * 2,
+                flops=GA,
+            )
+            (gain_d,) = gate((gain_d,), parts[0], G3)
+            high_back, low_back = call(
+                functools.partial(gather_kernel, (GROUP - 1,), 0, states),
+                (gain_d, neighbour(gain_d), *parts),
+                [((GROUP, rows, states, panel), BF16)] * 2,
+                aliases={2: 0, 3: 1},
+            )
     filtered, sent = filtered[0], filtered[1:]
 
-    high, low = call(
-        functools.partial(gather_kernel, 0, states),
-        (*gain_near, *gain_far),
-        [((GROUP, rows, states, panel), BF16)] * 2,
-    )
+    high, low = high_back, low_back
     start, packed = last, ()
     *joined, offset = call(
         functools.partial(joined_kernel, groups),
@@ -425,7 +477,7 @@
         middle = 0 < turn < groups - 1
         if middle:
             (first,) = call(
-                functools.partial(jump_kernel, turn, groups), (start, *joined, offset), [((share, states), F32)]
+                functools.partial(jump_kernel, groups - 1 - turn), (start, *joined, offset), [((share, states), F32)]
             )
             here = hop(first, groups - 1 - turn, groups - 2 - turn)
         packed = call(
@@ -444,7 +496,17 @@
         if turn < groups - 1:
             start = here
     near = (*sent, packed[0], *send_home(packed))
-    (far,) = call(across_kernel, near, [((2 * GROUP, share, panel), F32)])
+    early = (*range(GROUP + 1), 2 * GROUP - 1)
+    late = [slot for slot in range(2 * GROUP) if slot not in early]
+    far_shape = [((2 * GROUP, share, panel), F32)]
+    far = call(functools.partial(across_kernel, early), [near[slot] for slot in early], far_shape)
+    (far,) = call(
+        functools.partial(across_kernel, late),
+        (*[near[slot] for slot in late], *far),
+        far_shape,
+        aliases={len(late): 0},
+        flops=AF,
+    )
     filt, smooth = call(
         functools.partial(home_kernel, share),
         (*near, neighbour(far)),

time: 75.9 us -> 74.4 us (0.980)
  waiting for transfers between devices: 41.9 us -> 40.5 us
    ppermute x21, waiting for transfers between devices: 27.4 us -> 25.9 us  [swap(): return lax.ppermute(value, both, pairs)]
    pallas_call x23 -> x28, Pallas kernels: 6.5 us -> 6.49 us  [call(): pl.pallas_call(kernel, out_shape=[jax.ShapeDtypeStruct(shape, dtype) for...]
  transfers between devices with their start and end apart: 27 -> 27, of which waited for: 14 -> 17; matrix products, arithmetic and copies ran while one was open for 0% -> 0% of each run, Pallas kernels for 4% -> 5%
where the time goes in v4:
time: 74.4 us; the launch traced here: 74.2 us
  waiting for transfers between devices  40.5 us (54%)
  starting transfers between devices  25.3 us (34%)
  Pallas kernels  6.49 us (9%)
  local copies, waits for them, and re-layouts  1.05 us (1%)
  between operations  0.89 us (1%)
    ppermute x21, waiting for transfers between devices, swap(): return lax.ppermute(value, both, pairs)  25.9 us
    ppermute x21, starting transfers between devices, swap(): return lax.ppermute(value, both, pairs)  18.3 us
    ppermute x6, waiting for transfers between devices, hop(): return lax.ppermute(value, both, pairs)  14.6 us
    ppermute x6, starting transfers between devices, hop(): return lax.ppermute(value, both, pairs)  7 us
    pallas_call x28, Pallas kernels, call(): pl.pallas_call(kernel, out_shape=[jax.ShapeDtypeStruct(shape, dtype) for...  6.49 us
  transfers between devices with their start and end apart: 27, of which 17 were waited for; matrix products, arithmetic and copies ran while one was open for 0% of the time, Pallas kernels for 5%

profile of v4, /device:TPU:0, one launch (start us, length us, event | category | flops | bytes accessed | tf_op | source)
XLA Modules:
  0.0 74.2 jit_solution(13041381944770083180)
XLA Ops:
  0.6 1.4 %shard_map.77 = (f32[304,256]{1,0:T(8,128)S(1)}, f32[304,256]{1,0:T(8,128)S(1)}, f32[304,256]{1,0:T(8,128)S(1)}, f32[48,256]{1,0:T(8,128)S(1)}, f32[8,256]{1,0:T(8,128)S(1)}) custom-call(f32[1,256]{1,0:T(1,128)} %bitcast.9, s32[1,256]{1,0:T(1,128)} %mask_hbm.1, f32[256,256]{1,0:T(8,128)} %bitcast.8, f32[256,384]{1,0:T(8,128)} %bitcast.7), custom_call_target="tpu_custom_call" | custom-call | bytes 2097152 | tf_op jit(solution)/shard_map/pallas_call | solution.py:29
  2.6 2.6 %collective-permute-start.1 = (f32[304,256]{1,0:T(8,128)S(1)}, f32[304,256]{1,0:T(8,128)S(1)}, u32[]{:S(2)}, u32[]{:S(2)}) collective-permute-start(f32[304,256]{1,0:T(8,128)S(1)} %get-tuple-element.80), channel_id=1, source_target_pairs={{0,4},{1,5},{2,6},{3,7},{4,0},{5,1},{6,2},{7,3},{8,12},{9,13},{10,... | collective-permute-start | bytes 933896 | tf_op jit(solution)/shard_map/ppermute | solution.py:358
  5.2 1.4 %collective-permute-start.2 = (f32[304,256]{1,0:T(8,128)S(1)}, f32[304,256]{1,0:T(8,128)S(1)}, u32[]{:S(2)}, u32[]{:S(2)}) collective-permute-start(f32[304,256]{1,0:T(8,128)S(1)} %get-tuple-element.81), channel_id=1, source_target_pairs={{0,6},{1,7},{2,4},{3,5},{4,2},{5,3},{6,0},{7,1},{8,14},{9,15},{10,... | collective-permute-start | bytes 933896 | tf_op jit(solution)/shard_map/ppermute | solution.py:358
  6.7 1.0 %copy-done.1 = f32[1,256,512]{2,1,0:T(8,128)S(1)} copy-done((f32[1,256,512]{2,1,0:T(8,128)S(1)}, f32[1,256,512]{2,1,0:T(8,128)}, u32[]{:S(2)}) %copy-start.1) | copy-done | bytes 524312
  8.0 2.0 %collective-permute-start.11 = (f32[512,256]{1,0:T(8,128)S(1)}, f32[512,256]{1,0:T(8,128)S(1)}, u32[]{:S(2)}, u32[]{:S(2)}) collective-permute-start(f32[512,256]{1,0:T(8,128)S(1)} %shard_map.79.refs_0_), channel_id=1, source_target_pairs={{0,4},{1,5},{2,6},{3,7},{4,0},{5,1},{6,2},{7,3},{8,12},{9,13},{10,... | collective-permute-start | bytes 1572872 | tf_op jit(solution)/shard_map/ppermute | solution.py:358
  10.0 1.5 %collective-permute-start.10 = (f32[512,256]{1,0:T(8,128)S(1)}, f32[512,256]{1,0:T(8,128)S(1)}, u32[]{:S(2)}, u32[]{:S(2)}) collective-permute-start(f32[512,256]{1,0:T(8,128)S(1)} %shard_map.79.refs_0_), channel_id=1, source_target_pairs={{0,2},{1,3},{2,0},{3,1},{4,6},{5,7},{6,4},{7,5},{8,10},{9,11},{10,... | collective-permute-start | bytes 1572872 | tf_op jit(solution)/shard_map/ppermute | solution.py:358
  11.8 8.2 %collective-permute-done.1.refs_2_ = f32[304,256]{1,0:T(8,128)S(1)} collective-permute-done((f32[304,256]{1,0:T(8,128)S(1)}, f32[304,256]{1,0:T(8,128)S(1)}, u32[]{:S(2)}, u32[]{:S(2)}) %collective-permute-start.1) | collective-permute-done | bytes 311328 | tf_op jit(solution)/shard_map/ppermute | solution.py:358
  20.1 1.5 %collective-permute-done.refs_1_ = f32[304,256]{1,0:T(8,128)S(1)} collective-permute-done((f32[304,256]{1,0:T(8,128)S(1)}, f32[304,256]{1,0:T(8,128)S(1)}, u32[]{:S(2)}, u32[]{:S(2)}) %collective-permute-start) | collective-permute-done | bytes 311328 | tf_op jit(solution)/shard_map/ppermute | solution.py:358
  22.1 1.1 %collective-permute-done.4.refs_5_ = f32[304,256]{1,0:T(8,128)S(1)} collective-permute-done((f32[304,256]{1,0:T(8,128)S(1)}, f32[304,256]{1,0:T(8,128)S(1)}, u32[]{:S(2)}, u32[]{:S(2)}) %collective-permute-start.4) | collective-permute-done | bytes 311328 | tf_op jit(solution)/shard_map/ppermute | solution.py:358
  24.4 0.9 %shard_map.81 = (f32[4,48,512]{2,1,0:T(8,128)S(1)}, f32[48,512]{1,0:T(8,128)S(1)}, f32[48,512]{1,0:T(8,128)S(1)}, f32[48,512]{1,0:T(8,128)S(1)}, f32[48,512]{1,0:T(8,128)S(1)}, /*index=5*/f32[48,512]{1,0:T(8,128)S(1)}) custom-call(f32[48,512]{1,0:T(8,128)S(1)} %shard_map.78.start_ref, f32[8,256]{1,0:T(8,128)S(1)} %get-tuple-element.85.coef_ref, ...), custom_call_target="tpu_custom_call" | custom-call | bytes 2097152 | tf_op jit(solution)/shard_map/pallas_call | solution.py:29
  25.3 3.1 %collective-permute-start.7 = (f32[48,512]{1,0:T(8,128)S(1)}, f32[48,512]{1,0:T(8,128)S(1)}, u32[]{:S(2)}, u32[]{:S(2)}) collective-permute-start(f32[48,512]{1,0:T(8,128)S(1)} %get-tuple-element.94), channel_id=1, source_target_pairs={{0,8},{1,9},{2,10},{3,11},{4,12},{5,13},{6,14},{7,15}} | collective-permute-start | bytes 294920 | tf_op jit(solution)/shard_map/ppermute | solution.py:375
  28.4 2.3 %collective-permute-done.7.start_ref = f32[48,512]{1,0:T(8,128)S(1)} collective-permute-done((f32[48,512]{1,0:T(8,128)S(1)}, f32[48,512]{1,0:T(8,128)S(1)}, u32[]{:S(2)}, u32[]{:S(2)}) %collective-permute-start.7) | collective-permute-done | bytes 98336 | tf_op jit(solution)/shard_map/ppermute | solution.py:375
  31.4 0.9 %collective-permute-done.10.refs_1_ = f32[512,256]{1,0:T(8,128)S(1)} collective-permute-done((f32[512,256]{1,0:T(8,128)S(1)}, f32[512,256]{1,0:T(8,128)S(1)}, u32[]{:S(2)}, u32[]{:S(2)}) %collective-permute-start.10) | collective-permute-done | bytes 524320 | tf_op jit(solution)/shard_map/ppermute | solution.py:358
  32.4 1.8 %collective-permute-start.12 = (f32[512,256]{1,0:T(8,128)S(1)}, f32[512,256]{1,0:T(8,128)S(1)}, u32[]{:S(2)}, u32[]{:S(2)}) collective-permute-start(f32[512,256]{1,0:T(8,128)S(1)} %shard_map.89), channel_id=1, source_target_pairs={{0,4},{1,3},{2,6},{3,1},{4,0},{5,7},{6,2},{7,5},{8,12},{9,11},{10,... | collective-permute-start | bytes 1572872 | tf_op jit(solution)/shard_map/ppermute | solution.py:358
  34.1 0.7 collective-permute-start.9
  35.5 1.3 %collective-permute-done.13.refs_3_ = f32[512,256]{1,0:T(8,128)S(1)} collective-permute-done((f32[512,256]{1,0:T(8,128)S(1)}, f32[512,256]{1,0:T(8,128)S(1)}, u32[]{:S(2)}, u32[]{:S(2)}) %collective-permute-start.13) | collective-permute-done | bytes 524320 | tf_op jit(solution)/shard_map/ppermute | solution.py:358
  36.8 0.7 %collective-permute-done.14.refs_4_ = f32[512,256]{1,0:T(8,128)S(1)} collective-permute-done((f32[512,256]{1,0:T(8,128)S(1)}, f32[512,256]{1,0:T(8,128)S(1)}, u32[]{:S(2)}, u32[]{:S(2)}) %collective-permute-start.14) | collective-permute-done | bytes 524320 | tf_op jit(solution)/shard_map/ppermute | solution.py:358
  37.5 0.7 %collective-permute-done.15.refs_5_ = f32[512,256]{1,0:T(8,128)S(1)} collective-permute-done((f32[512,256]{1,0:T(8,128)S(1)}, f32[512,256]{1,0:T(8,128)S(1)}, u32[]{:S(2)}, u32[]{:S(2)}) %collective-permute-start.15) | collective-permute-done | bytes 524320 | tf_op jit(solution)/shard_map/ppermute | solution.py:358
  38.9 2.7 %collective-permute-done.12.refs_0_ = f32[512,256]{1,0:T(8,128)S(1)} collective-permute-done((f32[512,256]{1,0:T(8,128)S(1)}, f32[512,256]{1,0:T(8,128)S(1)}, u32[]{:S(2)}, u32[]{:S(2)}) %collective-permute-start.12) | collective-permute-done | bytes 524320 | tf_op jit(solution)/shard_map/ppermute | solution.py:358
  41.6 1.9 %collective-permute-done.16.refs_1_ = f32[512,256]{1,0:T(8,128)S(1)} collective-permute-done((f32[512,256]{1,0:T(8,128)S(1)}, f32[512,256]{1,0:T(8,128)S(1)}, u32[]{:S(2)}, u32[]{:S(2)}) %collective-permute-start.16) | collective-permute-done | bytes 524320 | tf_op jit(solution)/shard_map/ppermute | solution.py:358
  43.7 0.7 collective-permute-start.17
  44.5 0.7 collective-permute-start.18
  45.2 1.3 %collective-permute-start.22 = (f32[48,512]{1,0:T(8,128)S(1)}, f32[48,512]{1,0:T(8,128)S(1)}, u32[]{:S(2)}, u32[]{:S(2)}) collective-permute-start(f32[48,512]{1,0:T(8,128)S(1)} %shard_map.97.refs_4_), channel_id=1, source_target_pairs={{8,0},{9,1},{10,2},{11,3},{12,4},{13,5},{14,6},{15,7}} | collective-permute-start | bytes 294920 | tf_op jit(solution)/shard_map/ppermute | solution.py:375
  46.5 1.8 %collective-permute-start.19 = (f32[48,512]{1,0:T(8,128)S(1)}, f32[48,512]{1,0:T(8,128)S(1)}, u32[]{:S(2)}, u32[]{:S(2)}) collective-permute-start(f32[48,512]{1,0:T(8,128)S(1)} %get-tuple-element.135), channel_id=1, source_target_pairs={{0,2},{1,3},{2,0},{3,1},{4,6},{5,7},{6,4},{7,5},{8,10},{9,11},{10,... | collective-permute-start | bytes 294920 | tf_op jit(solution)/shard_map/ppermute | solution.py:358
  48.3 1.5 %collective-permute-start.20 = (f32[48,512]{1,0:T(8,128)S(1)}, f32[48,512]{1,0:T(8,128)S(1)}, u32[]{:S(2)}, u32[]{:S(2)}) collective-permute-start(f32[48,512]{1,0:T(8,128)S(1)} %get-tuple-element.136), channel_id=1, source_target_pairs={{0,4},{1,5},{2,6},{3,7},{4,0},{5,1},{6,2},{7,3},{8,12},{9,13},{10,... | collective-permute-start | bytes 294920 | tf_op jit(solution)/shard_map/ppermute | solution.py:358
  50.1 12.3 %collective-permute-done.22.start_ref = f32[48,512]{1,0:T(8,128)S(1)} collective-permute-done((f32[48,512]{1,0:T(8,128)S(1)}, f32[48,512]{1,0:T(8,128)S(1)}, u32[]{:S(2)}, u32[]{:S(2)}) %collective-permute-start.22) | collective-permute-done | bytes 98336 | tf_op jit(solution)/shard_map/ppermute | solution.py:375
  62.4 1.2 %shard_map.101 = (f32[48,512]{1,0:T(8,128)S(1)}, f32[48,512]{1,0:T(8,128)S(1)}, f32[48,512]{1,0:T(8,128)S(1)}, f32[48,512]{1,0:T(8,128)S(1)}) custom-call(f32[48,512]{1,0:T(8,128)S(1)} %collective-permute-done.22.start_ref, f32[8,256]{1,0:T(8,128)S(1)} %get-tuple-element.85.coef_ref, ...), custom_call_target="tpu_custom_call", output_to_operand_aliasing={{0}: (5, {}), {1}: (6, {}), {2}: (7, {}), {3}: (8, {})} | custom-call | bytes 2097152 | tf_op jit(solution)/shard_map/pallas_call | solution.py:29
  63.6 2.5 %collective-permute-start.25 = (f32[48,512]{1,0:T(8,128)S(1)}, f32[48,512]{1,0:T(8,128)S(1)}, u32[]{:S(2)}, u32[]{:S(2)}) collective-permute-start(f32[48,512]{1,0:T(8,128)S(1)} %get-tuple-element.153), channel_id=1, source_target_pairs={{0,6},{1,7},{2,4},{3,5},{4,2},{5,3},{6,0},{7,1},{8,14},{9,15},{10,... | collective-permute-start | bytes 294920 | tf_op jit(solution)/shard_map/ppermute | solution.py:358
  67.1 2.0 %collective-permute-done.25.refs_5_.refs_7_ = f32[48,512]{1,0:T(8,128)S(1)} collective-permute-done((f32[48,512]{1,0:T(8,128)S(1)}, f32[48,512]{1,0:T(8,128)S(1)}, u32[]{:S(2)}, u32[]{:S(2)}) %collective-permute-start.25) | collective-permute-done | bytes 98336 | tf_op jit(solution)/shard_map/ppermute | solution.py:358
  69.2 1.5 %collective-permute-done.23.refs_0_.refs_5_ = f32[48,512]{1,0:T(8,128)S(1)} collective-permute-done((f32[48,512]{1,0:T(8,128)S(1)}, f32[48,512]{1,0:T(8,128)S(1)}, u32[]{:S(2)}, u32[]{:S(2)}) %collective-permute-start.23) | collective-permute-done | bytes 98336 | tf_op jit(solution)/shard_map/ppermute | solution.py:358
  71.3 1.7 %collective-permute-done.26.refs_8_ = f32[8,48,256]{2,1,0:T(8,128)S(1)} collective-permute-done((f32[8,48,256]{2,1,0:T(8,128)S(1)}, f32[8,48,256]{2,1,0:T(8,128)S(1)}, u32[]{:S(2)}, u32[]{:S(2)}) %collective-permute-start.26) | collective-permute-done | bytes 393248 | tf_op jit(solution)/shard_map/ppermute | solution.py:358
  73.0 1.1 %shard_map.104 = (f32[256,384]{1,0:T(8,128)}, f32[256,384]{1,0:T(8,128)}) custom-call(f32[48,512]{1,0:T(8,128)S(1)} %get-tuple-element.134.refs_0_, f32[48,512]{1,0:T(8,128)S(1)} %collective-permute-done.19.refs_1_, f32[48,512]{1,0:T(8,128)S(1)} %collective-permute-done.20.refs_2_, f32[48,512]{1,0:T(8,128)S(1)} %collective-permute-done.21.refs_3_, ...), custom_call_target="tpu_custom_call" | custom-call | bytes 2097152 | tf_op jit(solution)/shard_map/pallas_call | solution.py:29
  (54 shorter events, 7.2 us)
Async XLA Ops:
  0.6 10.9 %copy-start = (f32[512,384]{1,0:T(8,128)S(1)}, f32[512,384]{1,0:T(8,128)}, u32[]{:S(2)}) copy-start(f32[512,384]{1,0:T(8,128)} %prior_ref.1) | copy-start | bytes 2359300
  2.1 8.0 %collective-permute-start.3 = (f32[304,256]{1,0:T(8,128)S(1)}, f32[304,256]{1,0:T(8,128)S(1)}, u32[]{:S(2)}, u32[]{:S(2)}) collective-permute-start(f32[304,256]{1,0:T(8,128)S(1)} %get-tuple-element.79.refs_0_), channel_id=1, source_target_pairs={{0,1},{1,0},{2,3},{3,2},{4,5},{5,4},{6,7},{7,6},{8,9},{9,8},{10,11... | collective-permute-start | bytes 933896 | tf_op jit(solution)/shard_map/ppermute | solution.py:358
  2.6 17.5 %collective-permute-start.1 = (f32[304,256]{1,0:T(8,128)S(1)}, f32[304,256]{1,0:T(8,128)S(1)}, u32[]{:S(2)}, u32[]{:S(2)}) collective-permute-start(f32[304,256]{1,0:T(8,128)S(1)} %get-tuple-element.80), channel_id=1, source_target_pairs={{0,4},{1,5},{2,6},{3,7},{4,0},{5,1},{6,2},{7,3},{8,12},{9,13},{10,... | collective-permute-start | bytes 933896 | tf_op jit(solution)/shard_map/ppermute | solution.py:358
  5.2 14.9 %collective-permute-start.2 = (f32[304,256]{1,0:T(8,128)S(1)}, f32[304,256]{1,0:T(8,128)S(1)}, u32[]{:S(2)}, u32[]{:S(2)}) collective-permute-start(f32[304,256]{1,0:T(8,128)S(1)} %get-tuple-element.81), channel_id=1, source_target_pairs={{0,6},{1,7},{2,4},{3,5},{4,2},{5,3},{6,0},{7,1},{8,14},{9,15},{10,... | collective-permute-start | bytes 933896 | tf_op jit(solution)/shard_map/ppermute | solution.py:358
  6.6 15.0 %collective-permute-start = (f32[304,256]{1,0:T(8,128)S(1)}, f32[304,256]{1,0:T(8,128)S(1)}, u32[]{:S(2)}, u32[]{:S(2)}) collective-permute-start(f32[304,256]{1,0:T(8,128)S(1)} %get-tuple-element.79.refs_0_), channel_id=1, source_target_pairs={{0,2},{1,3},{2,0},{3,1},{4,6},{5,7},{6,4},{7,5},{8,10},{9,11},{10,... | collective-permute-start | bytes 933896 | tf_op jit(solution)/shard_map/ppermute | solution.py:358
  6.7 1.0 %copy-start.1 = (f32[1,256,512]{2,1,0:T(8,128)S(1)}, f32[1,256,512]{2,1,0:T(8,128)}, u32[]{:S(2)}) copy-start(f32[1,256,512]{2,1,0:T(8,128)} %param.11) | copy-start | bytes 1572868
  8.0 23.4 %collective-permute-start.11 = (f32[512,256]{1,0:T(8,128)S(1)}, f32[512,256]{1,0:T(8,128)S(1)}, u32[]{:S(2)}, u32[]{:S(2)}) collective-permute-start(f32[512,256]{1,0:T(8,128)S(1)} %shard_map.79.refs_0_), channel_id=1, source_target_pairs={{0,4},{1,5},{2,6},{3,7},{4,0},{5,1},{6,2},{7,3},{8,12},{9,13},{10,... | collective-permute-start | bytes 1572872 | tf_op jit(solution)/shard_map/ppermute | solution.py:358
  10.0 22.3 %collective-permute-start.10 = (f32[512,256]{1,0:T(8,128)S(1)}, f32[512,256]{1,0:T(8,128)S(1)}, u32[]{:S(2)}, u32[]{:S(2)}) collective-permute-start(f32[512,256]{1,0:T(8,128)S(1)} %shard_map.79.refs_0_), channel_id=1, source_target_pairs={{0,2},{1,3},{2,0},{3,1},{4,6},{5,7},{6,4},{7,5},{8,10},{9,11},{10,... | collective-permute-start | bytes 1572872 | tf_op jit(solution)/shard_map/ppermute | solution.py:358
  21.6 1.6 %collective-permute-start.4 = (f32[304,256]{1,0:T(8,128)S(1)}, f32[304,256]{1,0:T(8,128)S(1)}, u32[]{:S(2)}, u32[]{:S(2)}) collective-permute-start(f32[304,256]{1,0:T(8,128)S(1)} %collective-permute-done.refs_1_), channel_id=1, source_target_pairs={{0,1},{1,0},{2,3},{3,2},{4,5},{5,4},{6,7},{7,6},{8,9},{9,8},{10,11... | collective-permute-start | bytes 933896 | tf_op jit(solution)/shard_map/ppermute | solution.py:358
  21.6 2.0 %collective-permute-start.5 = (f32[304,256]{1,0:T(8,128)S(1)}, f32[304,256]{1,0:T(8,128)S(1)}, u32[]{:S(2)}, u32[]{:S(2)}) collective-permute-start(f32[304,256]{1,0:T(8,128)S(1)} %collective-permute-done.1.refs_2_), channel_id=1, source_target_pairs={{0,1},{1,0},{2,3},{3,2},{4,5},{5,4},{6,7},{7,6},{8,9},{9,8},{10,11... | collective-permute-start | bytes 933896 | tf_op jit(solution)/shard_map/ppermute | solution.py:358
  22.1 2.0 %collective-permute-start.6 = (f32[304,256]{1,0:T(8,128)S(1)}, f32[304,256]{1,0:T(8,128)S(1)}, u32[]{:S(2)}, u32[]{:S(2)}) collective-permute-start(f32[304,256]{1,0:T(8,128)S(1)} %collective-permute-done.2.refs_3_), channel_id=1, source_target_pairs={{0,1},{1,0},{2,3},{3,2},{4,5},{5,4},{6,7},{7,6},{8,9},{9,8},{10,11... | collective-permute-start | bytes 933896 | tf_op jit(solution)/shard_map/ppermute | solution.py:358
  25.3 5.4 %collective-permute-start.7 = (f32[48,512]{1,0:T(8,128)S(1)}, f32[48,512]{1,0:T(8,128)S(1)}, u32[]{:S(2)}, u32[]{:S(2)}) collective-permute-start(f32[48,512]{1,0:T(8,128)S(1)} %get-tuple-element.94), channel_id=1, source_target_pairs={{0,8},{1,9},{2,10},{3,11},{4,12},{5,13},{6,14},{7,15}} | collective-permute-start | bytes 294920 | tf_op jit(solution)/shard_map/ppermute | solution.py:375
  30.7 3.4 %collective-permute-start.8 = (f32[48,512]{1,0:T(8,128)S(1)}, f32[48,512]{1,0:T(8,128)S(1)}, u32[]{:S(2)}, u32[]{:S(2)}) collective-permute-start(f32[48,512]{1,0:T(8,128)S(1)} %shard_map.83.refs_3_), channel_id=1, source_target_pairs={{8,16},{9,17},{10,18},{11,19},{12,20},{13,21},{14,22},{15,23}} | collective-permute-start | bytes 294920 | tf_op jit(solution)/shard_map/ppermute | solution.py:375
  32.4 9.2 %collective-permute-start.12 = (f32[512,256]{1,0:T(8,128)S(1)}, f32[512,256]{1,0:T(8,128)S(1)}, u32[]{:S(2)}, u32[]{:S(2)}) collective-permute-start(f32[512,256]{1,0:T(8,128)S(1)} %shard_map.89), channel_id=1, source_target_pairs={{0,4},{1,3},{2,6},{3,1},{4,0},{5,7},{6,2},{7,5},{8,12},{9,11},{10,... | collective-permute-start | bytes 1572872 | tf_op jit(solution)/shard_map/ppermute | solution.py:358
  34.1 7.5 %collective-permute-start.9 = (f32[48,512]{1,0:T(8,128)S(1)}, f32[48,512]{1,0:T(8,128)S(1)}, u32[]{:S(2)}, u32[]{:S(2)}) collective-permute-start(f32[48,512]{1,0:T(8,128)S(1)} %shard_map.84), channel_id=1, source_target_pairs={{16,24},{17,25},{18,26},{19,27},{20,28},{21,29},{22,30},{23,31}} | collective-permute-start | bytes 294920 | tf_op jit(solution)/shard_map/ppermute | solution.py:375
  34.8 2.0 %collective-permute-start.13 = (f32[512,256]{1,0:T(8,128)S(1)}, f32[512,256]{1,0:T(8,128)S(1)}, u32[]{:S(2)}, u32[]{:S(2)}) collective-permute-start(f32[512,256]{1,0:T(8,128)S(1)} %get-tuple-element.122.refs_0_), channel_id=1, source_target_pairs={{0,1},{1,0},{2,3},{3,2},{4,5},{5,4},{6,7},{7,6},{8,9},{9,8},{10,11... | collective-permute-start | bytes 1572872 | tf_op jit(solution)/shard_map/ppermute | solution.py:358
  34.9 2.6 %collective-permute-start.14 = (f32[512,256]{1,0:T(8,128)S(1)}, f32[512,256]{1,0:T(8,128)S(1)}, u32[]{:S(2)}, u32[]{:S(2)}) collective-permute-start(f32[512,256]{1,0:T(8,128)S(1)} %get-tuple-element.123.refs_1_), channel_id=1, source_target_pairs={{0,1},{1,0},{2,3},{3,2},{4,5},{5,4},{6,7},{7,6},{8,9},{9,8},{10,11... | collective-permute-start | bytes 1572872 | tf_op jit(solution)/shard_map/ppermute | solution.py:358
  35.4 2.9 %collective-permute-start.15 = (f32[512,256]{1,0:T(8,128)S(1)}, f32[512,256]{1,0:T(8,128)S(1)}, u32[]{:S(2)}, u32[]{:S(2)}) collective-permute-start(f32[512,256]{1,0:T(8,128)S(1)} %get-tuple-element.124.refs_2_), channel_id=1, source_target_pairs={{0,1},{1,0},{2,3},{3,2},{4,5},{5,4},{6,7},{7,6},{8,9},{9,8},{10,11... | collective-permute-start | bytes 1572872 | tf_op jit(solution)/shard_map/ppermute | solution.py:358
  41.6 1.9 %collective-permute-start.16 = (f32[512,256]{1,0:T(8,128)S(1)}, f32[512,256]{1,0:T(8,128)S(1)}, u32[]{:S(2)}, u32[]{:S(2)}) collective-permute-start(f32[512,256]{1,0:T(8,128)S(1)} %shard_map.92.refs_0_), channel_id=1, source_target_pairs={{0,1},{1,0},{2,3},{3,2},{4,5},{5,4},{6,7},{7,6},{8,9},{9,8},{10,11... | collective-permute-start | bytes 1572872 | tf_op jit(solution)/shard_map/ppermute | solution.py:358
  43.7 0.7 collective-permute-start.17
  44.5 0.7 collective-permute-start.18
  45.2 17.1 %collective-permute-start.22 = (f32[48,512]{1,0:T(8,128)S(1)}, f32[48,512]{1,0:T(8,128)S(1)}, u32[]{:S(2)}, u32[]{:S(2)}) collective-permute-start(f32[48,512]{1,0:T(8,128)S(1)} %shard_map.97.refs_4_), channel_id=1, source_target_pairs={{8,0},{9,1},{10,2},{11,3},{12,4},{13,5},{14,6},{15,7}} | collective-permute-start | bytes 294920 | tf_op jit(solution)/shard_map/ppermute | solution.py:375
  46.5 20.1 %collective-permute-start.19 = (f32[48,512]{1,0:T(8,128)S(1)}, f32[48,512]{1,0:T(8,128)S(1)}, u32[]{:S(2)}, u32[]{:S(2)}) collective-permute-start(f32[48,512]{1,0:T(8,128)S(1)} %get-tuple-element.135), channel_id=1, source_target_pairs={{0,2},{1,3},{2,0},{3,1},{4,6},{5,7},{6,4},{7,5},{8,10},{9,11},{10,... | collective-permute-start | bytes 294920 | tf_op jit(solution)/shard_map/ppermute | solution.py:358
  48.3 18.8 %collective-permute-start.20 = (f32[48,512]{1,0:T(8,128)S(1)}, f32[48,512]{1,0:T(8,128)S(1)}, u32[]{:S(2)}, u32[]{:S(2)}) collective-permute-start(f32[48,512]{1,0:T(8,128)S(1)} %get-tuple-element.136), channel_id=1, source_target_pairs={{0,4},{1,5},{2,6},{3,7},{4,0},{5,1},{6,2},{7,3},{8,12},{9,13},{10,... | collective-permute-start | bytes 294920 | tf_op jit(solution)/shard_map/ppermute | solution.py:358
  49.8 17.3 %collective-permute-start.21 = (f32[48,512]{1,0:T(8,128)S(1)}, f32[48,512]{1,0:T(8,128)S(1)}, u32[]{:S(2)}, u32[]{:S(2)}) collective-permute-start(f32[48,512]{1,0:T(8,128)S(1)} %get-tuple-element.137), channel_id=1, source_target_pairs={{0,6},{1,7},{2,4},{3,5},{4,2},{5,3},{6,0},{7,1},{8,14},{9,15},{10,... | collective-permute-start | bytes 294920 | tf_op jit(solution)/shard_map/ppermute | solution.py:358
  63.6 5.6 %collective-permute-start.25 = (f32[48,512]{1,0:T(8,128)S(1)}, f32[48,512]{1,0:T(8,128)S(1)}, u32[]{:S(2)}, u32[]{:S(2)}) collective-permute-start(f32[48,512]{1,0:T(8,128)S(1)} %get-tuple-element.153), channel_id=1, source_target_pairs={{0,6},{1,7},{2,4},{3,5},{4,2},{5,3},{6,0},{7,1},{8,14},{9,15},{10,... | collective-permute-start | bytes 294920 | tf_op jit(solution)/shard_map/ppermute | solution.py:358
  66.1 4.6 %collective-permute-start.23 = (f32[48,512]{1,0:T(8,128)S(1)}, f32[48,512]{1,0:T(8,128)S(1)}, u32[]{:S(2)}, u32[]{:S(2)}) collective-permute-start(f32[48,512]{1,0:T(8,128)S(1)} %get-tuple-element.151), channel_id=1, source_target_pairs={{0,2},{1,3},{2,0},{3,1},{4,6},{5,7},{6,4},{7,5},{8,10},{9,11},{10,... | collective-permute-start | bytes 294920 | tf_op jit(solution)/shard_map/ppermute | solution.py:358
  66.6 4.6 %collective-permute-start.24 = (f32[48,512]{1,0:T(8,128)S(1)}, f32[48,512]{1,0:T(8,128)S(1)}, u32[]{:S(2)}, u32[]{:S(2)}) collective-permute-start(f32[48,512]{1,0:T(8,128)S(1)} %get-tuple-element.152), channel_id=1, source_target_pairs={{0,4},{1,5},{2,6},{3,7},{4,0},{5,1},{6,2},{7,3},{8,12},{9,13},{10,... | collective-permute-start | bytes 294920 | tf_op jit(solution)/shard_map/ppermute | solution.py:358
  71.2 1.8 %collective-permute-start.26 = (f32[8,48,256]{2,1,0:T(8,128)S(1)}, f32[8,48,256]{2,1,0:T(8,128)S(1)}, u32[]{:S(2)}, u32[]{:S(2)}) collective-permute-start(f32[8,48,256]{2,1,0:T(8,128)S(1)} %shard_map.103), channel_id=1, source_target_pairs={{0,1},{1,0},{2,3},{3,2},{4,5},{5,4},{6,7},{7,6},{8,9},{9,8},{10,11... | collective-permute-start | bytes 1179656 | tf_op jit(solution)/shard_map/ppermute | solution.py:358

commit v5 on v4

--- a/solution.py
+++ b/solution.py
@@ -314,7 +314,8 @@
 
 
 def home_kernel(share, *refs):
-    near, (far_ref, *outs, turned, tiles) = refs[: 2 * GROUP], refs[2 * GROUP :]
+    near, (*fars, filt_ref, smooth_ref, turned, tiles) = refs[: 2 * GROUP], refs[2 * GROUP :]
+    outs = (filt_ref, smooth_ref)
     _, spot, row = place()
     rows = lax.axis_size("rows")
     panel, paths = outs[0].shape
@@ -325,7 +326,7 @@
             at = kind * GROUP + flip
             start = jnp.bitwise_xor(spot, flip) * rows
             turned[kind, pl.ds(pl.multiple_of((start + row) * share, 8), share), :] = near[at][:, lanes]
-            turned[kind, pl.ds(pl.multiple_of((start + 1 - row) * share, 8), share), :] = far_ref[at]
+            turned[kind, pl.ds(pl.multiple_of((start + 1 - row) * share, 8), share), :] = fars[kind][flip]
         for at in range(paths // LANES):
             lines = slice(at * LANES, (at + 1) * LANES)
             for part in range(2):
@@ -495,21 +496,21 @@
             sent = [sent[0], *send_home(sent)]
         if turn < groups - 1:
             start = here
-    near = (*sent, packed[0], *send_home(packed))
-    early = (*range(GROUP + 1), 2 * GROUP - 1)
-    late = [slot for slot in range(2 * GROUP) if slot not in early]
-    far_shape = [((2 * GROUP, share, panel), F32)]
-    far = call(functools.partial(across_kernel, early), [near[slot] for slot in early], far_shape)
+    far_shape = [((GROUP, share, panel), F32)]
+    smooth_near = (packed[0], *send_home(packed))
+    (filt_far,) = call(functools.partial(across_kernel, range(GROUP)), sent, far_shape)
+    early = (0, GROUP - 1)
+    late = range(1, GROUP - 1)
+    far = call(functools.partial(across_kernel, early), [smooth_near[slot] for slot in early], far_shape)
     (far,) = call(
         functools.partial(across_kernel, late),
-        (*[near[slot] for slot in late], *far),
+        (*[smooth_near[slot] for slot in late], *far),
         far_shape,
         aliases={len(late): 0},
-        flops=AF,
     )
     filt, smooth = call(
         functools.partial(home_kernel, share),
-        (*near, neighbour(far)),
+        (*sent, *smooth_near, neighbour(filt_far), neighbour(far)),
         [((panel, paths), F32)] * 2,
         [pltpu.VMEM((2, paths, panel), F32), pltpu.VMEM((2, paths // LANES, panel, LANES), F32)],
     )

time: 74.4 us -> 74.1 us (level)
    ppermute x21 -> x22, waiting for transfers between devices: 25.9 us -> 25.5 us  [swap(): return lax.ppermute(value, both, pairs)]
    ppermute x21 -> x22, starting transfers between devices: 18.3 us -> 18.3 us  [swap(): return lax.ppermute(value, both, pairs)]
    pallas_call x28 -> x29, Pallas kernels: 6.49 us -> 6.48 us  [call(): pl.pallas_call(kernel, out_shape=[jax.ShapeDtypeStruct(shape, dtype) for...]
  transfers between devices with their start and end apart: 27 -> 28, of which waited for: 17 -> 17; matrix products, arithmetic and copies ran while one was open for 0% -> 0% of each run, Pallas kernels for 5% -> 5%
where the time goes in v5:
time: 74.1 us; the launch traced here: 73.9 us
  waiting for transfers between devices  40.1 us (54%)
  starting transfers between devices  25.4 us (34%)
  Pallas kernels  6.48 us (9%)
  local copies, waits for them, and re-layouts  1.05 us (1%)
  between operations  0.91 us (1%)
    ppermute x22, waiting for transfers between devices, swap(): return lax.ppermute(value, both, pairs)  25.5 us
    ppermute x22, starting transfers between devices, swap(): return lax.ppermute(value, both, pairs)  18.3 us
    ppermute x6, waiting for transfers between devices, hop(): return lax.ppermute(value, both, pairs)  14.6 us
    ppermute x6, starting transfers between devices, hop(): return lax.ppermute(value, both, pairs)  7 us
    pallas_call x29, Pallas kernels, call(): pl.pallas_call(kernel, out_shape=[jax.ShapeDtypeStruct(shape, dtype) for...  6.48 us
  transfers between devices with their start and end apart: 28, of which 17 were waited for; matrix products, arithmetic and copies ran while one was open for 0% of the time, Pallas kernels for 5%

profile of v5, /device:TPU:0, one launch (start us, length us, event | category | flops | bytes accessed | tf_op | source)
XLA Modules:
  0.0 73.9 jit_solution(4733984408873231643)
XLA Ops:
  0.6 1.4 %shard_map.77 = (f32[304,256]{1,0:T(8,128)S(1)}, f32[304,256]{1,0:T(8,128)S(1)}, f32[304,256]{1,0:T(8,128)S(1)}, f32[48,256]{1,0:T(8,128)S(1)}, f32[8,256]{1,0:T(8,128)S(1)}) custom-call(f32[1,256]{1,0:T(1,128)} %bitcast.9, s32[1,256]{1,0:T(1,128)} %mask_hbm.1, f32[256,256]{1,0:T(8,128)} %bitcast.8, f32[256,384]{1,0:T(8,128)} %bitcast.7), custom_call_target="tpu_custom_call" | custom-call | bytes 2097152 | tf_op jit(solution)/shard_map/pallas_call | solution.py:29
  2.6 2.6 %collective-permute-start.1 = (f32[304,256]{1,0:T(8,128)S(1)}, f32[304,256]{1,0:T(8,128)S(1)}, u32[]{:S(2)}, u32[]{:S(2)}) collective-permute-start(f32[304,256]{1,0:T(8,128)S(1)} %get-tuple-element.80), channel_id=1, source_target_pairs={{0,4},{1,5},{2,6},{3,7},{4,0},{5,1},{6,2},{7,3},{8,12},{9,13},{10,... | collective-permute-start | bytes 933896 | tf_op jit(solution)/shard_map/ppermute | solution.py:359
  5.2 1.4 %collective-permute-start.2 = (f32[304,256]{1,0:T(8,128)S(1)}, f32[304,256]{1,0:T(8,128)S(1)}, u32[]{:S(2)}, u32[]{:S(2)}) collective-permute-start(f32[304,256]{1,0:T(8,128)S(1)} %get-tuple-element.81), channel_id=1, source_target_pairs={{0,6},{1,7},{2,4},{3,5},{4,2},{5,3},{6,0},{7,1},{8,14},{9,15},{10,... | collective-permute-start | bytes 933896 | tf_op jit(solution)/shard_map/ppermute | solution.py:359
  6.7 1.0 %copy-done.1 = f32[1,256,512]{2,1,0:T(8,128)S(1)} copy-done((f32[1,256,512]{2,1,0:T(8,128)S(1)}, f32[1,256,512]{2,1,0:T(8,128)}, u32[]{:S(2)}) %copy-start.1) | copy-done | bytes 524312
  8.0 2.0 %collective-permute-start.11 = (f32[512,256]{1,0:T(8,128)S(1)}, f32[512,256]{1,0:T(8,128)S(1)}, u32[]{:S(2)}, u32[]{:S(2)}) collective-permute-start(f32[512,256]{1,0:T(8,128)S(1)} %shard_map.79.refs_0_), channel_id=1, source_target_pairs={{0,4},{1,5},{2,6},{3,7},{4,0},{5,1},{6,2},{7,3},{8,12},{9,13},{10,... | collective-permute-start | bytes 1572872 | tf_op jit(solution)/shard_map/ppermute | solution.py:359
  10.0 1.5 %collective-permute-start.10 = (f32[512,256]{1,0:T(8,128)S(1)}, f32[512,256]{1,0:T(8,128)S(1)}, u32[]{:S(2)}, u32[]{:S(2)}) collective-permute-start(f32[512,256]{1,0:T(8,128)S(1)} %shard_map.79.refs_0_), channel_id=1, source_target_pairs={{0,2},{1,3},{2,0},{3,1},{4,6},{5,7},{6,4},{7,5},{8,10},{9,11},{10,... | collective-permute-start | bytes 1572872 | tf_op jit(solution)/shard_map/ppermute | solution.py:359
  11.8 8.2 %collective-permute-done.1.refs_2_ = f32[304,256]{1,0:T(8,128)S(1)} collective-permute-done((f32[304,256]{1,0:T(8,128)S(1)}, f32[304,256]{1,0:T(8,128)S(1)}, u32[]{:S(2)}, u32[]{:S(2)}) %collective-permute-start.1) | collective-permute-done | bytes 311328 | tf_op jit(solution)/shard_map/ppermute | solution.py:359
  20.1 1.5 %collective-permute-done.refs_1_ = f32[304,256]{1,0:T(8,128)S(1)} collective-permute-done((f32[304,256]{1,0:T(8,128)S(1)}, f32[304,256]{1,0:T(8,128)S(1)}, u32[]{:S(2)}, u32[]{:S(2)}) %collective-permute-start) | collective-permute-done | bytes 311328 | tf_op jit(solution)/shard_map/ppermute | solution.py:359
  22.1 1.1 %collective-permute-done.4.refs_5_ = f32[304,256]{1,0:T(8,128)S(1)} collective-permute-done((f32[304,256]{1,0:T(8,128)S(1)}, f32[304,256]{1,0:T(8,128)S(1)}, u32[]{:S(2)}, u32[]{:S(2)}) %collective-permute-start.4) | collective-permute-done | bytes 311328 | tf_op jit(solution)/shard_map/ppermute | solution.py:359
  24.4 0.9 %shard_map.81 = (f32[4,48,512]{2,1,0:T(8,128)S(1)}, f32[48,512]{1,0:T(8,128)S(1)}, f32[48,512]{1,0:T(8,128)S(1)}, f32[48,512]{1,0:T(8,128)S(1)}, f32[48,512]{1,0:T(8,128)S(1)}, /*index=5*/f32[48,512]{1,0:T(8,128)S(1)}) custom-call(f32[48,512]{1,0:T(8,128)S(1)} %shard_map.78.start_ref, f32[8,256]{1,0:T(8,128)S(1)} %get-tuple-element.85.coef_ref, ...), custom_call_target="tpu_custom_call" | custom-call | bytes 2097152 | tf_op jit(solution)/shard_map/pallas_call | solution.py:29
  25.3 3.1 %collective-permute-start.7 = (f32[48,512]{1,0:T(8,128)S(1)}, f32[48,512]{1,0:T(8,128)S(1)}, u32[]{:S(2)}, u32[]{:S(2)}) collective-permute-start(f32[48,512]{1,0:T(8,128)S(1)} %get-tuple-element.94), channel_id=1, source_target_pairs={{0,8},{1,9},{2,10},{3,11},{4,12},{5,13},{6,14},{7,15}} | collective-permute-start | bytes 294920 | tf_op jit(solution)/shard_map/ppermute | solution.py:376
  28.4 2.3 %collective-permute-done.7.start_ref = f32[48,512]{1,0:T(8,128)S(1)} collective-permute-done((f32[48,512]{1,0:T(8,128)S(1)}, f32[48,512]{1,0:T(8,128)S(1)}, u32[]{:S(2)}, u32[]{:S(2)}) %collective-permute-start.7) | collective-permute-done | bytes 98336 | tf_op jit(solution)/shard_map/ppermute | solution.py:376
  31.4 0.9 %collective-permute-done.10.refs_1_ = f32[512,256]{1,0:T(8,128)S(1)} collective-permute-done((f32[512,256]{1,0:T(8,128)S(1)}, f32[512,256]{1,0:T(8,128)S(1)}, u32[]{:S(2)}, u32[]{:S(2)}) %collective-permute-start.10) | collective-permute-done | bytes 524320 | tf_op jit(solution)/shard_map/ppermute | solution.py:359
  32.4 1.8 %collective-permute-start.12 = (f32[512,256]{1,0:T(8,128)S(1)}, f32[512,256]{1,0:T(8,128)S(1)}, u32[]{:S(2)}, u32[]{:S(2)}) collective-permute-start(f32[512,256]{1,0:T(8,128)S(1)} %shard_map.89), channel_id=1, source_target_pairs={{0,4},{1,3},{2,6},{3,1},{4,0},{5,7},{6,2},{7,5},{8,12},{9,11},{10,... | collective-permute-start | bytes 1572872 | tf_op jit(solution)/shard_map/ppermute | solution.py:359
  34.1 0.7 collective-permute-start.9
  35.5 1.3 %collective-permute-done.13.refs_3_ = f32[512,256]{1,0:T(8,128)S(1)} collective-permute-done((f32[512,256]{1,0:T(8,128)S(1)}, f32[512,256]{1,0:T(8,128)S(1)}, u32[]{:S(2)}, u32[]{:S(2)}) %collective-permute-start.13) | collective-permute-done | bytes 524320 | tf_op jit(solution)/shard_map/ppermute | solution.py:359
  36.8 0.7 %collective-permute-done.14.refs_4_ = f32[512,256]{1,0:T(8,128)S(1)} collective-permute-done((f32[512,256]{1,0:T(8,128)S(1)}, f32[512,256]{1,0:T(8,128)S(1)}, u32[]{:S(2)}, u32[]{:S(2)}) %collective-permute-start.14) | collective-permute-done | bytes 524320 | tf_op jit(solution)/shard_map/ppermute | solution.py:359
  37.5 0.7 %collective-permute-done.15.refs_5_ = f32[512,256]{1,0:T(8,128)S(1)} collective-permute-done((f32[512,256]{1,0:T(8,128)S(1)}, f32[512,256]{1,0:T(8,128)S(1)}, u32[]{:S(2)}, u32[]{:S(2)}) %collective-permute-start.15) | collective-permute-done | bytes 524320 | tf_op jit(solution)/shard_map/ppermute | solution.py:359
  38.9 2.7 %collective-permute-done.12.refs_0_ = f32[512,256]{1,0:T(8,128)S(1)} collective-permute-done((f32[512,256]{1,0:T(8,128)S(1)}, f32[512,256]{1,0:T(8,128)S(1)}, u32[]{:S(2)}, u32[]{:S(2)}) %collective-permute-start.12) | collective-permute-done | bytes 524320 | tf_op jit(solution)/shard_map/ppermute | solution.py:359
  41.6 1.9 %collective-permute-done.16.refs_1_ = f32[512,256]{1,0:T(8,128)S(1)} collective-permute-done((f32[512,256]{1,0:T(8,128)S(1)}, f32[512,256]{1,0:T(8,128)S(1)}, u32[]{:S(2)}, u32[]{:S(2)}) %collective-permute-start.16) | collective-permute-done | bytes 524320 | tf_op jit(solution)/shard_map/ppermute | solution.py:359
  43.7 0.7 collective-permute-start.17
  44.5 0.7 collective-permute-start.18
  45.2 1.3 %collective-permute-start.22 = (f32[48,512]{1,0:T(8,128)S(1)}, f32[48,512]{1,0:T(8,128)S(1)}, u32[]{:S(2)}, u32[]{:S(2)}) collective-permute-start(f32[48,512]{1,0:T(8,128)S(1)} %shard_map.97.refs_4_), channel_id=1, source_target_pairs={{8,0},{9,1},{10,2},{11,3},{12,4},{13,5},{14,6},{15,7}} | collective-permute-start | bytes 294920 | tf_op jit(solution)/shard_map/ppermute | solution.py:376
  46.5 1.8 %collective-permute-start.19 = (f32[48,512]{1,0:T(8,128)S(1)}, f32[48,512]{1,0:T(8,128)S(1)}, u32[]{:S(2)}, u32[]{:S(2)}) collective-permute-start(f32[48,512]{1,0:T(8,128)S(1)} %get-tuple-element.135), channel_id=1, source_target_pairs={{0,2},{1,3},{2,0},{3,1},{4,6},{5,7},{6,4},{7,5},{8,10},{9,11},{10,... | collective-permute-start | bytes 294920 | tf_op jit(solution)/shard_map/ppermute | solution.py:359
  48.3 1.5 %collective-permute-start.20 = (f32[48,512]{1,0:T(8,128)S(1)}, f32[48,512]{1,0:T(8,128)S(1)}, u32[]{:S(2)}, u32[]{:S(2)}) collective-permute-start(f32[48,512]{1,0:T(8,128)S(1)} %get-tuple-element.136), channel_id=1, source_target_pairs={{0,4},{1,5},{2,6},{3,7},{4,0},{5,1},{6,2},{7,3},{8,12},{9,13},{10,... | collective-permute-start | bytes 294920 | tf_op jit(solution)/shard_map/ppermute | solution.py:359
  50.1 12.3 %collective-permute-done.22.start_ref = f32[48,512]{1,0:T(8,128)S(1)} collective-permute-done((f32[48,512]{1,0:T(8,128)S(1)}, f32[48,512]{1,0:T(8,128)S(1)}, u32[]{:S(2)}, u32[]{:S(2)}) %collective-permute-start.22) | collective-permute-done | bytes 98336 | tf_op jit(solution)/shard_map/ppermute | solution.py:376
  62.4 1.2 %shard_map.101 = (f32[48,512]{1,0:T(8,128)S(1)}, f32[48,512]{1,0:T(8,128)S(1)}, f32[48,512]{1,0:T(8,128)S(1)}, f32[48,512]{1,0:T(8,128)S(1)}) custom-call(f32[48,512]{1,0:T(8,128)S(1)} %collective-permute-done.22.start_ref, f32[8,256]{1,0:T(8,128)S(1)} %get-tuple-element.85.coef_ref, ...), custom_call_target="tpu_custom_call", output_to_operand_aliasing={{0}: (5, {}), {1}: (6, {}), {2}: (7, {}), {3}: (8, {})} | custom-call | bytes 2097152 | tf_op jit(solution)/shard_map/pallas_call | solution.py:29
  63.5 2.5 %collective-permute-start.25 = (f32[48,512]{1,0:T(8,128)S(1)}, f32[48,512]{1,0:T(8,128)S(1)}, u32[]{:S(2)}, u32[]{:S(2)}) collective-permute-start(f32[48,512]{1,0:T(8,128)S(1)} %get-tuple-element.153), channel_id=1, source_target_pairs={{0,6},{1,7},{2,4},{3,5},{4,2},{5,3},{6,0},{7,1},{8,14},{9,15},{10,... | collective-permute-start | bytes 294920 | tf_op jit(solution)/shard_map/ppermute | solution.py:359
  67.2 1.9 %collective-permute-done.25.refs_1_.refs_7_ = f32[48,512]{1,0:T(8,128)S(1)} collective-permute-done((f32[48,512]{1,0:T(8,128)S(1)}, f32[48,512]{1,0:T(8,128)S(1)}, u32[]{:S(2)}, u32[]{:S(2)}) %collective-permute-start.25) | collective-permute-done | bytes 98336 | tf_op jit(solution)/shard_map/ppermute | solution.py:359
  69.1 1.5 %collective-permute-done.23.refs_0_.refs_5_ = f32[48,512]{1,0:T(8,128)S(1)} collective-permute-done((f32[48,512]{1,0:T(8,128)S(1)}, f32[48,512]{1,0:T(8,128)S(1)}, u32[]{:S(2)}, u32[]{:S(2)}) %collective-permute-start.23) | collective-permute-done | bytes 98336 | tf_op jit(solution)/shard_map/ppermute | solution.py:359
  71.3 1.4 %collective-permute-done.27.refs_9_ = f32[4,48,256]{2,1,0:T(8,128)S(1)} collective-permute-done((f32[4,48,256]{2,1,0:T(8,128)S(1)}, f32[4,48,256]{2,1,0:T(8,128)S(1)}, u32[]{:S(2)}, u32[]{:S(2)}) %collective-permute-start.27) | collective-permute-done | bytes 196640 | tf_op jit(solution)/shard_map/ppermute | solution.py:359
  72.7 1.1 %shard_map.105 = (f32[256,384]{1,0:T(8,128)}, f32[256,384]{1,0:T(8,128)}) custom-call(f32[48,512]{1,0:T(8,128)S(1)} %get-tuple-element.134.refs_0_, f32[48,512]{1,0:T(8,128)S(1)} %collective-permute-done.19.refs_1_, f32[48,512]{1,0:T(8,128)S(1)} %collective-permute-done.20.refs_2_, f32[48,512]{1,0:T(8,128)S(1)} %collective-permute-done.21.refs_3_, ...), custom_call_target="tpu_custom_call" | custom-call | bytes 2097152 | tf_op jit(solution)/shard_map/pallas_call | solution.py:29
  (57 shorter events, 7.2 us)
Async XLA Ops:
  0.6 10.9 %copy-start = (f32[512,384]{1,0:T(8,128)S(1)}, f32[512,384]{1,0:T(8,128)}, u32[]{:S(2)}) copy-start(f32[512,384]{1,0:T(8,128)} %prior_ref.1) | copy-start | bytes 2359300
  2.1 8.0 %collective-permute-start.3 = (f32[304,256]{1,0:T(8,128)S(1)}, f32[304,256]{1,0:T(8,128)S(1)}, u32[]{:S(2)}, u32[]{:S(2)}) collective-permute-start(f32[304,256]{1,0:T(8,128)S(1)} %get-tuple-element.79.refs_0_), channel_id=1, source_target_pairs={{0,1},{1,0},{2,3},{3,2},{4,5},{5,4},{6,7},{7,6},{8,9},{9,8},{10,11... | collective-permute-start | bytes 933896 | tf_op jit(solution)/shard_map/ppermute | solution.py:359
  2.6 17.5 %collective-permute-start.1 = (f32[304,256]{1,0:T(8,128)S(1)}, f32[304,256]{1,0:T(8,128)S(1)}, u32[]{:S(2)}, u32[]{:S(2)}) collective-permute-start(f32[304,256]{1,0:T(8,128)S(1)} %get-tuple-element.80), channel_id=1, source_target_pairs={{0,4},{1,5},{2,6},{3,7},{4,0},{5,1},{6,2},{7,3},{8,12},{9,13},{10,... | collective-permute-start | bytes 933896 | tf_op jit(solution)/shard_map/ppermute | solution.py:359
  5.2 14.9 %collective-permute-start.2 = (f32[304,256]{1,0:T(8,128)S(1)}, f32[304,256]{1,0:T(8,128)S(1)}, u32[]{:S(2)}, u32[]{:S(2)}) collective-permute-start(f32[304,256]{1,0:T(8,128)S(1)} %get-tuple-element.81), channel_id=1, source_target_pairs={{0,6},{1,7},{2,4},{3,5},{4,2},{5,3},{6,0},{7,1},{8,14},{9,15},{10,... | collective-permute-start | bytes 933896 | tf_op jit(solution)/shard_map/ppermute | solution.py:359
  6.6 15.0 %collective-permute-start = (f32[304,256]{1,0:T(8,128)S(1)}, f32[304,256]{1,0:T(8,128)S(1)}, u32[]{:S(2)}, u32[]{:S(2)}) collective-permute-start(f32[304,256]{1,0:T(8,128)S(1)} %get-tuple-element.79.refs_0_), channel_id=1, source_target_pairs={{0,2},{1,3},{2,0},{3,1},{4,6},{5,7},{6,4},{7,5},{8,10},{9,11},{10,... | collective-permute-start | bytes 933896 | tf_op jit(solution)/shard_map/ppermute | solution.py:359
  6.7 1.0 %copy-start.1 = (f32[1,256,512]{2,1,0:T(8,128)S(1)}, f32[1,256,512]{2,1,0:T(8,128)}, u32[]{:S(2)}) copy-start(f32[1,256,512]{2,1,0:T(8,128)} %param.11) | copy-start | bytes 1572868
  8.0 23.4 %collective-permute-start.11 = (f32[512,256]{1,0:T(8,128)S(1)}, f32[512,256]{1,0:T(8,128)S(1)}, u32[]{:S(2)}, u32[]{:S(2)}) collective-permute-start(f32[512,256]{1,0:T(8,128)S(1)} %shard_map.79.refs_0_), channel_id=1, source_target_pairs={{0,4},{1,5},{2,6},{3,7},{4,0},{5,1},{6,2},{7,3},{8,12},{9,13},{10,... | collective-permute-start | bytes 1572872 | tf_op jit(solution)/shard_map/ppermute | solution.py:359
  10.0 22.3 %collective-permute-start.10 = (f32[512,256]{1,0:T(8,128)S(1)}, f32[512,256]{1,0:T(8,128)S(1)}, u32[]{:S(2)}, u32[]{:S(2)}) collective-permute-start(f32[512,256]{1,0:T(8,128)S(1)} %shard_map.79.refs_0_), channel_id=1, source_target_pairs={{0,2},{1,3},{2,0},{3,1},{4,6},{5,7},{6,4},{7,5},{8,10},{9,11},{10,... | collective-permute-start | bytes 1572872 | tf_op jit(solution)/shard_map/ppermute | solution.py:359
  21.6 1.6 %collective-permute-start.4 = (f32[304,256]{1,0:T(8,128)S(1)}, f32[304,256]{1,0:T(8,128)S(1)}, u32[]{:S(2)}, u32[]{:S(2)}) collective-permute-start(f32[304,256]{1,0:T(8,128)S(1)} %collective-permute-done.refs_1_), channel_id=1, source_target_pairs={{0,1},{1,0},{2,3},{3,2},{4,5},{5,4},{6,7},{7,6},{8,9},{9,8},{10,11... | collective-permute-start | bytes 933896 | tf_op jit(solution)/shard_map/ppermute | solution.py:359
  21.6 2.0 %collective-permute-start.5 = (f32[304,256]{1,0:T(8,128)S(1)}, f32[304,256]{1,0:T(8,128)S(1)}, u32[]{:S(2)}, u32[]{:S(2)}) collective-permute-start(f32[304,256]{1,0:T(8,128)S(1)} %collective-permute-done.1.refs_2_), channel_id=1, source_target_pairs={{0,1},{1,0},{2,3},{3,2},{4,5},{5,4},{6,7},{7,6},{8,9},{9,8},{10,11... | collective-permute-start | bytes 933896 | tf_op jit(solution)/shard_map/ppermute | solution.py:359
  22.1 2.0 %collective-permute-start.6 = (f32[304,256]{1,0:T(8,128)S(1)}, f32[304,256]{1,0:T(8,128)S(1)}, u32[]{:S(2)}, u32[]{:S(2)}) collective-permute-start(f32[304,256]{1,0:T(8,128)S(1)} %collective-permute-done.2.refs_3_), channel_id=1, source_target_pairs={{0,1},{1,0},{2,3},{3,2},{4,5},{5,4},{6,7},{7,6},{8,9},{9,8},{10,11... | collective-permute-start | bytes 933896 | tf_op jit(solution)/shard_map/ppermute | solution.py:359
  25.3 5.4 %collective-permute-start.7 = (f32[48,512]{1,0:T(8,128)S(1)}, f32[48,512]{1,0:T(8,128)S(1)}, u32[]{:S(2)}, u32[]{:S(2)}) collective-permute-start(f32[48,512]{1,0:T(8,128)S(1)} %get-tuple-element.94), channel_id=1, source_target_pairs={{0,8},{1,9},{2,10},{3,11},{4,12},{5,13},{6,14},{7,15}} | collective-permute-start | bytes 294920 | tf_op jit(solution)/shard_map/ppermute | solution.py:376
  30.7 3.4 %collective-permute-start.8 = (f32[48,512]{1,0:T(8,128)S(1)}, f32[48,512]{1,0:T(8,128)S(1)}, u32[]{:S(2)}, u32[]{:S(2)}) collective-permute-start(f32[48,512]{1,0:T(8,128)S(1)} %shard_map.83.refs_3_), channel_id=1, source_target_pairs={{8,16},{9,17},{10,18},{11,19},{12,20},{13,21},{14,22},{15,23}} | collective-permute-start | bytes 294920 | tf_op jit(solution)/shard_map/ppermute | solution.py:376
  32.4 9.2 %collective-permute-start.12 = (f32[512,256]{1,0:T(8,128)S(1)}, f32[512,256]{1,0:T(8,128)S(1)}, u32[]{:S(2)}, u32[]{:S(2)}) collective-permute-start(f32[512,256]{1,0:T(8,128)S(1)} %shard_map.89), channel_id=1, source_target_pairs={{0,4},{1,3},{2,6},{3,1},{4,0},{5,7},{6,2},{7,5},{8,12},{9,11},{10,... | collective-permute-start | bytes 1572872 | tf_op jit(solution)/shard_map/ppermute | solution.py:359
  34.1 7.5 %collective-permute-start.9 = (f32[48,512]{1,0:T(8,128)S(1)}, f32[48,512]{1,0:T(8,128)S(1)}, u32[]{:S(2)}, u32[]{:S(2)}) collective-permute-start(f32[48,512]{1,0:T(8,128)S(1)} %shard_map.84), channel_id=1, source_target_pairs={{16,24},{17,25},{18,26},{19,27},{20,28},{21,29},{22,30},{23,31}} | collective-permute-start | bytes 294920 | tf_op jit(solution)/shard_map/ppermute | solution.py:376
  34.8 2.0 %collective-permute-start.13 = (f32[512,256]{1,0:T(8,128)S(1)}, f32[512,256]{1,0:T(8,128)S(1)}, u32[]{:S(2)}, u32[]{:S(2)}) collective-permute-start(f32[512,256]{1,0:T(8,128)S(1)} %get-tuple-element.122.refs_0_), channel_id=1, source_target_pairs={{0,1},{1,0},{2,3},{3,2},{4,5},{5,4},{6,7},{7,6},{8,9},{9,8},{10,11... | collective-permute-start | bytes 1572872 | tf_op jit(solution)/shard_map/ppermute | solution.py:359
  34.9 2.6 %collective-permute-start.14 = (f32[512,256]{1,0:T(8,128)S(1)}, f32[512,256]{1,0:T(8,128)S(1)}, u32[]{:S(2)}, u32[]{:S(2)}) collective-permute-start(f32[512,256]{1,0:T(8,128)S(1)} %get-tuple-element.123.refs_1_), channel_id=1, source_target_pairs={{0,1},{1,0},{2,3},{3,2},{4,5},{5,4},{6,7},{7,6},{8,9},{9,8},{10,11... | collective-permute-start | bytes 1572872 | tf_op jit(solution)/shard_map/ppermute | solution.py:359
  35.4 2.9 %collective-permute-start.15 = (f32[512,256]{1,0:T(8,128)S(1)}, f32[512,256]{1,0:T(8,128)S(1)}, u32[]{:S(2)}, u32[]{:S(2)}) collective-permute-start(f32[512,256]{1,0:T(8,128)S(1)} %get-tuple-element.124.refs_2_), channel_id=1, source_target_pairs={{0,1},{1,0},{2,3},{3,2},{4,5},{5,4},{6,7},{7,6},{8,9},{9,8},{10,11... | collective-permute-start | bytes 1572872 | tf_op jit(solution)/shard_map/ppermute | solution.py:359
  41.6 1.9 %collective-permute-start.16 = (f32[512,256]{1,0:T(8,128)S(1)}, f32[512,256]{1,0:T(8,128)S(1)}, u32[]{:S(2)}, u32[]{:S(2)}) collective-permute-start(f32[512,256]{1,0:T(8,128)S(1)} %shard_map.92.refs_0_), channel_id=1, source_target_pairs={{0,1},{1,0},{2,3},{3,2},{4,5},{5,4},{6,7},{7,6},{8,9},{9,8},{10,11... | collective-permute-start | bytes 1572872 | tf_op jit(solution)/shard_map/ppermute | solution.py:359
  43.7 0.7 collective-permute-start.17
  44.5 0.7 collective-permute-start.18
  45.2 17.1 %collective-permute-start.22 = (f32[48,512]{1,0:T(8,128)S(1)}, f32[48,512]{1,0:T(8,128)S(1)}, u32[]{:S(2)}, u32[]{:S(2)}) collective-permute-start(f32[48,512]{1,0:T(8,128)S(1)} %shard_map.97.refs_4_), channel_id=1, source_target_pairs={{8,0},{9,1},{10,2},{11,3},{12,4},{13,5},{14,6},{15,7}} | collective-permute-start | bytes 294920 | tf_op jit(solution)/shard_map/ppermute | solution.py:376
  46.5 20.1 %collective-permute-start.19 = (f32[48,512]{1,0:T(8,128)S(1)}, f32[48,512]{1,0:T(8,128)S(1)}, u32[]{:S(2)}, u32[]{:S(2)}) collective-permute-start(f32[48,512]{1,0:T(8,128)S(1)} %get-tuple-element.135), channel_id=1, source_target_pairs={{0,2},{1,3},{2,0},{3,1},{4,6},{5,7},{6,4},{7,5},{8,10},{9,11},{10,... | collective-permute-start | bytes 294920 | tf_op jit(solution)/shard_map/ppermute | solution.py:359
  48.3 18.8 %collective-permute-start.20 = (f32[48,512]{1,0:T(8,128)S(1)}, f32[48,512]{1,0:T(8,128)S(1)}, u32[]{:S(2)}, u32[]{:S(2)}) collective-permute-start(f32[48,512]{1,0:T(8,128)S(1)} %get-tuple-element.136), channel_id=1, source_target_pairs={{0,4},{1,5},{2,6},{3,7},{4,0},{5,1},{6,2},{7,3},{8,12},{9,13},{10,... | collective-permute-start | bytes 294920 | tf_op jit(solution)/shard_map/ppermute | solution.py:359
  49.8 17.3 %collective-permute-start.21 = (f32[48,512]{1,0:T(8,128)S(1)}, f32[48,512]{1,0:T(8,128)S(1)}, u32[]{:S(2)}, u32[]{:S(2)}) collective-permute-start(f32[48,512]{1,0:T(8,128)S(1)} %get-tuple-element.137), channel_id=1, source_target_pairs={{0,6},{1,7},{2,4},{3,5},{4,2},{5,3},{6,0},{7,1},{8,14},{9,15},{10,... | collective-permute-start | bytes 294920 | tf_op jit(solution)/shard_map/ppermute | solution.py:359
  63.5 5.6 %collective-permute-start.25 = (f32[48,512]{1,0:T(8,128)S(1)}, f32[48,512]{1,0:T(8,128)S(1)}, u32[]{:S(2)}, u32[]{:S(2)}) collective-permute-start(f32[48,512]{1,0:T(8,128)S(1)} %get-tuple-element.153), channel_id=1, source_target_pairs={{0,6},{1,7},{2,4},{3,5},{4,2},{5,3},{6,0},{7,1},{8,14},{9,15},{10,... | collective-permute-start | bytes 294920 | tf_op jit(solution)/shard_map/ppermute | solution.py:359
  66.1 4.6 %collective-permute-start.23 = (f32[48,512]{1,0:T(8,128)S(1)}, f32[48,512]{1,0:T(8,128)S(1)}, u32[]{:S(2)}, u32[]{:S(2)}) collective-permute-start(f32[48,512]{1,0:T(8,128)S(1)} %get-tuple-element.151), channel_id=1, source_target_pairs={{0,2},{1,3},{2,0},{3,1},{4,6},{5,7},{6,4},{7,5},{8,10},{9,11},{10,... | collective-permute-start | bytes 294920 | tf_op jit(solution)/shard_map/ppermute | solution.py:359
  66.6 4.6 %collective-permute-start.24 = (f32[48,512]{1,0:T(8,128)S(1)}, f32[48,512]{1,0:T(8,128)S(1)}, u32[]{:S(2)}, u32[]{:S(2)}) collective-permute-start(f32[48,512]{1,0:T(8,128)S(1)} %get-tuple-element.152), channel_id=1, source_target_pairs={{0,4},{1,5},{2,6},{3,7},{4,0},{5,1},{6,2},{7,3},{8,12},{9,13},{10,... | collective-permute-start | bytes 294920 | tf_op jit(solution)/shard_map/ppermute | solution.py:359
  67.1 4.2 %collective-permute-start.26 = (f32[4,48,256]{2,1,0:T(8,128)S(1)}, f32[4,48,256]{2,1,0:T(8,128)S(1)}, u32[]{:S(2)}, u32[]{:S(2)}) collective-permute-start(f32[4,48,256]{2,1,0:T(8,128)S(1)} %shard_map.102), channel_id=1, source_target_pairs={{0,1},{1,0},{2,3},{3,2},{4,5},{5,4},{6,7},{7,6},{8,9},{9,8},{10,11... | collective-permute-start | bytes 589832 | tf_op jit(solution)/shard_map/ppermute | solution.py:359
  71.2 1.5 %collective-permute-start.27 = (f32[4,48,256]{2,1,0:T(8,128)S(1)}, f32[4,48,256]{2,1,0:T(8,128)S(1)}, u32[]{:S(2)}, u32[]{:S(2)}) collective-permute-start(f32[4,48,256]{2,1,0:T(8,128)S(1)} %shard_map.104), channel_id=1, source_target_pairs={{0,1},{1,0},{2,3},{3,2},{4,5},{5,4},{6,7},{7,6},{8,9},{9,8},{10,11... | collective-permute-start | bytes 589832 | tf_op jit(solution)/shard_map/ppermute | solution.py:359

commit v6 on v5

--- a/solution.py
+++ b/solution.py
@@ -9,18 +9,15 @@
 
 GROUP = 4
 LANES = 128
-PIECES = 1
+SPARE = 8
 FW = (0, 0, 10**11, 10**11)
 BW = (0, 10**10)
 JF = 10**11
 JP = 0
 JJ = 0
 GA = 10**10
-AF = 0
 G1 = G2 = G3 = 10**9
 G4 = 10**9
-G6 = 10**9
-G5 = 10**10
 BF16 = jnp.bfloat16
 F32 = jnp.float32
 
@@ -110,7 +107,7 @@
     copies[1].wait()
     mask = mask_ref[...].astype(F32)
     for at, tile in enumerate(lane_tiles(gain_ref[...] * mask)):
-        tiles[at] = tile
+        tiles[at, 0 : tile.shape[0], :] = tile
         lines = slice(at * LANES, (at + 1) * LANES)
         for part in range(2):
             piece = tiles[at, pl.ds(part, half, stride=2), :].T
@@ -142,7 +139,7 @@
     _, spot, row = place()
     rows = lax.axis_size("rows")
     for at, tile in enumerate(lane_tiles(prior_ref[...])):
-        tiles[at] = tile
+        tiles[at, 0 : tile.shape[0], :] = tile
         for block in range(prior_ref.shape[0] // half):
             start = (block // 2) * 2 * half + block % 2
             piece = tiles[at, pl.ds(start, half, stride=2), :].T
@@ -157,7 +154,7 @@
     panel, states = gain_ref.shape
     half = panel // 2
     for at, tile in enumerate(lane_tiles(gain_ref[...])):
-        tiles[at] = tile
+        tiles[at, 0 : tile.shape[0], :] = tile
         for part in range(2):
             turned[part, at * LANES : (at + 1) * LANES, :] = tiles[at, pl.ds(part, half, stride=2), :].T
     for block in range(states // half):
@@ -332,7 +329,7 @@
             for part in range(2):
                 piece = turned[kind, lines, part * half : (part + 1) * half].T
                 tiles[kind, at, pl.ds(part, half, stride=2), :] = piece
-            out_ref[:, lines] = tiles[kind, at]
+            out_ref[:, lines] = tiles[kind, at, 0:panel, :]
 
 
 def gate(values, token, flops):
@@ -388,7 +385,7 @@
             pltpu.VMEM((panel, sites), F32),
             pltpu.VMEM((sites, paths), F32),
             pltpu.VMEM((paths, sites), F32),
-            pltpu.VMEM((sites // LANES, panel, LANES), F32),
+            pltpu.VMEM((sites // LANES, panel + SPARE, LANES), F32),
             pltpu.SemaphoreType.DMA((4,)),
         ],
         source=pltpu.HBM,
@@ -398,13 +395,13 @@
         functools.partial(prior_kernel, share, half),
         (prior_mean,),
         [((share, states), F32)],
-        [pltpu.VMEM((paths, states), F32), pltpu.VMEM((paths // LANES, states, LANES), F32)],
+        [pltpu.VMEM((paths, states), F32), pltpu.VMEM((paths // LANES, states + SPARE, LANES), F32)],
     )
     pieces = call(
         smoother_gain_kernel,
         (smooth_gains[0],),
-        [((states // PIECES, panel), F32)] * PIECES,
-        [pltpu.VMEM((2, states, half), F32), pltpu.VMEM((states // LANES, panel, LANES), F32)],
+        [((states, panel), F32)],
+        [pltpu.VMEM((2, states + SPARE, half), F32), pltpu.VMEM((states // LANES, panel + SPARE, LANES), F32)],
     )
     (turned_gain,) = pieces
     gain_x, gain_y = across(turned_gain, 1), across(turned_gain, 2)
@@ -512,7 +509,7 @@
         functools.partial(home_kernel, share),
         (*sent, *smooth_near, neighbour(filt_far), neighbour(far)),
         [((panel, paths), F32)] * 2,
-        [pltpu.VMEM((2, paths, panel), F32), pltpu.VMEM((2, paths // LANES, panel, LANES), F32)],
+        [pltpu.VMEM((2, paths, panel), F32), pltpu.VMEM((2, paths // LANES, panel + SPARE, LANES), F32)],
     )
     return filt[None], smooth[None]
 

time: 74.1 us -> 74.1 us (level)
  no operation moved by 1% of the time
where the time goes in v6:
time: 74.1 us; the launch traced here: 73.9 us
  waiting for transfers between devices  40.1 us (54%)
  starting transfers between devices  25.4 us (34%)
  Pallas kernels  6.49 us (9%)
  local copies, waits for them, and re-layouts  1.05 us (1%)
  between operations  0.91 us (1%)
    ppermute x22, waiting for transfers between devices, swap(): return lax.ppermute(value, both, pairs)  25.5 us
    ppermute x22, starting transfers between devices, swap(): return lax.ppermute(value, both, pairs)  18.3 us
    ppermute x6, waiting for transfers between devices, hop(): return lax.ppermute(value, both, pairs)  14.6 us
    ppermute x6, starting transfers between devices, hop(): return lax.ppermute(value, both, pairs)  7 us
    pallas_call x29, Pallas kernels, call(): pl.pallas_call(kernel, out_shape=[jax.ShapeDtypeStruct(shape, dtype) for...  6.49 us
  transfers between devices with their start and end apart: 28, of which 17 were waited for; matrix products, arithmetic and copies ran while one was open for 0% of the time, Pallas kernels for 5%

profile of v6, /device:TPU:0, one launch (start us, length us, event | category | flops | bytes accessed | tf_op | source)
XLA Modules:
  0.0 73.9 jit_solution(17376788487773938328)
XLA Ops:
  0.6 1.4 %shard_map.77 = (f32[304,256]{1,0:T(8,128)S(1)}, f32[304,256]{1,0:T(8,128)S(1)}, f32[304,256]{1,0:T(8,128)S(1)}, f32[48,256]{1,0:T(8,128)S(1)}, f32[8,256]{1,0:T(8,128)S(1)}) custom-call(f32[1,256]{1,0:T(1,128)} %bitcast.9, s32[1,256]{1,0:T(1,128)} %mask_hbm.1, f32[256,256]{1,0:T(8,128)} %bitcast.8, f32[256,384]{1,0:T(8,128)} %bitcast.7), custom_call_target="tpu_custom_call" | custom-call | bytes 2097152 | tf_op jit(solution)/shard_map/pallas_call | solution.py:26
  2.6 2.6 %collective-permute-start.1 = (f32[304,256]{1,0:T(8,128)S(1)}, f32[304,256]{1,0:T(8,128)S(1)}, u32[]{:S(2)}, u32[]{:S(2)}) collective-permute-start(f32[304,256]{1,0:T(8,128)S(1)} %get-tuple-element.80), channel_id=1, source_target_pairs={{0,4},{1,5},{2,6},{3,7},{4,0},{5,1},{6,2},{7,3},{8,12},{9,13},{10,... | collective-permute-start | bytes 933896 | tf_op jit(solution)/shard_map/ppermute | solution.py:356
  5.2 1.4 %collective-permute-start.2 = (f32[304,256]{1,0:T(8,128)S(1)}, f32[304,256]{1,0:T(8,128)S(1)}, u32[]{:S(2)}, u32[]{:S(2)}) collective-permute-start(f32[304,256]{1,0:T(8,128)S(1)} %get-tuple-element.81), channel_id=1, source_target_pairs={{0,6},{1,7},{2,4},{3,5},{4,2},{5,3},{6,0},{7,1},{8,14},{9,15},{10,... | collective-permute-start | bytes 933896 | tf_op jit(solution)/shard_map/ppermute | solution.py:356
  6.7 1.0 %copy-done.1 = f32[1,256,512]{2,1,0:T(8,128)S(1)} copy-done((f32[1,256,512]{2,1,0:T(8,128)S(1)}, f32[1,256,512]{2,1,0:T(8,128)}, u32[]{:S(2)}) %copy-start.1) | copy-done | bytes 524312
  8.0 2.0 %collective-permute-start.11 = (f32[512,256]{1,0:T(8,128)S(1)}, f32[512,256]{1,0:T(8,128)S(1)}, u32[]{:S(2)}, u32[]{:S(2)}) collective-permute-start(f32[512,256]{1,0:T(8,128)S(1)} %shard_map.79.refs_0_), channel_id=1, source_target_pairs={{0,4},{1,5},{2,6},{3,7},{4,0},{5,1},{6,2},{7,3},{8,12},{9,13},{10,... | collective-permute-start | bytes 1572872 | tf_op jit(solution)/shard_map/ppermute | solution.py:356
  10.1 1.5 %collective-permute-start.10 = (f32[512,256]{1,0:T(8,128)S(1)}, f32[512,256]{1,0:T(8,128)S(1)}, u32[]{:S(2)}, u32[]{:S(2)}) collective-permute-start(f32[512,256]{1,0:T(8,128)S(1)} %shard_map.79.refs_0_), channel_id=1, source_target_pairs={{0,2},{1,3},{2,0},{3,1},{4,6},{5,7},{6,4},{7,5},{8,10},{9,11},{10,... | collective-permute-start | bytes 1572872 | tf_op jit(solution)/shard_map/ppermute | solution.py:356
  11.8 8.2 %collective-permute-done.1.refs_2_ = f32[304,256]{1,0:T(8,128)S(1)} collective-permute-done((f32[304,256]{1,0:T(8,128)S(1)}, f32[304,256]{1,0:T(8,128)S(1)}, u32[]{:S(2)}, u32[]{:S(2)}) %collective-permute-start.1) | collective-permute-done | bytes 311328 | tf_op jit(solution)/shard_map/ppermute | solution.py:356
  20.1 1.5 %collective-permute-done.refs_1_ = f32[304,256]{1,0:T(8,128)S(1)} collective-permute-done((f32[304,256]{1,0:T(8,128)S(1)}, f32[304,256]{1,0:T(8,128)S(1)}, u32[]{:S(2)}, u32[]{:S(2)}) %collective-permute-start) | collective-permute-done | bytes 311328 | tf_op jit(solution)/shard_map/ppermute | solution.py:356
  22.1 1.1 %collective-permute-done.4.refs_5_ = f32[304,256]{1,0:T(8,128)S(1)} collective-permute-done((f32[304,256]{1,0:T(8,128)S(1)}, f32[304,256]{1,0:T(8,128)S(1)}, u32[]{:S(2)}, u32[]{:S(2)}) %collective-permute-start.4) | collective-permute-done | bytes 311328 | tf_op jit(solution)/shard_map/ppermute | solution.py:356
  24.4 0.9 %shard_map.81 = (f32[4,48,512]{2,1,0:T(8,128)S(1)}, f32[48,512]{1,0:T(8,128)S(1)}, f32[48,512]{1,0:T(8,128)S(1)}, f32[48,512]{1,0:T(8,128)S(1)}, f32[48,512]{1,0:T(8,128)S(1)}, /*index=5*/f32[48,512]{1,0:T(8,128)S(1)}) custom-call(f32[48,512]{1,0:T(8,128)S(1)} %shard_map.78.start_ref, f32[8,256]{1,0:T(8,128)S(1)} %get-tuple-element.85.coef_ref, ...), custom_call_target="tpu_custom_call" | custom-call | bytes 2097152 | tf_op jit(solution)/shard_map/pallas_call | solution.py:26
  25.3 3.1 %collective-permute-start.7 = (f32[48,512]{1,0:T(8,128)S(1)}, f32[48,512]{1,0:T(8,128)S(1)}, u32[]{:S(2)}, u32[]{:S(2)}) collective-permute-start(f32[48,512]{1,0:T(8,128)S(1)} %get-tuple-element.94), channel_id=1, source_target_pairs={{0,8},{1,9},{2,10},{3,11},{4,12},{5,13},{6,14},{7,15}} | collective-permute-start | bytes 294920 | tf_op jit(solution)/shard_map/ppermute | solution.py:373
  28.4 2.3 %collective-permute-done.7.start_ref = f32[48,512]{1,0:T(8,128)S(1)} collective-permute-done((f32[48,512]{1,0:T(8,128)S(1)}, f32[48,512]{1,0:T(8,128)S(1)}, u32[]{:S(2)}, u32[]{:S(2)}) %collective-permute-start.7) | collective-permute-done | bytes 98336 | tf_op jit(solution)/shard_map/ppermute | solution.py:373
  31.4 0.9 %collective-permute-done.10.refs_1_ = f32[512,256]{1,0:T(8,128)S(1)} collective-permute-done((f32[512,256]{1,0:T(8,128)S(1)}, f32[512,256]{1,0:T(8,128)S(1)}, u32[]{:S(2)}, u32[]{:S(2)}) %collective-permute-start.10) | collective-permute-done | bytes 524320 | tf_op jit(solution)/shard_map/ppermute | solution.py:356
  32.4 1.8 %collective-permute-start.12 = (f32[512,256]{1,0:T(8,128)S(1)}, f32[512,256]{1,0:T(8,128)S(1)}, u32[]{:S(2)}, u32[]{:S(2)}) collective-permute-start(f32[512,256]{1,0:T(8,128)S(1)} %shard_map.89), channel_id=1, source_target_pairs={{0,4},{1,3},{2,6},{3,1},{4,0},{5,7},{6,2},{7,5},{8,12},{9,11},{10,... | collective-permute-start | bytes 1572872 | tf_op jit(solution)/shard_map/ppermute | solution.py:356
  34.1 0.7 collective-permute-start.9
  35.5 1.3 %collective-permute-done.13.refs_3_ = f32[512,256]{1,0:T(8,128)S(1)} collective-permute-done((f32[512,256]{1,0:T(8,128)S(1)}, f32[512,256]{1,0:T(8,128)S(1)}, u32[]{:S(2)}, u32[]{:S(2)}) %collective-permute-start.13) | collective-permute-done | bytes 524320 | tf_op jit(solution)/shard_map/ppermute | solution.py:356
  36.8 0.7 %collective-permute-done.14.refs_4_ = f32[512,256]{1,0:T(8,128)S(1)} collective-permute-done((f32[512,256]{1,0:T(8,128)S(1)}, f32[512,256]{1,0:T(8,128)S(1)}, u32[]{:S(2)}, u32[]{:S(2)}) %collective-permute-start.14) | collective-permute-done | bytes 524320 | tf_op jit(solution)/shard_map/ppermute | solution.py:356
  37.5 0.7 %collective-permute-done.15.refs_5_ = f32[512,256]{1,0:T(8,128)S(1)} collective-permute-done((f32[512,256]{1,0:T(8,128)S(1)}, f32[512,256]{1,0:T(8,128)S(1)}, u32[]{:S(2)}, u32[]{:S(2)}) %collective-permute-start.15) | collective-permute-done | bytes 524320 | tf_op jit(solution)/shard_map/ppermute | solution.py:356
  38.9 2.7 %collective-permute-done.12.refs_0_ = f32[512,256]{1,0:T(8,128)S(1)} collective-permute-done((f32[512,256]{1,0:T(8,128)S(1)}, f32[512,256]{1,0:T(8,128)S(1)}, u32[]{:S(2)}, u32[]{:S(2)}) %collective-permute-start.12) | collective-permute-done | bytes 524320 | tf_op jit(solution)/shard_map/ppermute | solution.py:356
  41.6 1.9 %collective-permute-done.16.refs_1_ = f32[512,256]{1,0:T(8,128)S(1)} collective-permute-done((f32[512,256]{1,0:T(8,128)S(1)}, f32[512,256]{1,0:T(8,128)S(1)}, u32[]{:S(2)}, u32[]{:S(2)}) %collective-permute-start.16) | collective-permute-done | bytes 524320 | tf_op jit(solution)/shard_map/ppermute | solution.py:356
  43.7 0.7 collective-permute-start.17
  44.5 0.7 collective-permute-start.18
  45.2 1.3 %collective-permute-start.22 = (f32[48,512]{1,0:T(8,128)S(1)}, f32[48,512]{1,0:T(8,128)S(1)}, u32[]{:S(2)}, u32[]{:S(2)}) collective-permute-start(f32[48,512]{1,0:T(8,128)S(1)} %shard_map.97.refs_4_), channel_id=1, source_target_pairs={{8,0},{9,1},{10,2},{11,3},{12,4},{13,5},{14,6},{15,7}} | collective-permute-start | bytes 294920 | tf_op jit(solution)/shard_map/ppermute | solution.py:373
  46.5 1.8 %collective-permute-start.19 = (f32[48,512]{1,0:T(8,128)S(1)}, f32[48,512]{1,0:T(8,128)S(1)}, u32[]{:S(2)}, u32[]{:S(2)}) collective-permute-start(f32[48,512]{1,0:T(8,128)S(1)} %get-tuple-element.135), channel_id=1, source_target_pairs={{0,2},{1,3},{2,0},{3,1},{4,6},{5,7},{6,4},{7,5},{8,10},{9,11},{10,... | collective-permute-start | bytes 294920 | tf_op jit(solution)/shard_map/ppermute | solution.py:356
  48.3 1.5 %collective-permute-start.20 = (f32[48,512]{1,0:T(8,128)S(1)}, f32[48,512]{1,0:T(8,128)S(1)}, u32[]{:S(2)}, u32[]{:S(2)}) collective-permute-start(f32[48,512]{1,0:T(8,128)S(1)} %get-tuple-element.136), channel_id=1, source_target_pairs={{0,4},{1,5},{2,6},{3,7},{4,0},{5,1},{6,2},{7,3},{8,12},{9,13},{10,... | collective-permute-start | bytes 294920 | tf_op jit(solution)/shard_map/ppermute | solution.py:356
  50.1 12.3 %collective-permute-done.22.start_ref = f32[48,512]{1,0:T(8,128)S(1)} collective-permute-done((f32[48,512]{1,0:T(8,128)S(1)}, f32[48,512]{1,0:T(8,128)S(1)}, u32[]{:S(2)}, u32[]{:S(2)}) %collective-permute-start.22) | collective-permute-done | bytes 98336 | tf_op jit(solution)/shard_map/ppermute | solution.py:373
  62.4 1.2 %shard_map.101 = (f32[48,512]{1,0:T(8,128)S(1)}, f32[48,512]{1,0:T(8,128)S(1)}, f32[48,512]{1,0:T(8,128)S(1)}, f32[48,512]{1,0:T(8,128)S(1)}) custom-call(f32[48,512]{1,0:T(8,128)S(1)} %collective-permute-done.22.start_ref, f32[8,256]{1,0:T(8,128)S(1)} %get-tuple-element.85.coef_ref, ...), custom_call_target="tpu_custom_call", output_to_operand_aliasing={{0}: (5, {}), {1}: (6, {}), {2}: (7, {}), {3}: (8, {})} | custom-call | bytes 2097152 | tf_op jit(solution)/shard_map/pallas_call | solution.py:26
  63.5 2.5 %collective-permute-start.25 = (f32[48,512]{1,0:T(8,128)S(1)}, f32[48,512]{1,0:T(8,128)S(1)}, u32[]{:S(2)}, u32[]{:S(2)}) collective-permute-start(f32[48,512]{1,0:T(8,128)S(1)} %get-tuple-element.153), channel_id=1, source_target_pairs={{0,6},{1,7},{2,4},{3,5},{4,2},{5,3},{6,0},{7,1},{8,14},{9,15},{10,... | collective-permute-start | bytes 294920 | tf_op jit(solution)/shard_map/ppermute | solution.py:356
  67.2 1.9 %collective-permute-done.25.refs_1_.refs_7_ = f32[48,512]{1,0:T(8,128)S(1)} collective-permute-done((f32[48,512]{1,0:T(8,128)S(1)}, f32[48,512]{1,0:T(8,128)S(1)}, u32[]{:S(2)}, u32[]{:S(2)}) %collective-permute-start.25) | collective-permute-done | bytes 98336 | tf_op jit(solution)/shard_map/ppermute | solution.py:356
  69.1 1.5 %collective-permute-done.23.refs_0_.refs_5_ = f32[48,512]{1,0:T(8,128)S(1)} collective-permute-done((f32[48,512]{1,0:T(8,128)S(1)}, f32[48,512]{1,0:T(8,128)S(1)}, u32[]{:S(2)}, u32[]{:S(2)}) %collective-permute-start.23) | collective-permute-done | bytes 98336 | tf_op jit(solution)/shard_map/ppermute | solution.py:356
  71.3 1.4 %collective-permute-done.27.refs_9_ = f32[4,48,256]{2,1,0:T(8,128)S(1)} collective-permute-done((f32[4,48,256]{2,1,0:T(8,128)S(1)}, f32[4,48,256]{2,1,0:T(8,128)S(1)}, u32[]{:S(2)}, u32[]{:S(2)}) %collective-permute-start.27) | collective-permute-done | bytes 196640 | tf_op jit(solution)/shard_map/ppermute | solution.py:356
  72.7 1.1 %shard_map.105 = (f32[256,384]{1,0:T(8,128)}, f32[256,384]{1,0:T(8,128)}) custom-call(f32[48,512]{1,0:T(8,128)S(1)} %get-tuple-element.134.refs_0_, f32[48,512]{1,0:T(8,128)S(1)} %collective-permute-done.19.refs_1_, f32[48,512]{1,0:T(8,128)S(1)} %collective-permute-done.20.refs_2_, f32[48,512]{1,0:T(8,128)S(1)} %collective-permute-done.21.refs_3_, ...), custom_call_target="tpu_custom_call" | custom-call | bytes 2097152 | tf_op jit(solution)/shard_map/pallas_call | solution.py:26
  (57 shorter events, 7.2 us)
Async XLA Ops:
  0.6 10.9 %copy-start = (f32[512,384]{1,0:T(8,128)S(1)}, f32[512,384]{1,0:T(8,128)}, u32[]{:S(2)}) copy-start(f32[512,384]{1,0:T(8,128)} %prior_ref.1) | copy-start | bytes 2359300
  2.1 8.0 %collective-permute-start.3 = (f32[304,256]{1,0:T(8,128)S(1)}, f32[304,256]{1,0:T(8,128)S(1)}, u32[]{:S(2)}, u32[]{:S(2)}) collective-permute-start(f32[304,256]{1,0:T(8,128)S(1)} %get-tuple-element.79.refs_0_), channel_id=1, source_target_pairs={{0,1},{1,0},{2,3},{3,2},{4,5},{5,4},{6,7},{7,6},{8,9},{9,8},{10,11... | collective-permute-start | bytes 933896 | tf_op jit(solution)/shard_map/ppermute | solution.py:356
  2.6 17.5 %collective-permute-start.1 = (f32[304,256]{1,0:T(8,128)S(1)}, f32[304,256]{1,0:T(8,128)S(1)}, u32[]{:S(2)}, u32[]{:S(2)}) collective-permute-start(f32[304,256]{1,0:T(8,128)S(1)} %get-tuple-element.80), channel_id=1, source_target_pairs={{0,4},{1,5},{2,6},{3,7},{4,0},{5,1},{6,2},{7,3},{8,12},{9,13},{10,... | collective-permute-start | bytes 933896 | tf_op jit(solution)/shard_map/ppermute | solution.py:356
  5.2 14.9 %collective-permute-start.2 = (f32[304,256]{1,0:T(8,128)S(1)}, f32[304,256]{1,0:T(8,128)S(1)}, u32[]{:S(2)}, u32[]{:S(2)}) collective-permute-start(f32[304,256]{1,0:T(8,128)S(1)} %get-tuple-element.81), channel_id=1, source_target_pairs={{0,6},{1,7},{2,4},{3,5},{4,2},{5,3},{6,0},{7,1},{8,14},{9,15},{10,... | collective-permute-start | bytes 933896 | tf_op jit(solution)/shard_map/ppermute | solution.py:356
  6.6 15.0 %collective-permute-start = (f32[304,256]{1,0:T(8,128)S(1)}, f32[304,256]{1,0:T(8,128)S(1)}, u32[]{:S(2)}, u32[]{:S(2)}) collective-permute-start(f32[304,256]{1,0:T(8,128)S(1)} %get-tuple-element.79.refs_0_), channel_id=1, source_target_pairs={{0,2},{1,3},{2,0},{3,1},{4,6},{5,7},{6,4},{7,5},{8,10},{9,11},{10,... | collective-permute-start | bytes 933896 | tf_op jit(solution)/shard_map/ppermute | solution.py:356
  6.7 1.0 %copy-start.1 = (f32[1,256,512]{2,1,0:T(8,128)S(1)}, f32[1,256,512]{2,1,0:T(8,128)}, u32[]{:S(2)}) copy-start(f32[1,256,512]{2,1,0:T(8,128)} %param.11) | copy-start | bytes 1572868
  8.0 23.4 %collective-permute-start.11 = (f32[512,256]{1,0:T(8,128)S(1)}, f32[512,256]{1,0:T(8,128)S(1)}, u32[]{:S(2)}, u32[]{:S(2)}) collective-permute-start(f32[512,256]{1,0:T(8,128)S(1)} %shard_map.79.refs_0_), channel_id=1, source_target_pairs={{0,4},{1,5},{2,6},{3,7},{4,0},{5,1},{6,2},{7,3},{8,12},{9,13},{10,... | collective-permute-start | bytes 1572872 | tf_op jit(solution)/shard_map/ppermute | solution.py:356
  10.1 22.3 %collective-permute-start.10 = (f32[512,256]{1,0:T(8,128)S(1)}, f32[512,256]{1,0:T(8,128)S(1)}, u32[]{:S(2)}, u32[]{:S(2)}) collective-permute-start(f32[512,256]{1,0:T(8,128)S(1)} %shard_map.79.refs_0_), channel_id=1, source_target_pairs={{0,2},{1,3},{2,0},{3,1},{4,6},{5,7},{6,4},{7,5},{8,10},{9,11},{10,... | collective-permute-start | bytes 1572872 | tf_op jit(solution)/shard_map/ppermute | solution.py:356
  21.6 1.6 %collective-permute-start.4 = (f32[304,256]{1,0:T(8,128)S(1)}, f32[304,256]{1,0:T(8,128)S(1)}, u32[]{:S(2)}, u32[]{:S(2)}) collective-permute-start(f32[304,256]{1,0:T(8,128)S(1)} %collective-permute-done.refs_1_), channel_id=1, source_target_pairs={{0,1},{1,0},{2,3},{3,2},{4,5},{5,4},{6,7},{7,6},{8,9},{9,8},{10,11... | collective-permute-start | bytes 933896 | tf_op jit(solution)/shard_map/ppermute | solution.py:356
  21.6 2.0 %collective-permute-start.5 = (f32[304,256]{1,0:T(8,128)S(1)}, f32[304,256]{1,0:T(8,128)S(1)}, u32[]{:S(2)}, u32[]{:S(2)}) collective-permute-start(f32[304,256]{1,0:T(8,128)S(1)} %collective-permute-done.1.refs_2_), channel_id=1, source_target_pairs={{0,1},{1,0},{2,3},{3,2},{4,5},{5,4},{6,7},{7,6},{8,9},{9,8},{10,11... | collective-permute-start | bytes 933896 | tf_op jit(solution)/shard_map/ppermute | solution.py:356
  22.1 2.0 %collective-permute-start.6 = (f32[304,256]{1,0:T(8,128)S(1)}, f32[304,256]{1,0:T(8,128)S(1)}, u32[]{:S(2)}, u32[]{:S(2)}) collective-permute-start(f32[304,256]{1,0:T(8,128)S(1)} %collective-permute-done.2.refs_3_), channel_id=1, source_target_pairs={{0,1},{1,0},{2,3},{3,2},{4,5},{5,4},{6,7},{7,6},{8,9},{9,8},{10,11... | collective-permute-start | bytes 933896 | tf_op jit(solution)/shard_map/ppermute | solution.py:356
  25.3 5.4 %collective-permute-start.7 = (f32[48,512]{1,0:T(8,128)S(1)}, f32[48,512]{1,0:T(8,128)S(1)}, u32[]{:S(2)}, u32[]{:S(2)}) collective-permute-start(f32[48,512]{1,0:T(8,128)S(1)} %get-tuple-element.94), channel_id=1, source_target_pairs={{0,8},{1,9},{2,10},{3,11},{4,12},{5,13},{6,14},{7,15}} | collective-permute-start | bytes 294920 | tf_op jit(solution)/shard_map/ppermute | solution.py:373
  30.7 3.4 %collective-permute-start.8 = (f32[48,512]{1,0:T(8,128)S(1)}, f32[48,512]{1,0:T(8,128)S(1)}, u32[]{:S(2)}, u32[]{:S(2)}) collective-permute-start(f32[48,512]{1,0:T(8,128)S(1)} %shard_map.83.refs_3_), channel_id=1, source_target_pairs={{8,16},{9,17},{10,18},{11,19},{12,20},{13,21},{14,22},{15,23}} | collective-permute-start | bytes 294920 | tf_op jit(solution)/shard_map/ppermute | solution.py:373
  32.4 9.2 %collective-permute-start.12 = (f32[512,256]{1,0:T(8,128)S(1)}, f32[512,256]{1,0:T(8,128)S(1)}, u32[]{:S(2)}, u32[]{:S(2)}) collective-permute-start(f32[512,256]{1,0:T(8,128)S(1)} %shard_map.89), channel_id=1, source_target_pairs={{0,4},{1,3},{2,6},{3,1},{4,0},{5,7},{6,2},{7,5},{8,12},{9,11},{10,... | collective-permute-start | bytes 1572872 | tf_op jit(solution)/shard_map/ppermute | solution.py:356
  34.1 7.5 %collective-permute-start.9 = (f32[48,512]{1,0:T(8,128)S(1)}, f32[48,512]{1,0:T(8,128)S(1)}, u32[]{:S(2)}, u32[]{:S(2)}) collective-permute-start(f32[48,512]{1,0:T(8,128)S(1)} %shard_map.84), channel_id=1, source_target_pairs={{16,24},{17,25},{18,26},{19,27},{20,28},{21,29},{22,30},{23,31}} | collective-permute-start | bytes 294920 | tf_op jit(solution)/shard_map/ppermute | solution.py:373
  34.8 2.0 %collective-permute-start.13 = (f32[512,256]{1,0:T(8,128)S(1)}, f32[512,256]{1,0:T(8,128)S(1)}, u32[]{:S(2)}, u32[]{:S(2)}) collective-permute-start(f32[512,256]{1,0:T(8,128)S(1)} %get-tuple-element.122.refs_0_), channel_id=1, source_target_pairs={{0,1},{1,0},{2,3},{3,2},{4,5},{5,4},{6,7},{7,6},{8,9},{9,8},{10,11... | collective-permute-start | bytes 1572872 | tf_op jit(solution)/shard_map/ppermute | solution.py:356
  34.9 2.6 %collective-permute-start.14 = (f32[512,256]{1,0:T(8,128)S(1)}, f32[512,256]{1,0:T(8,128)S(1)}, u32[]{:S(2)}, u32[]{:S(2)}) collective-permute-start(f32[512,256]{1,0:T(8,128)S(1)} %get-tuple-element.123.refs_1_), channel_id=1, source_target_pairs={{0,1},{1,0},{2,3},{3,2},{4,5},{5,4},{6,7},{7,6},{8,9},{9,8},{10,11... | collective-permute-start | bytes 1572872 | tf_op jit(solution)/shard_map/ppermute | solution.py:356
  35.4 2.9 %collective-permute-start.15 = (f32[512,256]{1,0:T(8,128)S(1)}, f32[512,256]{1,0:T(8,128)S(1)}, u32[]{:S(2)}, u32[]{:S(2)}) collective-permute-start(f32[512,256]{1,0:T(8,128)S(1)} %get-tuple-element.124.refs_2_), channel_id=1, source_target_pairs={{0,1},{1,0},{2,3},{3,2},{4,5},{5,4},{6,7},{7,6},{8,9},{9,8},{10,11... | collective-permute-start | bytes 1572872 | tf_op jit(solution)/shard_map/ppermute | solution.py:356
  41.6 1.9 %collective-permute-start.16 = (f32[512,256]{1,0:T(8,128)S(1)}, f32[512,256]{1,0:T(8,128)S(1)}, u32[]{:S(2)}, u32[]{:S(2)}) collective-permute-start(f32[512,256]{1,0:T(8,128)S(1)} %shard_map.92.refs_0_), channel_id=1, source_target_pairs={{0,1},{1,0},{2,3},{3,2},{4,5},{5,4},{6,7},{7,6},{8,9},{9,8},{10,11... | collective-permute-start | bytes 1572872 | tf_op jit(solution)/shard_map/ppermute | solution.py:356
  43.7 0.7 collective-permute-start.17
  44.5 0.7 collective-permute-start.18
  45.2 17.1 %collective-permute-start.22 = (f32[48,512]{1,0:T(8,128)S(1)}, f32[48,512]{1,0:T(8,128)S(1)}, u32[]{:S(2)}, u32[]{:S(2)}) collective-permute-start(f32[48,512]{1,0:T(8,128)S(1)} %shard_map.97.refs_4_), channel_id=1, source_target_pairs={{8,0},{9,1},{10,2},{11,3},{12,4},{13,5},{14,6},{15,7}} | collective-permute-start | bytes 294920 | tf_op jit(solution)/shard_map/ppermute | solution.py:373
  46.5 20.1 %collective-permute-start.19 = (f32[48,512]{1,0:T(8,128)S(1)}, f32[48,512]{1,0:T(8,128)S(1)}, u32[]{:S(2)}, u32[]{:S(2)}) collective-permute-start(f32[48,512]{1,0:T(8,128)S(1)} %get-tuple-element.135), channel_id=1, source_target_pairs={{0,2},{1,3},{2,0},{3,1},{4,6},{5,7},{6,4},{7,5},{8,10},{9,11},{10,... | collective-permute-start | bytes 294920 | tf_op jit(solution)/shard_map/ppermute | solution.py:356
  48.3 18.8 %collective-permute-start.20 = (f32[48,512]{1,0:T(8,128)S(1)}, f32[48,512]{1,0:T(8,128)S(1)}, u32[]{:S(2)}, u32[]{:S(2)}) collective-permute-start(f32[48,512]{1,0:T(8,128)S(1)} %get-tuple-element.136), channel_id=1, source_target_pairs={{0,4},{1,5},{2,6},{3,7},{4,0},{5,1},{6,2},{7,3},{8,12},{9,13},{10,... | collective-permute-start | bytes 294920 | tf_op jit(solution)/shard_map/ppermute | solution.py:356
  49.8 17.3 %collective-permute-start.21 = (f32[48,512]{1,0:T(8,128)S(1)}, f32[48,512]{1,0:T(8,128)S(1)}, u32[]{:S(2)}, u32[]{:S(2)}) collective-permute-start(f32[48,512]{1,0:T(8,128)S(1)} %get-tuple-element.137), channel_id=1, source_target_pairs={{0,6},{1,7},{2,4},{3,5},{4,2},{5,3},{6,0},{7,1},{8,14},{9,15},{10,... | collective-permute-start | bytes 294920 | tf_op jit(solution)/shard_map/ppermute | solution.py:356
  63.5 5.6 %collective-permute-start.25 = (f32[48,512]{1,0:T(8,128)S(1)}, f32[48,512]{1,0:T(8,128)S(1)}, u32[]{:S(2)}, u32[]{:S(2)}) collective-permute-start(f32[48,512]{1,0:T(8,128)S(1)} %get-tuple-element.153), channel_id=1, source_target_pairs={{0,6},{1,7},{2,4},{3,5},{4,2},{5,3},{6,0},{7,1},{8,14},{9,15},{10,... | collective-permute-start | bytes 294920 | tf_op jit(solution)/shard_map/ppermute | solution.py:356
  66.1 4.6 %collective-permute-start.23 = (f32[48,512]{1,0:T(8,128)S(1)}, f32[48,512]{1,0:T(8,128)S(1)}, u32[]{:S(2)}, u32[]{:S(2)}) collective-permute-start(f32[48,512]{1,0:T(8,128)S(1)} %get-tuple-element.151), channel_id=1, source_target_pairs={{0,2},{1,3},{2,0},{3,1},{4,6},{5,7},{6,4},{7,5},{8,10},{9,11},{10,... | collective-permute-start | bytes 294920 | tf_op jit(solution)/shard_map/ppermute | solution.py:356
  66.6 4.6 %collective-permute-start.24 = (f32[48,512]{1,0:T(8,128)S(1)}, f32[48,512]{1,0:T(8,128)S(1)}, u32[]{:S(2)}, u32[]{:S(2)}) collective-permute-start(f32[48,512]{1,0:T(8,128)S(1)} %get-tuple-element.152), channel_id=1, source_target_pairs={{0,4},{1,5},{2,6},{3,7},{4,0},{5,1},{6,2},{7,3},{8,12},{9,13},{10,... | collective-permute-start | bytes 294920 | tf_op jit(solution)/shard_map/ppermute | solution.py:356
  67.1 4.2 %collective-permute-start.26 = (f32[4,48,256]{2,1,0:T(8,128)S(1)}, f32[4,48,256]{2,1,0:T(8,128)S(1)}, u32[]{:S(2)}, u32[]{:S(2)}) collective-permute-start(f32[4,48,256]{2,1,0:T(8,128)S(1)} %shard_map.102), channel_id=1, source_target_pairs={{0,1},{1,0},{2,3},{3,2},{4,5},{5,4},{6,7},{7,6},{8,9},{9,8},{10,11... | collective-permute-start | bytes 589832 | tf_op jit(solution)/shard_map/ppermute | solution.py:356
  71.2 1.5 %collective-permute-start.27 = (f32[4,48,256]{2,1,0:T(8,128)S(1)}, f32[4,48,256]{2,1,0:T(8,128)S(1)}, u32[]{:S(2)}, u32[]{:S(2)}) collective-permute-start(f32[4,48,256]{2,1,0:T(8,128)S(1)} %shard_map.104), channel_id=1, source_target_pairs={{0,1},{1,0},{2,3},{3,2},{4,5},{5,4},{6,7},{7,6},{8,9},{9,8},{10,11... | collective-permute-start | bytes 589832 | tf_op jit(solution)/shard_map/ppermute | solution.py:356

commit v7 on v6

--- a/solution.py
+++ b/solution.py
@@ -365,12 +365,17 @@
         return swap(value, lambda t, r: t * rows + 1 - r)
 
     def hop(value, source, target):
-        pairs = [
-            ((source * GROUP + m) * rows + r, (target * GROUP + m) * rows + r)
-            for m in range(GROUP)
-            for r in range(rows)
-        ]
-        return lax.ppermute(value, both, pairs)
+        pairs = [(g, g ^ 1) for g in range(groups)] if source ^ 1 == target and groups % 2 == 0 else [(source, target)]
+        return lax.ppermute(
+            value,
+            both,
+            [
+                ((here * GROUP + m) * rows + r, (there * GROUP + m) * rows + r)
+                for here, there in pairs
+                for m in range(GROUP)
+                for r in range(rows)
+            ],
+        )
 
     def send_home(sent):
         return [across(sent[flip], flip) for flip in reversed(range(1, GROUP))][::-1]

time: 74.1 us -> 73.3 us (0.989)
  waiting for transfers between devices: 40.1 us -> 30.1 us
  starting transfers between devices: 25.4 us -> 34.7 us
    ppermute x6, starting transfers between devices: 7 us -> 16.5 us  [hop(): lax.ppermute(value, both, [((here * GROUP + m) * rows + r, (there * GROUP...]
    ppermute x6, waiting for transfers between devices: 14.6 us -> 6.79 us  [hop(): lax.ppermute(value, both, [((here * GROUP + m) * rows + r, (there * GROUP...]
    ppermute x22, waiting for transfers between devices: 25.5 us -> 23.3 us  [swap(): return lax.ppermute(value, both, pairs)]
  transfers between devices with their start and end apart: 28 -> 28, of which waited for: 17 -> 19; matrix products, arithmetic and copies ran while one was open for 0% -> 0% of each run, Pallas kernels for 5% -> 5%
where the time goes in v7:
time: 73.3 us; the launch traced here: 73.1 us
  starting transfers between devices  34.7 us (47%)
  waiting for transfers between devices  30.1 us (41%)
  Pallas kernels  6.41 us (9%)
  local copies, waits for them, and re-layouts  1.05 us (1%)
  between operations  0.81 us (1%)
    ppermute x22, waiting for transfers between devices, swap(): return lax.ppermute(value, both, pairs)  23.3 us
    ppermute x22, starting transfers between devices, swap(): return lax.ppermute(value, both, pairs)  18.3 us
    ppermute x6, starting transfers between devices, hop(): lax.ppermute(value, both, [((here * GROUP + m) * rows + r, (there * GROUP...  16.5 us
    ppermute x6, waiting for transfers between devices, hop(): lax.ppermute(value, both, [((here * GROUP + m) * rows + r, (there * GROUP...  6.79 us
    pallas_call x29, Pallas kernels, call(): pl.pallas_call(kernel, out_shape=[jax.ShapeDtypeStruct(shape, dtype) for...  6.41 us
  transfers between devices with their start and end apart: 28, of which 19 were waited for; matrix products, arithmetic and copies ran while one was open for 0% of the time, Pallas kernels for 5%

profile of v7, /device:TPU:0, one launch (start us, length us, event | category | flops | bytes accessed | tf_op | source)
XLA Modules:
  0.0 73.1 jit_solution(13145557556711083836)
XLA Ops:
  0.6 1.4 %shard_map.77 = (f32[304,256]{1,0:T(8,128)S(1)}, f32[304,256]{1,0:T(8,128)S(1)}, f32[304,256]{1,0:T(8,128)S(1)}, f32[48,256]{1,0:T(8,128)S(1)}, f32[8,256]{1,0:T(8,128)S(1)}) custom-call(f32[1,256]{1,0:T(1,128)} %bitcast.9, s32[1,256]{1,0:T(1,128)} %mask_hbm.1, f32[256,256]{1,0:T(8,128)} %bitcast.8, f32[256,384]{1,0:T(8,128)} %bitcast.7), custom_call_target="tpu_custom_call" | custom-call | bytes 2097152 | tf_op jit(solution)/shard_map/pallas_call | solution.py:26
  2.6 2.6 %collective-permute-start.1 = (f32[304,256]{1,0:T(8,128)S(1)}, f32[304,256]{1,0:T(8,128)S(1)}, u32[]{:S(2)}, u32[]{:S(2)}) collective-permute-start(f32[304,256]{1,0:T(8,128)S(1)} %get-tuple-element.80), channel_id=1, source_target_pairs={{0,4},{1,5},{2,6},{3,7},{4,0},{5,1},{6,2},{7,3},{8,12},{9,13},{10,... | collective-permute-start | bytes 933896 | tf_op jit(solution)/shard_map/ppermute | solution.py:356
  5.2 1.4 %collective-permute-start.2 = (f32[304,256]{1,0:T(8,128)S(1)}, f32[304,256]{1,0:T(8,128)S(1)}, u32[]{:S(2)}, u32[]{:S(2)}) collective-permute-start(f32[304,256]{1,0:T(8,128)S(1)} %get-tuple-element.81), channel_id=1, source_target_pairs={{0,6},{1,7},{2,4},{3,5},{4,2},{5,3},{6,0},{7,1},{8,14},{9,15},{10,... | collective-permute-start | bytes 933896 | tf_op jit(solution)/shard_map/ppermute | solution.py:356
  6.7 1.0 %copy-done.1 = f32[1,256,512]{2,1,0:T(8,128)S(1)} copy-done((f32[1,256,512]{2,1,0:T(8,128)S(1)}, f32[1,256,512]{2,1,0:T(8,128)}, u32[]{:S(2)}) %copy-start.1) | copy-done | bytes 524312
  8.0 2.0 %collective-permute-start.11 = (f32[512,256]{1,0:T(8,128)S(1)}, f32[512,256]{1,0:T(8,128)S(1)}, u32[]{:S(2)}, u32[]{:S(2)}) collective-permute-start(f32[512,256]{1,0:T(8,128)S(1)} %shard_map.79.refs_0_), channel_id=1, source_target_pairs={{0,4},{1,5},{2,6},{3,7},{4,0},{5,1},{6,2},{7,3},{8,12},{9,13},{10,... | collective-permute-start | bytes 1572872 | tf_op jit(solution)/shard_map/ppermute | solution.py:356
  10.1 1.5 %collective-permute-start.10 = (f32[512,256]{1,0:T(8,128)S(1)}, f32[512,256]{1,0:T(8,128)S(1)}, u32[]{:S(2)}, u32[]{:S(2)}) collective-permute-start(f32[512,256]{1,0:T(8,128)S(1)} %shard_map.79.refs_0_), channel_id=1, source_target_pairs={{0,2},{1,3},{2,0},{3,1},{4,6},{5,7},{6,4},{7,5},{8,10},{9,11},{10,... | collective-permute-start | bytes 1572872 | tf_op jit(solution)/shard_map/ppermute | solution.py:356
  11.8 8.2 %collective-permute-done.1.refs_2_ = f32[304,256]{1,0:T(8,128)S(1)} collective-permute-done((f32[304,256]{1,0:T(8,128)S(1)}, f32[304,256]{1,0:T(8,128)S(1)}, u32[]{:S(2)}, u32[]{:S(2)}) %collective-permute-start.1) | collective-permute-done | bytes 311328 | tf_op jit(solution)/shard_map/ppermute | solution.py:356
  20.1 1.5 %collective-permute-done.refs_1_ = f32[304,256]{1,0:T(8,128)S(1)} collective-permute-done((f32[304,256]{1,0:T(8,128)S(1)}, f32[304,256]{1,0:T(8,128)S(1)}, u32[]{:S(2)}, u32[]{:S(2)}) %collective-permute-start) | collective-permute-done | bytes 311328 | tf_op jit(solution)/shard_map/ppermute | solution.py:356
  22.1 1.1 %collective-permute-done.4.refs_5_ = f32[304,256]{1,0:T(8,128)S(1)} collective-permute-done((f32[304,256]{1,0:T(8,128)S(1)}, f32[304,256]{1,0:T(8,128)S(1)}, u32[]{:S(2)}, u32[]{:S(2)}) %collective-permute-start.4) | collective-permute-done | bytes 311328 | tf_op jit(solution)/shard_map/ppermute | solution.py:356
  24.4 0.9 %shard_map.81 = (f32[4,48,512]{2,1,0:T(8,128)S(1)}, f32[48,512]{1,0:T(8,128)S(1)}, f32[48,512]{1,0:T(8,128)S(1)}, f32[48,512]{1,0:T(8,128)S(1)}, f32[48,512]{1,0:T(8,128)S(1)}, /*index=5*/f32[48,512]{1,0:T(8,128)S(1)}) custom-call(f32[48,512]{1,0:T(8,128)S(1)} %shard_map.78.start_ref, f32[8,256]{1,0:T(8,128)S(1)} %get-tuple-element.85.coef_ref, ...), custom_call_target="tpu_custom_call" | custom-call | bytes 2097152 | tf_op jit(solution)/shard_map/pallas_call | solution.py:26
  25.3 1.2 %collective-permute-start.7 = (f32[48,512]{1,0:T(8,128)S(1)}, f32[48,512]{1,0:T(8,128)S(1)}, u32[]{:S(2)}, u32[]{:S(2)}) collective-permute-start(f32[48,512]{1,0:T(8,128)S(1)} %get-tuple-element.94), channel_id=1, source_target_pairs={{0,8},{1,9},{2,10},{3,11},{4,12},{5,13},{6,14},{7,15},{8,0},{9,1},... | collective-permute-start | bytes 294920 | tf_op jit(solution)/shard_map/ppermute | solution.py:369
  26.5 3.7 %collective-permute-done.7.start_ref = f32[48,512]{1,0:T(8,128)S(1)} collective-permute-done((f32[48,512]{1,0:T(8,128)S(1)}, f32[48,512]{1,0:T(8,128)S(1)}, u32[]{:S(2)}, u32[]{:S(2)}) %collective-permute-start.7) | collective-permute-done | bytes 98336 | tf_op jit(solution)/shard_map/ppermute | solution.py:369
  30.2 0.7 collective-permute-start.8
  31.0 1.3 %collective-permute-done.10.refs_1_ = f32[512,256]{1,0:T(8,128)S(1)} collective-permute-done((f32[512,256]{1,0:T(8,128)S(1)}, f32[512,256]{1,0:T(8,128)S(1)}, u32[]{:S(2)}, u32[]{:S(2)}) %collective-permute-start.10) | collective-permute-done | bytes 524320 | tf_op jit(solution)/shard_map/ppermute | solution.py:356
  32.4 1.8 %collective-permute-start.12 = (f32[512,256]{1,0:T(8,128)S(1)}, f32[512,256]{1,0:T(8,128)S(1)}, u32[]{:S(2)}, u32[]{:S(2)}) collective-permute-start(f32[512,256]{1,0:T(8,128)S(1)} %shard_map.89), channel_id=1, source_target_pairs={{0,4},{1,3},{2,6},{3,1},{4,0},{5,7},{6,2},{7,5},{8,12},{9,11},{10,... | collective-permute-start | bytes 1572872 | tf_op jit(solution)/shard_map/ppermute | solution.py:356
  34.1 3.4 %collective-permute-start.9 = (f32[48,512]{1,0:T(8,128)S(1)}, f32[48,512]{1,0:T(8,128)S(1)}, u32[]{:S(2)}, u32[]{:S(2)}) collective-permute-start(f32[48,512]{1,0:T(8,128)S(1)} %shard_map.84), channel_id=1, source_target_pairs={{0,8},{1,9},{2,10},{3,11},{4,12},{5,13},{6,14},{7,15},{8,0},{9,1},... | collective-permute-start | bytes 294920 | tf_op jit(solution)/shard_map/ppermute | solution.py:369
  38.0 1.4 %collective-permute-done.13.refs_3_ = f32[512,256]{1,0:T(8,128)S(1)} collective-permute-done((f32[512,256]{1,0:T(8,128)S(1)}, f32[512,256]{1,0:T(8,128)S(1)}, u32[]{:S(2)}, u32[]{:S(2)}) %collective-permute-start.13) | collective-permute-done | bytes 524320 | tf_op jit(solution)/shard_map/ppermute | solution.py:356
  39.4 0.7 %collective-permute-done.14.refs_4_ = f32[512,256]{1,0:T(8,128)S(1)} collective-permute-done((f32[512,256]{1,0:T(8,128)S(1)}, f32[512,256]{1,0:T(8,128)S(1)}, u32[]{:S(2)}, u32[]{:S(2)}) %collective-permute-start.14) | collective-permute-done | bytes 524320 | tf_op jit(solution)/shard_map/ppermute | solution.py:356
  40.2 0.7 %collective-permute-done.15.refs_5_ = f32[512,256]{1,0:T(8,128)S(1)} collective-permute-done((f32[512,256]{1,0:T(8,128)S(1)}, f32[512,256]{1,0:T(8,128)S(1)}, u32[]{:S(2)}, u32[]{:S(2)}) %collective-permute-start.15) | collective-permute-done | bytes 524320 | tf_op jit(solution)/shard_map/ppermute | solution.py:356
  41.7 1.8 %collective-permute-done.16.refs_1_ = f32[512,256]{1,0:T(8,128)S(1)} collective-permute-done((f32[512,256]{1,0:T(8,128)S(1)}, f32[512,256]{1,0:T(8,128)S(1)}, u32[]{:S(2)}, u32[]{:S(2)}) %collective-permute-start.16) | collective-permute-done | bytes 524320 | tf_op jit(solution)/shard_map/ppermute | solution.py:356
  43.7 2.7 %collective-permute-start.17 = (f32[48,512]{1,0:T(8,128)S(1)}, f32[48,512]{1,0:T(8,128)S(1)}, u32[]{:S(2)}, u32[]{:S(2)}) collective-permute-start(f32[48,512]{1,0:T(8,128)S(1)} %get-tuple-element.130), channel_id=1, source_target_pairs={{0,8},{1,9},{2,10},{3,11},{4,12},{5,13},{6,14},{7,15},{8,0},{9,1},... | collective-permute-start | bytes 294920 | tf_op jit(solution)/shard_map/ppermute | solution.py:369
  46.4 3.1 %collective-permute-done.17.start_ref = f32[48,512]{1,0:T(8,128)S(1)} collective-permute-done((f32[48,512]{1,0:T(8,128)S(1)}, f32[48,512]{1,0:T(8,128)S(1)}, u32[]{:S(2)}, u32[]{:S(2)}) %collective-permute-start.17) | collective-permute-done | bytes 98336 | tf_op jit(solution)/shard_map/ppermute | solution.py:369
  50.2 7.9 %collective-permute-start.22 = (f32[48,512]{1,0:T(8,128)S(1)}, f32[48,512]{1,0:T(8,128)S(1)}, u32[]{:S(2)}, u32[]{:S(2)}) collective-permute-start(f32[48,512]{1,0:T(8,128)S(1)} %shard_map.97.refs_4_), channel_id=1, source_target_pairs={{0,8},{1,9},{2,10},{3,11},{4,12},{5,13},{6,14},{7,15},{8,0},{9,1},... | collective-permute-start | bytes 294920 | tf_op jit(solution)/shard_map/ppermute | solution.py:369
  58.1 1.5 %collective-permute-start.19 = (f32[48,512]{1,0:T(8,128)S(1)}, f32[48,512]{1,0:T(8,128)S(1)}, u32[]{:S(2)}, u32[]{:S(2)}) collective-permute-start(f32[48,512]{1,0:T(8,128)S(1)} %get-tuple-element.135), channel_id=1, source_target_pairs={{0,2},{1,3},{2,0},{3,1},{4,6},{5,7},{6,4},{7,5},{8,10},{9,11},{10,... | collective-permute-start | bytes 294920 | tf_op jit(solution)/shard_map/ppermute | solution.py:356
  59.6 1.5 %collective-permute-start.20 = (f32[48,512]{1,0:T(8,128)S(1)}, f32[48,512]{1,0:T(8,128)S(1)}, u32[]{:S(2)}, u32[]{:S(2)}) collective-permute-start(f32[48,512]{1,0:T(8,128)S(1)} %get-tuple-element.136), channel_id=1, source_target_pairs={{0,4},{1,5},{2,6},{3,7},{4,0},{5,1},{6,2},{7,3},{8,12},{9,13},{10,... | collective-permute-start | bytes 294920 | tf_op jit(solution)/shard_map/ppermute | solution.py:356
  61.6 1.2 %shard_map.101 = (f32[48,512]{1,0:T(8,128)S(1)}, f32[48,512]{1,0:T(8,128)S(1)}, f32[48,512]{1,0:T(8,128)S(1)}, f32[48,512]{1,0:T(8,128)S(1)}) custom-call(f32[48,512]{1,0:T(8,128)S(1)} %collective-permute-done.22.start_ref, f32[8,256]{1,0:T(8,128)S(1)} %get-tuple-element.85.coef_ref, ...), custom_call_target="tpu_custom_call", output_to_operand_aliasing={{0}: (5, {}), {1}: (6, {}), {2}: (7, {}), {3}: (8, {})} | custom-call | bytes 2097152 | tf_op jit(solution)/shard_map/pallas_call | solution.py:26
  62.8 2.5 %collective-permute-start.25 = (f32[48,512]{1,0:T(8,128)S(1)}, f32[48,512]{1,0:T(8,128)S(1)}, u32[]{:S(2)}, u32[]{:S(2)}) collective-permute-start(f32[48,512]{1,0:T(8,128)S(1)} %get-tuple-element.153), channel_id=1, source_target_pairs={{0,6},{1,7},{2,4},{3,5},{4,2},{5,3},{6,0},{7,1},{8,14},{9,15},{10,... | collective-permute-start | bytes 294920 | tf_op jit(solution)/shard_map/ppermute | solution.py:356
  66.4 1.3 %collective-permute-done.21.refs_3_ = f32[48,512]{1,0:T(8,128)S(1)} collective-permute-done((f32[48,512]{1,0:T(8,128)S(1)}, f32[48,512]{1,0:T(8,128)S(1)}, u32[]{:S(2)}, u32[]{:S(2)}) %collective-permute-start.21) | collective-permute-done | bytes 98336 | tf_op jit(solution)/shard_map/ppermute | solution.py:356
  67.8 1.0 %collective-permute-done.25.refs_1_.refs_7_ = f32[48,512]{1,0:T(8,128)S(1)} collective-permute-done((f32[48,512]{1,0:T(8,128)S(1)}, f32[48,512]{1,0:T(8,128)S(1)}, u32[]{:S(2)}, u32[]{:S(2)}) %collective-permute-start.25) | collective-permute-done | bytes 98336 | tf_op jit(solution)/shard_map/ppermute | solution.py:356
  68.8 1.1 %collective-permute-done.23.refs_0_.refs_5_ = f32[48,512]{1,0:T(8,128)S(1)} collective-permute-done((f32[48,512]{1,0:T(8,128)S(1)}, f32[48,512]{1,0:T(8,128)S(1)}, u32[]{:S(2)}, u32[]{:S(2)}) %collective-permute-start.23) | collective-permute-done | bytes 98336 | tf_op jit(solution)/shard_map/ppermute | solution.py:356
  70.6 1.4 %collective-permute-done.27.refs_9_ = f32[4,48,256]{2,1,0:T(8,128)S(1)} collective-permute-done((f32[4,48,256]{2,1,0:T(8,128)S(1)}, f32[4,48,256]{2,1,0:T(8,128)S(1)}, u32[]{:S(2)}, u32[]{:S(2)}) %collective-permute-start.27) | collective-permute-done | bytes 196640 | tf_op jit(solution)/shard_map/ppermute | solution.py:356
  72.0 1.1 %shard_map.105 = (f32[256,384]{1,0:T(8,128)}, f32[256,384]{1,0:T(8,128)}) custom-call(f32[48,512]{1,0:T(8,128)S(1)} %get-tuple-element.134.refs_0_, f32[48,512]{1,0:T(8,128)S(1)} %collective-permute-done.19.refs_1_, f32[48,512]{1,0:T(8,128)S(1)} %collective-permute-done.20.refs_2_, f32[48,512]{1,0:T(8,128)S(1)} %collective-permute-done.21.refs_3_, ...), custom_call_target="tpu_custom_call" | custom-call | bytes 2097152 | tf_op jit(solution)/shard_map/pallas_call | solution.py:26
  (57 shorter events, 7.6 us)
Async XLA Ops:
  0.6 10.9 %copy-start = (f32[512,384]{1,0:T(8,128)S(1)}, f32[512,384]{1,0:T(8,128)}, u32[]{:S(2)}) copy-start(f32[512,384]{1,0:T(8,128)} %prior_ref.1) | copy-start | bytes 2359300
  2.1 8.0 %collective-permute-start.3 = (f32[304,256]{1,0:T(8,128)S(1)}, f32[304,256]{1,0:T(8,128)S(1)}, u32[]{:S(2)}, u32[]{:S(2)}) collective-permute-start(f32[304,256]{1,0:T(8,128)S(1)} %get-tuple-element.79.refs_0_), channel_id=1, source_target_pairs={{0,1},{1,0},{2,3},{3,2},{4,5},{5,4},{6,7},{7,6},{8,9},{9,8},{10,11... | collective-permute-start | bytes 933896 | tf_op jit(solution)/shard_map/ppermute | solution.py:356
  2.6 17.5 %collective-permute-start.1 = (f32[304,256]{1,0:T(8,128)S(1)}, f32[304,256]{1,0:T(8,128)S(1)}, u32[]{:S(2)}, u32[]{:S(2)}) collective-permute-start(f32[304,256]{1,0:T(8,128)S(1)} %get-tuple-element.80), channel_id=1, source_target_pairs={{0,4},{1,5},{2,6},{3,7},{4,0},{5,1},{6,2},{7,3},{8,12},{9,13},{10,... | collective-permute-start | bytes 933896 | tf_op jit(solution)/shard_map/ppermute | solution.py:356
  5.2 14.9 %collective-permute-start.2 = (f32[304,256]{1,0:T(8,128)S(1)}, f32[304,256]{1,0:T(8,128)S(1)}, u32[]{:S(2)}, u32[]{:S(2)}) collective-permute-start(f32[304,256]{1,0:T(8,128)S(1)} %get-tuple-element.81), channel_id=1, source_target_pairs={{0,6},{1,7},{2,4},{3,5},{4,2},{5,3},{6,0},{7,1},{8,14},{9,15},{10,... | collective-permute-start | bytes 933896 | tf_op jit(solution)/shard_map/ppermute | solution.py:356
  6.6 15.0 %collective-permute-start = (f32[304,256]{1,0:T(8,128)S(1)}, f32[304,256]{1,0:T(8,128)S(1)}, u32[]{:S(2)}, u32[]{:S(2)}) collective-permute-start(f32[304,256]{1,0:T(8,128)S(1)} %get-tuple-element.79.refs_0_), channel_id=1, source_target_pairs={{0,2},{1,3},{2,0},{3,1},{4,6},{5,7},{6,4},{7,5},{8,10},{9,11},{10,... | collective-permute-start | bytes 933896 | tf_op jit(solution)/shard_map/ppermute | solution.py:356
  6.7 1.0 %copy-start.1 = (f32[1,256,512]{2,1,0:T(8,128)S(1)}, f32[1,256,512]{2,1,0:T(8,128)}, u32[]{:S(2)}) copy-start(f32[1,256,512]{2,1,0:T(8,128)} %param.11) | copy-start | bytes 1572868
  8.0 23.0 %collective-permute-start.11 = (f32[512,256]{1,0:T(8,128)S(1)}, f32[512,256]{1,0:T(8,128)S(1)}, u32[]{:S(2)}, u32[]{:S(2)}) collective-permute-start(f32[512,256]{1,0:T(8,128)S(1)} %shard_map.79.refs_0_), channel_id=1, source_target_pairs={{0,4},{1,5},{2,6},{3,7},{4,0},{5,1},{6,2},{7,3},{8,12},{9,13},{10,... | collective-permute-start | bytes 1572872 | tf_op jit(solution)/shard_map/ppermute | solution.py:356
  10.1 22.3 %collective-permute-start.10 = (f32[512,256]{1,0:T(8,128)S(1)}, f32[512,256]{1,0:T(8,128)S(1)}, u32[]{:S(2)}, u32[]{:S(2)}) collective-permute-start(f32[512,256]{1,0:T(8,128)S(1)} %shard_map.79.refs_0_), channel_id=1, source_target_pairs={{0,2},{1,3},{2,0},{3,1},{4,6},{5,7},{6,4},{7,5},{8,10},{9,11},{10,... | collective-permute-start | bytes 1572872 | tf_op jit(solution)/shard_map/ppermute | solution.py:356
  21.6 1.6 %collective-permute-start.4 = (f32[304,256]{1,0:T(8,128)S(1)}, f32[304,256]{1,0:T(8,128)S(1)}, u32[]{:S(2)}, u32[]{:S(2)}) collective-permute-start(f32[304,256]{1,0:T(8,128)S(1)} %collective-permute-done.refs_1_), channel_id=1, source_target_pairs={{0,1},{1,0},{2,3},{3,2},{4,5},{5,4},{6,7},{7,6},{8,9},{9,8},{10,11... | collective-permute-start | bytes 933896 | tf_op jit(solution)/shard_map/ppermute | solution.py:356
  21.6 2.0 %collective-permute-start.5 = (f32[304,256]{1,0:T(8,128)S(1)}, f32[304,256]{1,0:T(8,128)S(1)}, u32[]{:S(2)}, u32[]{:S(2)}) collective-permute-start(f32[304,256]{1,0:T(8,128)S(1)} %collective-permute-done.1.refs_2_), channel_id=1, source_target_pairs={{0,1},{1,0},{2,3},{3,2},{4,5},{5,4},{6,7},{7,6},{8,9},{9,8},{10,11... | collective-permute-start | bytes 933896 | tf_op jit(solution)/shard_map/ppermute | solution.py:356
  22.1 2.0 %collective-permute-start.6 = (f32[304,256]{1,0:T(8,128)S(1)}, f32[304,256]{1,0:T(8,128)S(1)}, u32[]{:S(2)}, u32[]{:S(2)}) collective-permute-start(f32[304,256]{1,0:T(8,128)S(1)} %collective-permute-done.2.refs_3_), channel_id=1, source_target_pairs={{0,1},{1,0},{2,3},{3,2},{4,5},{5,4},{6,7},{7,6},{8,9},{9,8},{10,11... | collective-permute-start | bytes 933896 | tf_op jit(solution)/shard_map/ppermute | solution.py:356
  25.3 4.9 %collective-permute-start.7 = (f32[48,512]{1,0:T(8,128)S(1)}, f32[48,512]{1,0:T(8,128)S(1)}, u32[]{:S(2)}, u32[]{:S(2)}) collective-permute-start(f32[48,512]{1,0:T(8,128)S(1)} %get-tuple-element.94), channel_id=1, source_target_pairs={{0,8},{1,9},{2,10},{3,11},{4,12},{5,13},{6,14},{7,15},{8,0},{9,1},... | collective-permute-start | bytes 294920 | tf_op jit(solution)/shard_map/ppermute | solution.py:369
  30.2 3.9 %collective-permute-start.8 = (f32[48,512]{1,0:T(8,128)S(1)}, f32[48,512]{1,0:T(8,128)S(1)}, u32[]{:S(2)}, u32[]{:S(2)}) collective-permute-start(f32[48,512]{1,0:T(8,128)S(1)} %shard_map.83.refs_3_), channel_id=1, source_target_pairs={{8,16},{9,17},{10,18},{11,19},{12,20},{13,21},{14,22},{15,23}} | collective-permute-start | bytes 294920 | tf_op jit(solution)/shard_map/ppermute | solution.py:369
  32.4 9.2 %collective-permute-start.12 = (f32[512,256]{1,0:T(8,128)S(1)}, f32[512,256]{1,0:T(8,128)S(1)}, u32[]{:S(2)}, u32[]{:S(2)}) collective-permute-start(f32[512,256]{1,0:T(8,128)S(1)} %shard_map.89), channel_id=1, source_target_pairs={{0,4},{1,3},{2,6},{3,1},{4,0},{5,7},{6,2},{7,5},{8,12},{9,11},{10,... | collective-permute-start | bytes 1572872 | tf_op jit(solution)/shard_map/ppermute | solution.py:356
  34.1 7.6 %collective-permute-start.9 = (f32[48,512]{1,0:T(8,128)S(1)}, f32[48,512]{1,0:T(8,128)S(1)}, u32[]{:S(2)}, u32[]{:S(2)}) collective-permute-start(f32[48,512]{1,0:T(8,128)S(1)} %shard_map.84), channel_id=1, source_target_pairs={{0,8},{1,9},{2,10},{3,11},{4,12},{5,13},{6,14},{7,15},{8,0},{9,1},... | collective-permute-start | bytes 294920 | tf_op jit(solution)/shard_map/ppermute | solution.py:369
  37.5 1.9 %collective-permute-start.13 = (f32[512,256]{1,0:T(8,128)S(1)}, f32[512,256]{1,0:T(8,128)S(1)}, u32[]{:S(2)}, u32[]{:S(2)}) collective-permute-start(f32[512,256]{1,0:T(8,128)S(1)} %get-tuple-element.122.refs_0_), channel_id=1, source_target_pairs={{0,1},{1,0},{2,3},{3,2},{4,5},{5,4},{6,7},{7,6},{8,9},{9,8},{10,11... | collective-permute-start | bytes 1572872 | tf_op jit(solution)/shard_map/ppermute | solution.py:356
  37.5 2.7 %collective-permute-start.14 = (f32[512,256]{1,0:T(8,128)S(1)}, f32[512,256]{1,0:T(8,128)S(1)}, u32[]{:S(2)}, u32[]{:S(2)}) collective-permute-start(f32[512,256]{1,0:T(8,128)S(1)} %get-tuple-element.123.refs_1_), channel_id=1, source_target_pairs={{0,1},{1,0},{2,3},{3,2},{4,5},{5,4},{6,7},{7,6},{8,9},{9,8},{10,11... | collective-permute-start | bytes 1572872 | tf_op jit(solution)/shard_map/ppermute | solution.py:356
  38.0 2.9 %collective-permute-start.15 = (f32[512,256]{1,0:T(8,128)S(1)}, f32[512,256]{1,0:T(8,128)S(1)}, u32[]{:S(2)}, u32[]{:S(2)}) collective-permute-start(f32[512,256]{1,0:T(8,128)S(1)} %get-tuple-element.124.refs_2_), channel_id=1, source_target_pairs={{0,1},{1,0},{2,3},{3,2},{4,5},{5,4},{6,7},{7,6},{8,9},{9,8},{10,11... | collective-permute-start | bytes 1572872 | tf_op jit(solution)/shard_map/ppermute | solution.py:356
  41.6 1.9 %collective-permute-start.16 = (f32[512,256]{1,0:T(8,128)S(1)}, f32[512,256]{1,0:T(8,128)S(1)}, u32[]{:S(2)}, u32[]{:S(2)}) collective-permute-start(f32[512,256]{1,0:T(8,128)S(1)} %shard_map.92.refs_0_), channel_id=1, source_target_pairs={{0,1},{1,0},{2,3},{3,2},{4,5},{5,4},{6,7},{7,6},{8,9},{9,8},{10,11... | collective-permute-start | bytes 1572872 | tf_op jit(solution)/shard_map/ppermute | solution.py:356
  43.7 5.8 %collective-permute-start.17 = (f32[48,512]{1,0:T(8,128)S(1)}, f32[48,512]{1,0:T(8,128)S(1)}, u32[]{:S(2)}, u32[]{:S(2)}) collective-permute-start(f32[48,512]{1,0:T(8,128)S(1)} %get-tuple-element.130), channel_id=1, source_target_pairs={{0,8},{1,9},{2,10},{3,11},{4,12},{5,13},{6,14},{7,15},{8,0},{9,1},... | collective-permute-start | bytes 294920 | tf_op jit(solution)/shard_map/ppermute | solution.py:369
  49.5 0.7 collective-permute-start.18
  50.2 11.4 %collective-permute-start.22 = (f32[48,512]{1,0:T(8,128)S(1)}, f32[48,512]{1,0:T(8,128)S(1)}, u32[]{:S(2)}, u32[]{:S(2)}) collective-permute-start(f32[48,512]{1,0:T(8,128)S(1)} %shard_map.97.refs_4_), channel_id=1, source_target_pairs={{0,8},{1,9},{2,10},{3,11},{4,12},{5,13},{6,14},{7,15},{8,0},{9,1},... | collective-permute-start | bytes 294920 | tf_op jit(solution)/shard_map/ppermute | solution.py:369
  58.1 7.7 %collective-permute-start.19 = (f32[48,512]{1,0:T(8,128)S(1)}, f32[48,512]{1,0:T(8,128)S(1)}, u32[]{:S(2)}, u32[]{:S(2)}) collective-permute-start(f32[48,512]{1,0:T(8,128)S(1)} %get-tuple-element.135), channel_id=1, source_target_pairs={{0,2},{1,3},{2,0},{3,1},{4,6},{5,7},{6,4},{7,5},{8,10},{9,11},{10,... | collective-permute-start | bytes 294920 | tf_op jit(solution)/shard_map/ppermute | solution.py:356
  59.6 6.8 %collective-permute-start.20 = (f32[48,512]{1,0:T(8,128)S(1)}, f32[48,512]{1,0:T(8,128)S(1)}, u32[]{:S(2)}, u32[]{:S(2)}) collective-permute-start(f32[48,512]{1,0:T(8,128)S(1)} %get-tuple-element.136), channel_id=1, source_target_pairs={{0,4},{1,5},{2,6},{3,7},{4,0},{5,1},{6,2},{7,3},{8,12},{9,13},{10,... | collective-permute-start | bytes 294920 | tf_op jit(solution)/shard_map/ppermute | solution.py:356
  61.1 6.5 %collective-permute-start.21 = (f32[48,512]{1,0:T(8,128)S(1)}, f32[48,512]{1,0:T(8,128)S(1)}, u32[]{:S(2)}, u32[]{:S(2)}) collective-permute-start(f32[48,512]{1,0:T(8,128)S(1)} %get-tuple-element.137), channel_id=1, source_target_pairs={{0,6},{1,7},{2,4},{3,5},{4,2},{5,3},{6,0},{7,1},{8,14},{9,15},{10,... | collective-permute-start | bytes 294920 | tf_op jit(solution)/shard_map/ppermute | solution.py:356
  62.8 6.0 %collective-permute-start.25 = (f32[48,512]{1,0:T(8,128)S(1)}, f32[48,512]{1,0:T(8,128)S(1)}, u32[]{:S(2)}, u32[]{:S(2)}) collective-permute-start(f32[48,512]{1,0:T(8,128)S(1)} %get-tuple-element.153), channel_id=1, source_target_pairs={{0,6},{1,7},{2,4},{3,5},{4,2},{5,3},{6,0},{7,1},{8,14},{9,15},{10,... | collective-permute-start | bytes 294920 | tf_op jit(solution)/shard_map/ppermute | solution.py:356
  65.3 4.6 %collective-permute-start.23 = (f32[48,512]{1,0:T(8,128)S(1)}, f32[48,512]{1,0:T(8,128)S(1)}, u32[]{:S(2)}, u32[]{:S(2)}) collective-permute-start(f32[48,512]{1,0:T(8,128)S(1)} %get-tuple-element.151), channel_id=1, source_target_pairs={{0,2},{1,3},{2,0},{3,1},{4,6},{5,7},{6,4},{7,5},{8,10},{9,11},{10,... | collective-permute-start | bytes 294920 | tf_op jit(solution)/shard_map/ppermute | solution.py:356
  65.8 4.6 %collective-permute-start.24 = (f32[48,512]{1,0:T(8,128)S(1)}, f32[48,512]{1,0:T(8,128)S(1)}, u32[]{:S(2)}, u32[]{:S(2)}) collective-permute-start(f32[48,512]{1,0:T(8,128)S(1)} %get-tuple-element.152), channel_id=1, source_target_pairs={{0,4},{1,5},{2,6},{3,7},{4,0},{5,1},{6,2},{7,3},{8,12},{9,13},{10,... | collective-permute-start | bytes 294920 | tf_op jit(solution)/shard_map/ppermute | solution.py:356
  67.7 2.9 %collective-permute-start.26 = (f32[4,48,256]{2,1,0:T(8,128)S(1)}, f32[4,48,256]{2,1,0:T(8,128)S(1)}, u32[]{:S(2)}, u32[]{:S(2)}) collective-permute-start(f32[4,48,256]{2,1,0:T(8,128)S(1)} %shard_map.102), channel_id=1, source_target_pairs={{0,1},{1,0},{2,3},{3,2},{4,5},{5,4},{6,7},{7,6},{8,9},{9,8},{10,11... | collective-permute-start | bytes 589832 | tf_op jit(solution)/shard_map/ppermute | solution.py:356
  70.5 1.5 %collective-permute-start.27 = (f32[4,48,256]{2,1,0:T(8,128)S(1)}, f32[4,48,256]{2,1,0:T(8,128)S(1)}, u32[]{:S(2)}, u32[]{:S(2)}) collective-permute-start(f32[4,48,256]{2,1,0:T(8,128)S(1)} %shard_map.104), channel_id=1, source_target_pairs={{0,1},{1,0},{2,3},{3,2},{4,5},{5,4},{6,7},{7,6},{8,9},{9,8},{10,11... | collective-permute-start | bytes 589832 | tf_op jit(solution)/shard_map/ppermute | solution.py:356

commit v8 on v7

--- a/solution.py
+++ b/solution.py
@@ -410,10 +410,9 @@
     )
     (turned_gain,) = pieces
     gain_x, gain_y = across(turned_gain, 1), across(turned_gain, 2)
-    own_far, prior = lax.optimization_barrier((neighbour(messages[0]), prior))
-    *near, own_far, prior, turned_gain = lax.optimization_barrier((*near, own_far, prior, turned_gain))
-    far = [own_far] + [neighbour(value) for value in near]
+    *near, prior, turned_gain = lax.optimization_barrier((*near, prior, turned_gain))
     near = [messages[0], *near]
+    far = [neighbour(value) for value in near]
     high, low, obs = call(
         functools.partial(gather_kernel, range(GROUP), share, sites),
         (*near, *far, own_obs),

time: 73.3 us -> 73.6 us (level)
    ppermute x22, waiting for transfers between devices: 23.3 us -> 22.5 us  [swap(): return lax.ppermute(value, both, pairs)]
  transfers between devices with their start and end apart: 28 -> 28, of which waited for: 19 -> 16; matrix products, arithmetic and copies ran while one was open for 0% -> 0% of each run, Pallas kernels for 5% -> 5%
where the time goes in v8:
time: 73.6 us; the launch traced here: 73.4 us
  starting transfers between devices  35.3 us (48%)
  waiting for transfers between devices  29.8 us (40%)
  Pallas kernels  6.41 us (9%)
  local copies, waits for them, and re-layouts  1.05 us (1%)
  between operations  0.86 us (1%)
    ppermute x22, waiting for transfers between devices, swap(): return lax.ppermute(value, both, pairs)  22.5 us
    ppermute x22, starting transfers between devices, swap(): return lax.ppermute(value, both, pairs)  18.7 us
    ppermute x6, starting transfers between devices, hop(): lax.ppermute(value, both, [((here * GROUP + m) * rows + r, (there * GROUP...  16.6 us
    ppermute x6, waiting for transfers between devices, hop(): lax.ppermute(value, both, [((here * GROUP + m) * rows + r, (there * GROUP...  7.24 us
    pallas_call x29, Pallas kernels, call(): pl.pallas_call(kernel, out_shape=[jax.ShapeDtypeStruct(shape, dtype) for...  6.41 us
  transfers between devices with their start and end apart: 28, of which 16 were waited for; matrix products, arithmetic and copies ran while one was open for 0% of the time, Pallas kernels for 5%

profile of v8, /device:TPU:0, one launch (start us, length us, event | category | flops | bytes accessed | tf_op | source)
XLA Modules:
  0.0 73.4 jit_solution(10639410110558527052)
XLA Ops:
  0.6 1.4 %shard_map.77 = (f32[304,256]{1,0:T(8,128)S(1)}, f32[304,256]{1,0:T(8,128)S(1)}, f32[304,256]{1,0:T(8,128)S(1)}, f32[48,256]{1,0:T(8,128)S(1)}, f32[8,256]{1,0:T(8,128)S(1)}) custom-call(f32[1,256]{1,0:T(1,128)} %bitcast.9, s32[1,256]{1,0:T(1,128)} %mask_hbm.1, f32[256,256]{1,0:T(8,128)} %bitcast.8, f32[256,384]{1,0:T(8,128)} %bitcast.7), custom_call_target="tpu_custom_call" | custom-call | bytes 2097152 | tf_op jit(solution)/shard_map/pallas_call | solution.py:26
  2.1 3.0 %collective-permute-start.1 = (f32[304,256]{1,0:T(8,128)S(1)}, f32[304,256]{1,0:T(8,128)S(1)}, u32[]{:S(2)}, u32[]{:S(2)}) collective-permute-start(f32[304,256]{1,0:T(8,128)S(1)} %get-tuple-element.77), channel_id=1, source_target_pairs={{0,4},{1,5},{2,6},{3,7},{4,0},{5,1},{6,2},{7,3},{8,12},{9,13},{10,... | collective-permute-start | bytes 933896 | tf_op jit(solution)/shard_map/ppermute | solution.py:356
  5.1 1.4 %collective-permute-start.2 = (f32[304,256]{1,0:T(8,128)S(1)}, f32[304,256]{1,0:T(8,128)S(1)}, u32[]{:S(2)}, u32[]{:S(2)}) collective-permute-start(f32[304,256]{1,0:T(8,128)S(1)} %get-tuple-element.78), channel_id=1, source_target_pairs={{0,6},{1,7},{2,4},{3,5},{4,2},{5,3},{6,0},{7,1},{8,14},{9,15},{10,... | collective-permute-start | bytes 933896 | tf_op jit(solution)/shard_map/ppermute | solution.py:356
  6.6 1.0 %copy-done.1 = f32[1,256,512]{2,1,0:T(8,128)S(1)} copy-done((f32[1,256,512]{2,1,0:T(8,128)S(1)}, f32[1,256,512]{2,1,0:T(8,128)}, u32[]{:S(2)}) %copy-start.1) | copy-done | bytes 524312
  8.0 2.0 %collective-permute-start.11 = (f32[512,256]{1,0:T(8,128)S(1)}, f32[512,256]{1,0:T(8,128)S(1)}, u32[]{:S(2)}, u32[]{:S(2)}) collective-permute-start(f32[512,256]{1,0:T(8,128)S(1)} %shard_map.79.refs_0_), channel_id=1, source_target_pairs={{0,4},{1,5},{2,6},{3,7},{4,0},{5,1},{6,2},{7,3},{8,12},{9,13},{10,... | collective-permute-start | bytes 1572872 | tf_op jit(solution)/shard_map/ppermute | solution.py:356
  10.0 10.0 %collective-permute-done.1.refs_2_ = f32[304,256]{1,0:T(8,128)S(1)} collective-permute-done((f32[304,256]{1,0:T(8,128)S(1)}, f32[304,256]{1,0:T(8,128)S(1)}, u32[]{:S(2)}, u32[]{:S(2)}) %collective-permute-start.1) | collective-permute-done | bytes 311328 | tf_op jit(solution)/shard_map/ppermute | solution.py:356
  20.0 2.0 %collective-permute-start.10 = (f32[512,256]{1,0:T(8,128)S(1)}, f32[512,256]{1,0:T(8,128)S(1)}, u32[]{:S(2)}, u32[]{:S(2)}) collective-permute-start(f32[512,256]{1,0:T(8,128)S(1)} %shard_map.79.refs_0_), channel_id=1, source_target_pairs={{0,2},{1,3},{2,0},{3,1},{4,6},{5,7},{6,4},{7,5},{8,10},{9,11},{10,... | collective-permute-start | bytes 1572872 | tf_op jit(solution)/shard_map/ppermute | solution.py:356
  23.0 1.0 %collective-permute-done.4.refs_5_ = f32[304,256]{1,0:T(8,128)S(1)} collective-permute-done((f32[304,256]{1,0:T(8,128)S(1)}, f32[304,256]{1,0:T(8,128)S(1)}, u32[]{:S(2)}, u32[]{:S(2)}) %collective-permute-start.4) | collective-permute-done | bytes 311328 | tf_op jit(solution)/shard_map/ppermute | solution.py:356
  25.2 0.9 %shard_map.81 = (f32[4,48,512]{2,1,0:T(8,128)S(1)}, f32[48,512]{1,0:T(8,128)S(1)}, f32[48,512]{1,0:T(8,128)S(1)}, f32[48,512]{1,0:T(8,128)S(1)}, f32[48,512]{1,0:T(8,128)S(1)}, /*index=5*/f32[48,512]{1,0:T(8,128)S(1)}) custom-call(f32[48,512]{1,0:T(8,128)S(1)} %shard_map.78.start_ref, f32[8,256]{1,0:T(8,128)S(1)} %get-tuple-element.80.coef_ref, ...), custom_call_target="tpu_custom_call" | custom-call | bytes 2097152 | tf_op jit(solution)/shard_map/pallas_call | solution.py:26
  26.1 0.8 %collective-permute-start.7 = (f32[48,512]{1,0:T(8,128)S(1)}, f32[48,512]{1,0:T(8,128)S(1)}, u32[]{:S(2)}, u32[]{:S(2)}) collective-permute-start(f32[48,512]{1,0:T(8,128)S(1)} %get-tuple-element.88), channel_id=1, source_target_pairs={{0,8},{1,9},{2,10},{3,11},{4,12},{5,13},{6,14},{7,15},{8,0},{9,1},... | collective-permute-start | bytes 294920 | tf_op jit(solution)/shard_map/ppermute | solution.py:369
  26.9 4.1 %collective-permute-done.7.start_ref = f32[48,512]{1,0:T(8,128)S(1)} collective-permute-done((f32[48,512]{1,0:T(8,128)S(1)}, f32[48,512]{1,0:T(8,128)S(1)}, u32[]{:S(2)}, u32[]{:S(2)}) %collective-permute-start.7) | collective-permute-done | bytes 98336 | tf_op jit(solution)/shard_map/ppermute | solution.py:369
  31.0 0.7 collective-permute-start.8
  32.3 1.5 %collective-permute-start.12 = (f32[512,256]{1,0:T(8,128)S(1)}, f32[512,256]{1,0:T(8,128)S(1)}, u32[]{:S(2)}, u32[]{:S(2)}) collective-permute-start(f32[512,256]{1,0:T(8,128)S(1)} %shard_map.89), channel_id=1, source_target_pairs={{0,4},{1,3},{2,6},{3,1},{4,0},{5,7},{6,2},{7,5},{8,12},{9,11},{10,... | collective-permute-start | bytes 1572872 | tf_op jit(solution)/shard_map/ppermute | solution.py:356
  33.8 4.0 %collective-permute-start.9 = (f32[48,512]{1,0:T(8,128)S(1)}, f32[48,512]{1,0:T(8,128)S(1)}, u32[]{:S(2)}, u32[]{:S(2)}) collective-permute-start(f32[48,512]{1,0:T(8,128)S(1)} %shard_map.84), channel_id=1, source_target_pairs={{0,8},{1,9},{2,10},{3,11},{4,12},{5,13},{6,14},{7,15},{8,0},{9,1},... | collective-permute-start | bytes 294920 | tf_op jit(solution)/shard_map/ppermute | solution.py:369
  38.4 1.4 %collective-permute-done.13.refs_3_ = f32[512,256]{1,0:T(8,128)S(1)} collective-permute-done((f32[512,256]{1,0:T(8,128)S(1)}, f32[512,256]{1,0:T(8,128)S(1)}, u32[]{:S(2)}, u32[]{:S(2)}) %collective-permute-start.13) | collective-permute-done | bytes 524320 | tf_op jit(solution)/shard_map/ppermute | solution.py:356
  39.8 0.7 %collective-permute-done.14.refs_4_ = f32[512,256]{1,0:T(8,128)S(1)} collective-permute-done((f32[512,256]{1,0:T(8,128)S(1)}, f32[512,256]{1,0:T(8,128)S(1)}, u32[]{:S(2)}, u32[]{:S(2)}) %collective-permute-start.14) | collective-permute-done | bytes 524320 | tf_op jit(solution)/shard_map/ppermute | solution.py:356
  40.5 0.7 %collective-permute-done.15.refs_5_ = f32[512,256]{1,0:T(8,128)S(1)} collective-permute-done((f32[512,256]{1,0:T(8,128)S(1)}, f32[512,256]{1,0:T(8,128)S(1)}, u32[]{:S(2)}, u32[]{:S(2)}) %collective-permute-start.15) | collective-permute-done | bytes 524320 | tf_op jit(solution)/shard_map/ppermute | solution.py:356
  42.1 1.8 %collective-permute-done.16.refs_1_ = f32[512,256]{1,0:T(8,128)S(1)} collective-permute-done((f32[512,256]{1,0:T(8,128)S(1)}, f32[512,256]{1,0:T(8,128)S(1)}, u32[]{:S(2)}, u32[]{:S(2)}) %collective-permute-start.16) | collective-permute-done | bytes 524320 | tf_op jit(solution)/shard_map/ppermute | solution.py:356
  44.0 2.7 %collective-permute-start.17 = (f32[48,512]{1,0:T(8,128)S(1)}, f32[48,512]{1,0:T(8,128)S(1)}, u32[]{:S(2)}, u32[]{:S(2)}) collective-permute-start(f32[48,512]{1,0:T(8,128)S(1)} %get-tuple-element.124), channel_id=1, source_target_pairs={{0,8},{1,9},{2,10},{3,11},{4,12},{5,13},{6,14},{7,15},{8,0},{9,1},... | collective-permute-start | bytes 294920 | tf_op jit(solution)/shard_map/ppermute | solution.py:369
  46.7 3.1 %collective-permute-done.17.start_ref = f32[48,512]{1,0:T(8,128)S(1)} collective-permute-done((f32[48,512]{1,0:T(8,128)S(1)}, f32[48,512]{1,0:T(8,128)S(1)}, u32[]{:S(2)}, u32[]{:S(2)}) %collective-permute-start.17) | collective-permute-done | bytes 98336 | tf_op jit(solution)/shard_map/ppermute | solution.py:369
  50.5 7.9 %collective-permute-start.22 = (f32[48,512]{1,0:T(8,128)S(1)}, f32[48,512]{1,0:T(8,128)S(1)}, u32[]{:S(2)}, u32[]{:S(2)}) collective-permute-start(f32[48,512]{1,0:T(8,128)S(1)} %shard_map.97.refs_4_), channel_id=1, source_target_pairs={{0,8},{1,9},{2,10},{3,11},{4,12},{5,13},{6,14},{7,15},{8,0},{9,1},... | collective-permute-start | bytes 294920 | tf_op jit(solution)/shard_map/ppermute | solution.py:369
  58.4 0.7 collective-permute-start.19
  59.1 1.5 %collective-permute-start.20 = (f32[48,512]{1,0:T(8,128)S(1)}, f32[48,512]{1,0:T(8,128)S(1)}, u32[]{:S(2)}, u32[]{:S(2)}) collective-permute-start(f32[48,512]{1,0:T(8,128)S(1)} %get-tuple-element.130), channel_id=1, source_target_pairs={{0,4},{1,5},{2,6},{3,7},{4,0},{5,1},{6,2},{7,3},{8,12},{9,13},{10,... | collective-permute-start | bytes 294920 | tf_op jit(solution)/shard_map/ppermute | solution.py:356
  60.6 1.3 %collective-permute-start.21 = (f32[48,512]{1,0:T(8,128)S(1)}, f32[48,512]{1,0:T(8,128)S(1)}, u32[]{:S(2)}, u32[]{:S(2)}) collective-permute-start(f32[48,512]{1,0:T(8,128)S(1)} %get-tuple-element.131), channel_id=1, source_target_pairs={{0,6},{1,7},{2,4},{3,5},{4,2},{5,3},{6,0},{7,1},{8,14},{9,15},{10,... | collective-permute-start | bytes 294920 | tf_op jit(solution)/shard_map/ppermute | solution.py:356
  61.9 1.2 %shard_map.101 = (f32[48,512]{1,0:T(8,128)S(1)}, f32[48,512]{1,0:T(8,128)S(1)}, f32[48,512]{1,0:T(8,128)S(1)}, f32[48,512]{1,0:T(8,128)S(1)}) custom-call(f32[48,512]{1,0:T(8,128)S(1)} %collective-permute-done.22.start_ref, f32[8,256]{1,0:T(8,128)S(1)} %get-tuple-element.80.coef_ref, ...), custom_call_target="tpu_custom_call", output_to_operand_aliasing={{0}: (5, {}), {1}: (6, {}), {2}: (7, {}), {3}: (8, {})} | custom-call | bytes 2097152 | tf_op jit(solution)/shard_map/pallas_call | solution.py:26
  63.1 1.7 %collective-permute-start.25 = (f32[48,512]{1,0:T(8,128)S(1)}, f32[48,512]{1,0:T(8,128)S(1)}, u32[]{:S(2)}, u32[]{:S(2)}) collective-permute-start(f32[48,512]{1,0:T(8,128)S(1)} %get-tuple-element.147), channel_id=1, source_target_pairs={{0,6},{1,7},{2,4},{3,5},{4,2},{5,3},{6,0},{7,1},{8,14},{9,15},{10,... | collective-permute-start | bytes 294920 | tf_op jit(solution)/shard_map/ppermute | solution.py:356
  64.8 1.3 %collective-permute-start.23 = (f32[48,512]{1,0:T(8,128)S(1)}, f32[48,512]{1,0:T(8,128)S(1)}, u32[]{:S(2)}, u32[]{:S(2)}) collective-permute-start(f32[48,512]{1,0:T(8,128)S(1)} %get-tuple-element.145), channel_id=1, source_target_pairs={{0,2},{1,3},{2,0},{3,1},{4,6},{5,7},{6,4},{7,5},{8,10},{9,11},{10,... | collective-permute-start | bytes 294920 | tf_op jit(solution)/shard_map/ppermute | solution.py:356
  67.3 1.5 %collective-permute-done.25.refs_1_.refs_7_ = f32[48,512]{1,0:T(8,128)S(1)} collective-permute-done((f32[48,512]{1,0:T(8,128)S(1)}, f32[48,512]{1,0:T(8,128)S(1)}, u32[]{:S(2)}, u32[]{:S(2)}) %collective-permute-start.25) | collective-permute-done | bytes 98336 | tf_op jit(solution)/shard_map/ppermute | solution.py:356
  68.8 1.0 %collective-permute-done.23.refs_0_.refs_5_ = f32[48,512]{1,0:T(8,128)S(1)} collective-permute-done((f32[48,512]{1,0:T(8,128)S(1)}, f32[48,512]{1,0:T(8,128)S(1)}, u32[]{:S(2)}, u32[]{:S(2)}) %collective-permute-start.23) | collective-permute-done | bytes 98336 | tf_op jit(solution)/shard_map/ppermute | solution.py:356
  69.8 1.0 %collective-permute-done.24.refs_1_.refs_6_ = f32[48,512]{1,0:T(8,128)S(1)} collective-permute-done((f32[48,512]{1,0:T(8,128)S(1)}, f32[48,512]{1,0:T(8,128)S(1)}, u32[]{:S(2)}, u32[]{:S(2)}) %collective-permute-start.24) | collective-permute-done | bytes 98336 | tf_op jit(solution)/shard_map/ppermute | solution.py:356
  70.9 1.4 %collective-permute-done.27.refs_9_ = f32[4,48,256]{2,1,0:T(8,128)S(1)} collective-permute-done((f32[4,48,256]{2,1,0:T(8,128)S(1)}, f32[4,48,256]{2,1,0:T(8,128)S(1)}, u32[]{:S(2)}, u32[]{:S(2)}) %collective-permute-start.27) | collective-permute-done | bytes 196640 | tf_op jit(solution)/shard_map/ppermute | solution.py:356
  72.3 1.1 %shard_map.105 = (f32[256,384]{1,0:T(8,128)}, f32[256,384]{1,0:T(8,128)}) custom-call(f32[48,512]{1,0:T(8,128)S(1)} %get-tuple-element.128.refs_0_, f32[48,512]{1,0:T(8,128)S(1)} %collective-permute-done.19.refs_1_, f32[48,512]{1,0:T(8,128)S(1)} %collective-permute-done.20.refs_2_, f32[48,512]{1,0:T(8,128)S(1)} %collective-permute-done.21.refs_3_, ...), custom_call_target="tpu_custom_call" | custom-call | bytes 2097152 | tf_op jit(solution)/shard_map/pallas_call | solution.py:26
  (57 shorter events, 6.6 us)
Async XLA Ops:
  0.6 21.4 %copy-start = (f32[512,384]{1,0:T(8,128)S(1)}, f32[512,384]{1,0:T(8,128)}, u32[]{:S(2)}) copy-start(f32[512,384]{1,0:T(8,128)} %prior_ref.1) | copy-start | bytes 2359300
  2.1 17.9 %collective-permute-start.1 = (f32[304,256]{1,0:T(8,128)S(1)}, f32[304,256]{1,0:T(8,128)S(1)}, u32[]{:S(2)}, u32[]{:S(2)}) collective-permute-start(f32[304,256]{1,0:T(8,128)S(1)} %get-tuple-element.77), channel_id=1, source_target_pairs={{0,4},{1,5},{2,6},{3,7},{4,0},{5,1},{6,2},{7,3},{8,12},{9,13},{10,... | collective-permute-start | bytes 933896 | tf_op jit(solution)/shard_map/ppermute | solution.py:356
  5.1 17.2 %collective-permute-start.2 = (f32[304,256]{1,0:T(8,128)S(1)}, f32[304,256]{1,0:T(8,128)S(1)}, u32[]{:S(2)}, u32[]{:S(2)}) collective-permute-start(f32[304,256]{1,0:T(8,128)S(1)} %get-tuple-element.78), channel_id=1, source_target_pairs={{0,6},{1,7},{2,4},{3,5},{4,2},{5,3},{6,0},{7,1},{8,14},{9,15},{10,... | collective-permute-start | bytes 933896 | tf_op jit(solution)/shard_map/ppermute | solution.py:356
  6.5 15.8 %collective-permute-start = (f32[304,256]{1,0:T(8,128)S(1)}, f32[304,256]{1,0:T(8,128)S(1)}, u32[]{:S(2)}, u32[]{:S(2)}) collective-permute-start(f32[304,256]{1,0:T(8,128)S(1)} %get-tuple-element.76.refs_0_), channel_id=1, source_target_pairs={{0,2},{1,3},{2,0},{3,1},{4,6},{5,7},{6,4},{7,5},{8,10},{9,11},{10,... | collective-permute-start | bytes 933896 | tf_op jit(solution)/shard_map/ppermute | solution.py:356
  6.6 16.2 %collective-permute-start.3 = (f32[304,256]{1,0:T(8,128)S(1)}, f32[304,256]{1,0:T(8,128)S(1)}, u32[]{:S(2)}, u32[]{:S(2)}) collective-permute-start(f32[304,256]{1,0:T(8,128)S(1)} %get-tuple-element.76.refs_0_), channel_id=1, source_target_pairs={{0,1},{1,0},{2,3},{3,2},{4,5},{5,4},{6,7},{7,6},{8,9},{9,8},{10,11... | collective-permute-start | bytes 933896 | tf_op jit(solution)/shard_map/ppermute | solution.py:356
  6.6 1.0 %copy-start.1 = (f32[1,256,512]{2,1,0:T(8,128)S(1)}, f32[1,256,512]{2,1,0:T(8,128)}, u32[]{:S(2)}) copy-start(f32[1,256,512]{2,1,0:T(8,128)} %param.11) | copy-start | bytes 1572868
  8.0 23.7 %collective-permute-start.11 = (f32[512,256]{1,0:T(8,128)S(1)}, f32[512,256]{1,0:T(8,128)S(1)}, u32[]{:S(2)}, u32[]{:S(2)}) collective-permute-start(f32[512,256]{1,0:T(8,128)S(1)} %shard_map.79.refs_0_), channel_id=1, source_target_pairs={{0,4},{1,5},{2,6},{3,7},{4,0},{5,1},{6,2},{7,3},{8,12},{9,13},{10,... | collective-permute-start | bytes 1572872 | tf_op jit(solution)/shard_map/ppermute | solution.py:356
  20.0 12.3 %collective-permute-start.10 = (f32[512,256]{1,0:T(8,128)S(1)}, f32[512,256]{1,0:T(8,128)S(1)}, u32[]{:S(2)}, u32[]{:S(2)}) collective-permute-start(f32[512,256]{1,0:T(8,128)S(1)} %shard_map.79.refs_0_), channel_id=1, source_target_pairs={{0,2},{1,3},{2,0},{3,1},{4,6},{5,7},{6,4},{7,5},{8,10},{9,11},{10,... | collective-permute-start | bytes 1572872 | tf_op jit(solution)/shard_map/ppermute | solution.py:356
  22.3 1.7 %collective-permute-start.4 = (f32[304,256]{1,0:T(8,128)S(1)}, f32[304,256]{1,0:T(8,128)S(1)}, u32[]{:S(2)}, u32[]{:S(2)}) collective-permute-start(f32[304,256]{1,0:T(8,128)S(1)} %collective-permute-done.refs_1_), channel_id=1, source_target_pairs={{0,1},{1,0},{2,3},{3,2},{4,5},{5,4},{6,7},{7,6},{8,9},{9,8},{10,11... | collective-permute-start | bytes 933896 | tf_op jit(solution)/shard_map/ppermute | solution.py:356
  22.4 2.0 %collective-permute-start.5 = (f32[304,256]{1,0:T(8,128)S(1)}, f32[304,256]{1,0:T(8,128)S(1)}, u32[]{:S(2)}, u32[]{:S(2)}) collective-permute-start(f32[304,256]{1,0:T(8,128)S(1)} %collective-permute-done.1.refs_2_), channel_id=1, source_target_pairs={{0,1},{1,0},{2,3},{3,2},{4,5},{5,4},{6,7},{7,6},{8,9},{9,8},{10,11... | collective-permute-start | bytes 933896 | tf_op jit(solution)/shard_map/ppermute | solution.py:356
  22.9 2.0 %collective-permute-start.6 = (f32[304,256]{1,0:T(8,128)S(1)}, f32[304,256]{1,0:T(8,128)S(1)}, u32[]{:S(2)}, u32[]{:S(2)}) collective-permute-start(f32[304,256]{1,0:T(8,128)S(1)} %collective-permute-done.2.refs_3_), channel_id=1, source_target_pairs={{0,1},{1,0},{2,3},{3,2},{4,5},{5,4},{6,7},{7,6},{8,9},{9,8},{10,11... | collective-permute-start | bytes 933896 | tf_op jit(solution)/shard_map/ppermute | solution.py:356
  26.1 4.9 %collective-permute-start.7 = (f32[48,512]{1,0:T(8,128)S(1)}, f32[48,512]{1,0:T(8,128)S(1)}, u32[]{:S(2)}, u32[]{:S(2)}) collective-permute-start(f32[48,512]{1,0:T(8,128)S(1)} %get-tuple-element.88), channel_id=1, source_target_pairs={{0,8},{1,9},{2,10},{3,11},{4,12},{5,13},{6,14},{7,15},{8,0},{9,1},... | collective-permute-start | bytes 294920 | tf_op jit(solution)/shard_map/ppermute | solution.py:369
  31.0 2.8 %collective-permute-start.8 = (f32[48,512]{1,0:T(8,128)S(1)}, f32[48,512]{1,0:T(8,128)S(1)}, u32[]{:S(2)}, u32[]{:S(2)}) collective-permute-start(f32[48,512]{1,0:T(8,128)S(1)} %shard_map.83.refs_3_), channel_id=1, source_target_pairs={{8,16},{9,17},{10,18},{11,19},{12,20},{13,21},{14,22},{15,23}} | collective-permute-start | bytes 294920 | tf_op jit(solution)/shard_map/ppermute | solution.py:369
  32.3 9.5 %collective-permute-start.12 = (f32[512,256]{1,0:T(8,128)S(1)}, f32[512,256]{1,0:T(8,128)S(1)}, u32[]{:S(2)}, u32[]{:S(2)}) collective-permute-start(f32[512,256]{1,0:T(8,128)S(1)} %shard_map.89), channel_id=1, source_target_pairs={{0,4},{1,3},{2,6},{3,1},{4,0},{5,7},{6,2},{7,5},{8,12},{9,11},{10,... | collective-permute-start | bytes 1572872 | tf_op jit(solution)/shard_map/ppermute | solution.py:356
  33.8 8.2 %collective-permute-start.9 = (f32[48,512]{1,0:T(8,128)S(1)}, f32[48,512]{1,0:T(8,128)S(1)}, u32[]{:S(2)}, u32[]{:S(2)}) collective-permute-start(f32[48,512]{1,0:T(8,128)S(1)} %shard_map.84), channel_id=1, source_target_pairs={{0,8},{1,9},{2,10},{3,11},{4,12},{5,13},{6,14},{7,15},{8,0},{9,1},... | collective-permute-start | bytes 294920 | tf_op jit(solution)/shard_map/ppermute | solution.py:369
  37.8 1.9 %collective-permute-start.13 = (f32[512,256]{1,0:T(8,128)S(1)}, f32[512,256]{1,0:T(8,128)S(1)}, u32[]{:S(2)}, u32[]{:S(2)}) collective-permute-start(f32[512,256]{1,0:T(8,128)S(1)} %get-tuple-element.116.refs_0_), channel_id=1, source_target_pairs={{0,1},{1,0},{2,3},{3,2},{4,5},{5,4},{6,7},{7,6},{8,9},{9,8},{10,11... | collective-permute-start | bytes 1572872 | tf_op jit(solution)/shard_map/ppermute | solution.py:356
  37.8 2.7 %collective-permute-start.14 = (f32[512,256]{1,0:T(8,128)S(1)}, f32[512,256]{1,0:T(8,128)S(1)}, u32[]{:S(2)}, u32[]{:S(2)}) collective-permute-start(f32[512,256]{1,0:T(8,128)S(1)} %get-tuple-element.117.refs_1_), channel_id=1, source_target_pairs={{0,1},{1,0},{2,3},{3,2},{4,5},{5,4},{6,7},{7,6},{8,9},{9,8},{10,11... | collective-permute-start | bytes 1572872 | tf_op jit(solution)/shard_map/ppermute | solution.py:356
  38.4 2.9 %collective-permute-start.15 = (f32[512,256]{1,0:T(8,128)S(1)}, f32[512,256]{1,0:T(8,128)S(1)}, u32[]{:S(2)}, u32[]{:S(2)}) collective-permute-start(f32[512,256]{1,0:T(8,128)S(1)} %get-tuple-element.118.refs_2_), channel_id=1, source_target_pairs={{0,1},{1,0},{2,3},{3,2},{4,5},{5,4},{6,7},{7,6},{8,9},{9,8},{10,11... | collective-permute-start | bytes 1572872 | tf_op jit(solution)/shard_map/ppermute | solution.py:356
  41.8 2.0 %collective-permute-start.16 = (f32[512,256]{1,0:T(8,128)S(1)}, f32[512,256]{1,0:T(8,128)S(1)}, u32[]{:S(2)}, u32[]{:S(2)}) collective-permute-start(f32[512,256]{1,0:T(8,128)S(1)} %shard_map.92.refs_0_), channel_id=1, source_target_pairs={{0,1},{1,0},{2,3},{3,2},{4,5},{5,4},{6,7},{7,6},{8,9},{9,8},{10,11... | collective-permute-start | bytes 1572872 | tf_op jit(solution)/shard_map/ppermute | solution.py:356
  44.0 5.8 %collective-permute-start.17 = (f32[48,512]{1,0:T(8,128)S(1)}, f32[48,512]{1,0:T(8,128)S(1)}, u32[]{:S(2)}, u32[]{:S(2)}) collective-permute-start(f32[48,512]{1,0:T(8,128)S(1)} %get-tuple-element.124), channel_id=1, source_target_pairs={{0,8},{1,9},{2,10},{3,11},{4,12},{5,13},{6,14},{7,15},{8,0},{9,1},... | collective-permute-start | bytes 294920 | tf_op jit(solution)/shard_map/ppermute | solution.py:369
  49.8 0.7 collective-permute-start.18
  50.5 11.4 %collective-permute-start.22 = (f32[48,512]{1,0:T(8,128)S(1)}, f32[48,512]{1,0:T(8,128)S(1)}, u32[]{:S(2)}, u32[]{:S(2)}) collective-permute-start(f32[48,512]{1,0:T(8,128)S(1)} %shard_map.97.refs_4_), channel_id=1, source_target_pairs={{0,8},{1,9},{2,10},{3,11},{4,12},{5,13},{6,14},{7,15},{8,0},{9,1},... | collective-permute-start | bytes 294920 | tf_op jit(solution)/shard_map/ppermute | solution.py:369
  58.4 7.7 %collective-permute-start.19 = (f32[48,512]{1,0:T(8,128)S(1)}, f32[48,512]{1,0:T(8,128)S(1)}, u32[]{:S(2)}, u32[]{:S(2)}) collective-permute-start(f32[48,512]{1,0:T(8,128)S(1)} %get-tuple-element.129), channel_id=1, source_target_pairs={{0,2},{1,3},{2,0},{3,1},{4,6},{5,7},{6,4},{7,5},{8,10},{9,11},{10,... | collective-permute-start | bytes 294920 | tf_op jit(solution)/shard_map/ppermute | solution.py:356
  59.1 7.6 %collective-permute-start.20 = (f32[48,512]{1,0:T(8,128)S(1)}, f32[48,512]{1,0:T(8,128)S(1)}, u32[]{:S(2)}, u32[]{:S(2)}) collective-permute-start(f32[48,512]{1,0:T(8,128)S(1)} %get-tuple-element.130), channel_id=1, source_target_pairs={{0,4},{1,5},{2,6},{3,7},{4,0},{5,1},{6,2},{7,3},{8,12},{9,13},{10,... | collective-permute-start | bytes 294920 | tf_op jit(solution)/shard_map/ppermute | solution.py:356
  60.6 6.6 %collective-permute-start.21 = (f32[48,512]{1,0:T(8,128)S(1)}, f32[48,512]{1,0:T(8,128)S(1)}, u32[]{:S(2)}, u32[]{:S(2)}) collective-permute-start(f32[48,512]{1,0:T(8,128)S(1)} %get-tuple-element.131), channel_id=1, source_target_pairs={{0,6},{1,7},{2,4},{3,5},{4,2},{5,3},{6,0},{7,1},{8,14},{9,15},{10,... | collective-permute-start | bytes 294920 | tf_op jit(solution)/shard_map/ppermute | solution.py:356
  63.1 5.7 %collective-permute-start.25 = (f32[48,512]{1,0:T(8,128)S(1)}, f32[48,512]{1,0:T(8,128)S(1)}, u32[]{:S(2)}, u32[]{:S(2)}) collective-permute-start(f32[48,512]{1,0:T(8,128)S(1)} %get-tuple-element.147), channel_id=1, source_target_pairs={{0,6},{1,7},{2,4},{3,5},{4,2},{5,3},{6,0},{7,1},{8,14},{9,15},{10,... | collective-permute-start | bytes 294920 | tf_op jit(solution)/shard_map/ppermute | solution.py:356
  64.8 5.0 %collective-permute-start.23 = (f32[48,512]{1,0:T(8,128)S(1)}, f32[48,512]{1,0:T(8,128)S(1)}, u32[]{:S(2)}, u32[]{:S(2)}) collective-permute-start(f32[48,512]{1,0:T(8,128)S(1)} %get-tuple-element.145), channel_id=1, source_target_pairs={{0,2},{1,3},{2,0},{3,1},{4,6},{5,7},{6,4},{7,5},{8,10},{9,11},{10,... | collective-permute-start | bytes 294920 | tf_op jit(solution)/shard_map/ppermute | solution.py:356
  66.2 4.6 %collective-permute-start.24 = (f32[48,512]{1,0:T(8,128)S(1)}, f32[48,512]{1,0:T(8,128)S(1)}, u32[]{:S(2)}, u32[]{:S(2)}) collective-permute-start(f32[48,512]{1,0:T(8,128)S(1)} %get-tuple-element.146), channel_id=1, source_target_pairs={{0,4},{1,5},{2,6},{3,7},{4,0},{5,1},{6,2},{7,3},{8,12},{9,13},{10,... | collective-permute-start | bytes 294920 | tf_op jit(solution)/shard_map/ppermute | solution.py:356
  67.3 3.6 %collective-permute-start.26 = (f32[4,48,256]{2,1,0:T(8,128)S(1)}, f32[4,48,256]{2,1,0:T(8,128)S(1)}, u32[]{:S(2)}, u32[]{:S(2)}) collective-permute-start(f32[4,48,256]{2,1,0:T(8,128)S(1)} %shard_map.102), channel_id=1, source_target_pairs={{0,1},{1,0},{2,3},{3,2},{4,5},{5,4},{6,7},{7,6},{8,9},{9,8},{10,11... | collective-permute-start | bytes 589832 | tf_op jit(solution)/shard_map/ppermute | solution.py:356
  70.8 1.5 %collective-permute-start.27 = (f32[4,48,256]{2,1,0:T(8,128)S(1)}, f32[4,48,256]{2,1,0:T(8,128)S(1)}, u32[]{:S(2)}, u32[]{:S(2)}) collective-permute-start(f32[4,48,256]{2,1,0:T(8,128)S(1)} %shard_map.104), channel_id=1, source_target_pairs={{0,1},{1,0},{2,3},{3,2},{4,5},{5,4},{6,7},{7,6},{8,9},{9,8},{10,11... | collective-permute-start | bytes 589832 | tf_op jit(solution)/shard_map/ppermute | solution.py:356
